TPU v7x, 256 devices: a whole 4x4x8 slice. The times are simulated.
256 devices in a mesh: ctx: 8 (over y, core), req: 8 (over z), mp: 4 (over x).
Axes of the slice: x: 4, y: 4, z: 8, core: 2. Of those that a mesh axis runs over, the one named last changes fastest.
Arguments:
- token_ids: int32 [64, 16], replicated, may hold values from 0 to 25599
- embed_table: bfloat16 [25600, 7168], P('mp', ('ctx', 'req')), may hold values from -0.29882812 to 0.29882812
- queries: bfloat16 [64, 16, 3584], P(('ctx', 'req'), None, 'mp'), may hold values from -80 to 80
- draft_kv: bfloat16 [2, 64, 16, 3584], P(None, ('ctx', 'req'), None, 'mp'), may hold values from -4 to 4
- prefix_kv: bfloat16 [2, 16384, 3584], P(None, 'ctx', 'mp'), may hold values from -4 to 4
- suffix_kv: bfloat16 [2, 64, 512, 3584], P(None, ('ctx', 'req'), None, 'mp'), may hold values from -4 to 4
- suffix_len: int32 [64], P(('ctx', 'req')), may hold values from 1 to 512, as said below
- slopes: float32 [32], P('mp'), may hold values from 3.0517578e-06 to 0.08
- out_weight: bfloat16 [3584, 7168], P('mp', ('ctx', 'req')), may hold values from -0.09375 to 0.09375
- ln_gain: float32 [7168], P('mp'), may hold values from 0.5 to 1.5
- up_weight: bfloat16 [7168, 14336], P('mp', ('ctx', 'req')), may hold values from -0.0625 to 0.0625
- down_weight: bfloat16 [14336, 7168], P(('ctx', 'req'), 'mp'), may hold values from -0.046875 to 0.046875
Outputs:
- residual: float32 [64, 16, 7168], P(('ctx', 'req'), None, 'mp')
- layer_out: float32 [64, 16, 7168], P(('ctx', 'req'), None, 'mp')
Inputs may be any that keep to these rules, and one draw needn't show every extreme that they name: `suffix_len`: in every draw some request has exactly 512 filled slots.
All inputs are finite; a program needn't handle non-finite values.
Results may differ from a plain program's by a relative error of at most 0.015.
Values may be sent and summed in bfloat16 or wider, within the bound.
No kernel may reach another device: no remote copies, remote signals or barrier semaphores. Data moves between devices by JAX's collectives and lax.ppermute only.
A program may use at most 128 MiB of HBM per device.

v0:
```python
import math

import jax
import jax.numpy as jnp
from jax import lax
from jax.sharding import PartitionSpec as P


def joined(value, axis, join):
    pieces = jax.tree.map(lambda part: lax.all_gather(part, axis), value)
    head = jax.tree.map(lambda part: part[0], pieces)
    tail = jax.tree.map(lambda part: part[1:], pieces)
    total, _ = lax.scan(lambda total, piece: (join(total, piece), None), head, tail)
    return total


def combine_parts(left_part, right_part):
    left_top, left_total, left_sum = left_part
    right_top, right_total, right_sum = right_part
    joint_top = jnp.maximum(left_top, right_top)
    left_factor = jnp.exp(left_top - joint_top)
    right_factor = jnp.exp(right_top - joint_top)
    joint_total = left_total * left_factor + right_total * right_factor
    head_count = left_top.shape[-1]
    shaped = left_sum.shape[:-1] + (head_count, left_sum.shape[-1] // head_count)
    joint_sum = (
        left_sum.reshape(shaped) * left_factor[..., None]
        + right_sum.reshape(shaped) * right_factor[..., None]
    )
    return (joint_top, joint_total, joint_sum.reshape(left_sum.shape))


def partial_softmax(query_rows, key_rows, value_rows, key_bias, visible, head_count):
    batch_size, row_count, feature_width = query_rows.shape
    head_size = feature_width // head_count
    query_heads = query_rows.reshape(batch_size, row_count, head_count, head_size)
    key_heads = key_rows.reshape(batch_size, key_rows.shape[1], head_count, head_size)
    value_heads = value_rows.reshape(batch_size, value_rows.shape[1], head_count, head_size)
    scores = (
        jnp.einsum("bthd,bkhd->bhtk", query_heads, key_heads, preferred_element_type=jnp.float32)
        * (1.0 / math.sqrt(head_size))
        + key_bias
    )
    if visible is not None:
        scores = jnp.where(visible, scores, -jnp.inf)
    row_top = jnp.max(scores, axis=3)
    weights = jnp.exp(scores - row_top[..., None])
    row_total = jnp.sum(weights, axis=3)
    weighted = jnp.einsum(
        "bhtk,bkhd->bthd",
        weights.astype(jnp.bfloat16),
        value_heads,
        preferred_element_type=jnp.float32,
    )
    flat_rows = batch_size * row_count
    return (
        row_top.transpose(0, 2, 1).reshape(flat_rows, head_count),
        row_total.transpose(0, 2, 1).reshape(flat_rows, head_count),
        weighted.reshape(flat_rows, feature_width),
    )


def per_device(
    token_ids,
    embed_table,
    queries,
    draft_kv,
    prefix_kv,
    suffix_kv,
    suffix_len,
    slopes,
    out_weight,
    ln_gain,
    up_weight,
    down_weight,
):
    head_count = slopes.shape[0]
    req_local, draft_count, feature_width = queries.shape
    own_rows = req_local * draft_count
    prompt_local = prefix_kv.shape[1]
    context_count = lax.axis_size("ctx")
    context_index = lax.axis_index("ctx")
    prompt_total = prompt_local * context_count
    gathered = lax.all_gather(queries, "ctx", axis=0, tiled=True)
    prompt_pos = context_index * prompt_local + jnp.arange(prompt_local, dtype=jnp.int32)
    prompt_bias = (
        -slopes[None, :, None, None]
        * (prompt_total - prompt_pos).astype(jnp.float32)[None, None, None, :]
    )
    prompt_top, prompt_sums, prompt_weighted = partial_softmax(
        gathered.reshape(1, -1, feature_width),
        prefix_kv[0][None],
        prefix_kv[1][None],
        prompt_bias,
        None,
        head_count,
    )
    merged_top, merged_total, merged_sum = joined(
        (prompt_top, prompt_sums, prompt_weighted), "ctx", combine_parts
    )
    prompt_own = (
        lax.dynamic_slice_in_dim(merged_top, context_index * own_rows, own_rows, 0),
        lax.dynamic_slice_in_dim(merged_total, context_index * own_rows, own_rows, 0),
        lax.dynamic_slice_in_dim(merged_sum, context_index * own_rows, own_rows, 0),
    )
    slot_count = suffix_kv.shape[2]
    slot_pos = jnp.arange(slot_count, dtype=jnp.int32)
    suffix_bias = slopes[None, :, None, None] * slot_pos.astype(jnp.float32)[None, None, None, :]
    suffix_visible = slot_pos[None, None, None, :] < suffix_len[:, None, None, None]
    suffix_parts = partial_softmax(
        queries, suffix_kv[0], suffix_kv[1], suffix_bias, suffix_visible, head_count
    )
    draft_pos = jnp.arange(draft_count, dtype=jnp.int32)
    draft_bias = slopes[None, :, None, None] * (
        suffix_len[:, None, None, None] + draft_pos[None, None, None, :]
    ).astype(jnp.float32)
    draft_visible = draft_pos[None, None, None, :] <= draft_pos[None, None, :, None]
    draft_parts = partial_softmax(
        queries, draft_kv[0], draft_kv[1], draft_bias, draft_visible, head_count
    )
    finished = combine_parts(combine_parts(prompt_own, suffix_parts), draft_parts)
    attended = (
        (finished[2].reshape(own_rows, head_count, -1) / finished[1][..., None])
        .reshape(own_rows, feature_width)
        .astype(jnp.bfloat16)
    )
    projected = jnp.dot(
        lax.all_gather(attended, ("ctx", "req"), axis=0, tiled=True),
        out_weight,
        preferred_element_type=jnp.float32,
    )
    vocab_local = embed_table.shape[0]
    model_index = lax.axis_index("mp")
    shifted_ids = token_ids.reshape(-1) - model_index * vocab_local
    one_hot = (shifted_ids[:, None] == jnp.arange(vocab_local, dtype=jnp.int32)[None, :]).astype(
        jnp.bfloat16
    )
    looked_up = jnp.dot(one_hot, embed_table, preferred_element_type=jnp.float32)
    regrouped = lax.all_to_all(
        projected + looked_up, ("ctx", "req"), split_axis=0, concat_axis=1, tiled=True
    )
    quarter = ln_gain.shape[0]
    residual_wide = lax.psum(regrouped, "mp")
    mean_value = jnp.mean(residual_wide, axis=1, keepdims=True)
    mean_square = jnp.mean(residual_wide * residual_wide, axis=1, keepdims=True)
    own_wide = lax.dynamic_slice_in_dim(residual_wide, model_index * quarter, quarter, 1)
    normed = (
        (own_wide - mean_value)
        * lax.rsqrt(mean_square - mean_value * mean_value + 1e-05)
        * ln_gain[None, :]
    ).astype(jnp.bfloat16)
    lifted = jnp.dot(
        lax.all_gather(normed, ("ctx", "req"), axis=0, tiled=True),
        up_weight,
        preferred_element_type=jnp.float32,
    )
    hidden_total = lax.psum(lifted, "mp")
    activated = jax.nn.gelu(hidden_total, approximate=False).astype(jnp.bfloat16)
    lowered = lax.psum_scatter(
        jnp.dot(activated, down_weight, preferred_element_type=jnp.float32),
        ("ctx", "req"),
        scatter_dimension=0,
        tiled=True,
    )
    layer_out = own_wide + lowered
    return (
        own_wide.reshape(req_local, draft_count, quarter),
        layer_out.reshape(req_local, draft_count, quarter),
    )


def solution(mesh):
    in_specs = (
        P(),
        P("mp", ("ctx", "req")),
        P(("ctx", "req"), None, "mp"),
        P(None, ("ctx", "req"), None, "mp"),
        P(None, "ctx", "mp"),
        P(None, ("ctx", "req"), None, "mp"),
        P(("ctx", "req")),
        P("mp"),
        P("mp", ("ctx", "req")),
        P("mp"),
        P("mp", ("ctx", "req")),
        P(("ctx", "req"), "mp"),
    )
    out_specs = (P(("ctx", "req"), None, "mp"), P(("ctx", "req"), None, "mp"))
    return jax.shard_map(
        per_device, mesh=mesh, in_specs=in_specs, out_specs=out_specs, check_vma=False
    )
```

profile of v0, /device:TPU:2, one launch (start us, length us, event | category | flops | bytes accessed | tf_op | source)
XLA Modules:
  0.0 557.7 jit_solution(478384381965529517)
XLA Ops:
  7.2 0.8 neg.7
  8.0 6.8 %fusion.115 = (bf16[1,2048,896]{2,1,0:T(8,128)(2,1)}, bf16[1,2048,896]{2,1,0:T(8,128)(2,1)}) fusion(bf16[2,2048,896]{2,1,0:T(8,128)(2,1)} %param.18), kind=kLoop, calls=%fused_computation.159 | loop fusion | bytes 14680064 | tf_op jit(solution)/shard_map/slice | solution.py:93
  14.8 6.1 %copy.52 = bf16[1,2048,896]{1,2,0:T(8,128)(2,1)} copy(bf16[1,2048,896]{2,1,0:T(8,128)(2,1)} %get-tuple-element.77) | data formatting | bytes 7340032 | tf_op jit(solution)/shard_map/slice | solution.py:92
  20.9 13.3 %all_gather.18 = bf16[8,16,896]{2,1,0:T(8,128)(2,1)S(1)} all-gather(bf16[1,16,896]{2,1,0:T(8,128)(2,1)S(1)} %copy-done.6), channel_id=1, replica_groups=mesh['ctx'=8,'req'=8,'mp'=4] {'ctx'}, dimensions={0}, use_global_device_ids=true | all-gather | bytes 258048 | tf_op jit(solution)/shard_map/all_gather | solution.py:84
  34.2 0.3 reshape.308
  34.5 6.2 %copy.54 = bf16[1,2048,896]{1,2,0:T(8,128)(2,1)} copy(bf16[1,2048,896]{2,1,0:T(8,128)(2,1)} %get-tuple-element.76) | data formatting | bytes 7340032 | tf_op jit(solution)/shard_map/slice | solution.py:93
  40.7 3.6 fusion.5
  44.3 2.3 fusion.8
  46.7 0.9 copy-done.1
  47.6 1.0 copy.55
  48.7 4.4 fusion.7
  53.2 13.0 %all_gather.20 = f32[8,128,8]{1,2,0:T(8,128)S(1)} all-gather(f32[1,128,8]{1,2,0:T(8,128)S(1)} %bitcast.138), channel_id=1, replica_groups=mesh['ctx'=8,'req'=8,'mp'=4] {'ctx'}, dimensions={0}, use_global_device_ids=true | all-gather | bytes 36864 | tf_op jit(solution)/shard_map/all_gather | solution.py:10
  66.2 12.8 %all_gather.19 = f32[8,128,8]{1,2,0:T(8,128)S(1)} all-gather(f32[1,128,8]{1,2,0:T(8,128)S(1)} %bitcast.137), channel_id=1, replica_groups=mesh['ctx'=8,'req'=8,'mp'=4] {'ctx'}, dimensions={0}, use_global_device_ids=true | all-gather | bytes 36864 | tf_op jit(solution)/shard_map/all_gather | solution.py:10
  79.0 1.6 fusion.116
  80.6 1.3 copy.59
  82.7 0.5 copy.62
  83.4 1.5 fusion.119
  84.8 0.4 convolution_bitcast_fusion.1
  85.7 0.2 convolution_bitcast_fusion
  86.4 1.0 slice_bitcast_fusion
  87.4 0.2 copy.56
  87.6 3.8 slice.53
  91.4 10.3 %while.14 = (s32[]{:T(128)}, f32[128,8]{0,1:T(8,128)S(1)}, f32[128,8]{0,1:T(8,128)S(1)}, f32[128,896]{0,1:T(8,128)S(1)}, f32[7,128,8]{1,2,0:T(8,128)S(1)}, /*ind...) while((s32[]{:T(128)}, f32[128,8]{0,1:T(8,128)S(1)}, f32[128,8]{0,1:T(8,128)S(1)}, ...), condition=%wide.region_3.4_spmd, body=%wide.region_2.3_spmd.sunk | while | flops 350210 | bytes 3252317 | solution.py:13
  91.5 1.1 constant_dynamic-slice_fusion.2
  92.9 1.1 constant_dynamic-slice_fusion.2
  94.4 1.1 constant_dynamic-slice_fusion.2
  95.9 1.1 constant_dynamic-slice_fusion.2
  97.3 1.1 constant_dynamic-slice_fusion.2
  98.8 1.1 constant_dynamic-slice_fusion.2
  100.3 1.1 constant_dynamic-slice_fusion.2
  103.1 0.2 copy.58
  103.3 0.7 divide_convert_fusion
  104.0 0.2 all-reduce.3.cloned.1.call-start
  104.4 5.8 %fusion.3 = f32[1024,112]{0,1:T(8,128)S(1)} fusion(bf16[6400,112]{0,1:T(8,128)(2,1)S(1)} %copy-done, s32[1024]{0:T(1024)S(1)} %sub.98), kind=kOutput, calls=%fused_computation.11 | convolution fusion | flops 1474560000 | bytes 1896448 | tf_op jit(solution)/shard_map/dot_general | solution.py:138
  110.3 73.1 %all-gather.6.cloned.1.call-done = bf16[1024,896]{1,0:T(8,128)(2,1)} async-done(((bf16[16,896]{1,0:T(8,128)(2,1)}), bf16[1024,896]{1,0:T(8,128)(2,1)}) %all-gather.6.cloned.1.call-update) | async-done | bytes 1835024 | tf_op jit(solution)/shard_map/all_gather | solution.py:128
  183.4 2.2 convolution_add_fusion
  185.6 0.2 copy.74
  185.8 24.7 %all_to_all.19 = f32[64,16,112]{2,1,0:T(8,128)S(1)} all-to-all(f32[64,16,112]{2,1,0:T(8,128)S(1)} %bitcast.134), channel_id=1, replica_groups=mesh['ctx'=8,'req'=8,'mp'=4] {'ctx','req'}, dimensions={0} | all-to-all | bytes 917504 | tf_op jit(solution)/shard_map/all_to_all | solution.py:139
  210.7 1.1 all_to_all.17
  211.9 43.3 %all-reduce.3.cloned.1.call-done = f32[16,7168]{1,0:T(8,128)} async-done(((f32[16,7168]{1,0:T(8,128)}), f32[16,7168]{1,0:T(8,128)}) %all-reduce.3.cloned.1.call-update) | async-done | bytes 458768 | tf_op jit(solution)/shard_map/psum | solution.py:143
  255.1 1.2 fusion.110
  256.3 1.6 multiply_convert_fusion
  258.0 80.8 %all-gather.8.cloned.1.call-done = bf16[1024,1792]{1,0:T(8,128)(2,1)} async-done(((bf16[16,1792]{1,0:T(8,128)(2,1)}), bf16[1024,1792]{1,0:T(8,128)(2,1)}) %all-gather.8.cloned.1.call-update) | async-done | bytes 3670032 | tf_op jit(solution)/shard_map/all_gather | solution.py:153
  338.8 4.2 fusion.120
  343.1 47.2 %all-reduce.5.cloned.1.call-done = f32[1024,224]{0,1:T(8,128)} async-done(((f32[1024,224]{0,1:T(8,128)}), f32[1024,224]{0,1:T(8,128)}) %all-reduce.5.cloned.1.call-update) | async-done | bytes 917520 | tf_op jit(solution)/shard_map/psum | solution.py:157
  390.3 7.2 %fusion.27 = f32[1024,1792]{1,0:T(8,128)} fusion(bf16[224,1792]{1,0:T(8,128)(2,1)S(1)} %copy-done.12, f32[1024,224]{0,1:T(8,128)} %all-reduce.5.cloned.1.call-done), kind=kOutput, calls=%fused_computation.50 | convolution fusion | flops 836993024 | bytes 9060352 | tf_op jit(solution)/shard_map/dot_general | solution.py:160
  397.4 151.8 %reduce-scatter.2.cloned.1.call-done = f32[16,1792]{1,0:T(8,128)} async-done(((f32[1024,1792]{1,0:T(8,128)}), f32[16,1792]{1,0:T(8,128)}) %reduce-scatter.2.cloned.1.call-update) | async-done | bytes 114704 | tf_op jit(solution)/shard_map/reduce_scatter | solution.py:159
  549.2 1.7 add_bitcast_fusion
  (104 shorter events, 5.8 us)
Async XLA Ops:
  7.2 97.2 %copy-start = (bf16[6400,112]{0,1:T(8,128)(2,1)S(1)}, bf16[6400,112]{0,1:T(8,128)(2,1)}, u32[]{:S(2)}) copy-start(bf16[6400,112]{0,1:T(8,128)(2,1)} %param.15) | copy-start | bytes 4300804
  7.2 79.2 %all-gather.4.cloned.1.call-start = ((), (), s32[]{:S(2)}) async-start(), calls=%async_computation.2 | async-start | bytes 4128768 | tf_op jit(solution)/shard_map/all_gather | solution.py:10
  14.8 6.1 %copy-start.6 = (bf16[1,16,896]{2,1,0:T(8,128)(2,1)S(1)}, bf16[1,16,896]{2,1,0:T(8,128)(2,1)}, u32[]{:S(2)}) copy-start(bf16[1,16,896]{2,1,0:T(8,128)(2,1)} %param.16) | copy-start | bytes 86020
  40.7 3.6 copy-start.2
  44.3 3.2 copy-start.1
  48.6 134.8 %all-gather.6.cloned.1.call-start = ((), (), s32[]{:S(2)}) async-start(), calls=%async_computation.3 | async-start | bytes 1863680 | tf_op jit(solution)/shard_map/all_gather | solution.py:128
  53.2 29.4 %copy-start.7 = (bf16[2,1,16,896]{3,2,1,0:T(8,128)(2,1)S(1)}, bf16[2,1,16,896]{3,2,1,0:T(8,128)(2,1)}, u32[]{:S(2)}) copy-start(bf16[2,1,16,896]{3,2,1,0:T(8,128)(2,1)} %param.17) | copy-start | bytes 172036
  53.2 30.1 %copy-start.10 = (f32[8]{0:T(128)S(1)}, f32[8]{0:T(128)}, u32[]{:S(2)}) copy-start(f32[8]{0:T(128)} %param.21) | copy-start | bytes 100
  66.1 20.1 %copy-start.4 = (f32[8,128,8]{1,2,0:T(8,128)}, f32[8,128,8]{1,2,0:T(8,128)S(1)}, u32[]{:S(2)}) copy-start(f32[8,128,8]{1,2,0:T(8,128)S(1)} %all_gather.20) | copy-start | bytes 98308
  79.0 7.3 %copy-start.5 = (f32[8,128,8]{1,2,0:T(8,128)}, f32[8,128,8]{1,2,0:T(8,128)S(1)}, u32[]{:S(2)}) copy-start(f32[8,128,8]{1,2,0:T(8,128)S(1)} %all_gather.19) | copy-start | bytes 98308
  86.3 5.1 slice-start
  86.3 5.1 slice-start.1
  91.4 12.8 %copy-start.9 = (s32[64,16]{0,1:T(8,128)S(1)}, s32[64,16]{0,1:T(8,128)}, u32[]{:S(2)}) copy-start(s32[64,16]{0,1:T(8,128)} %param.14) | copy-start | bytes 12292
  104.0 151.2 %all-reduce.3.cloned.1.call-start = ((), (), s32[]{:S(2)}) async-start(), calls=%async_computation.4 | async-start | bytes 917504 | tf_op jit(solution)/shard_map/psum | solution.py:143
  104.4 79.0 %copy-start.3 = (bf16[896,112]{0,1:T(8,128)(2,1)S(1)}, bf16[896,112]{0,1:T(8,128)(2,1)}, u32[]{:S(2)}) copy-start(bf16[896,112]{0,1:T(8,128)(2,1)} %param.22) | copy-start | bytes 602116
  110.2 146.1 %copy-start.8 = (f32[1792]{0:T(1024)S(1)}, f32[1792]{0:T(1024)}, u32[]{:S(2)}) copy-start(f32[1792]{0:T(1024)} %param.23) | copy-start | bytes 21508
  110.2 228.6 %copy-start.11 = (bf16[1792,224]{0,1:T(8,128)(2,1)S(1)}, bf16[1792,224]{0,1:T(8,128)(2,1)}, u32[]{:S(2)}) copy-start(bf16[1792,224]{0,1:T(8,128)(2,1)} %param.24) | copy-start | bytes 2408452
  211.8 178.5 %copy-start.12 = (bf16[224,1792]{1,0:T(8,128)(2,1)S(1)}, bf16[224,1792]{1,0:T(8,128)(2,1)}, u32[]{:S(2)}) copy-start(bf16[224,1792]{1,0:T(8,128)(2,1)} %param.25) | copy-start | bytes 2408452
  211.8 127.0 %all-gather.8.cloned.1.call-start = ((), (), s32[]{:S(2)}) async-start(), calls=%async_computation.5 | async-start | bytes 3727360 | tf_op jit(solution)/shard_map/all_gather | solution.py:153
  258.0 132.3 %all-reduce.5.cloned.1.call-start = ((), (), s32[]{:S(2)}) async-start(), calls=%async_computation.6 | async-start | bytes 1835008 | tf_op jit(solution)/shard_map/psum | solution.py:157
  343.0 206.2 %reduce-scatter.2.cloned.1.call-start = ((), (), s32[]{:S(2)}) async-start(), calls=%async_computation.7 | async-start | bytes 7454720 | tf_op jit(solution)/shard_map/reduce_scatter | solution.py:159
Sparse Core Ops, SparseCore 0:
  48.7 34.9 all-gather.3
  104.1 79.2 all-gather.5
  211.9 43.1 all-reduce.2
  258.7 80.0 all-gather.7
  343.1 47.0 all-reduce.4
  397.6 151.6 reduce-scatter.1
where the time goes:
time: 559 us; the launch traced here: 558 us
  waiting for transfers between devices  396 us (71%)
  blocking collectives  63.8 us (11%)
  local copies, waits for them, and re-layouts  42 us (8%)
  matrix products  27.6 us (5%)
  between operations  15.2 us (3%)
  other arithmetic  12.2 us (2%)
    reduce_scatter x1, waiting for transfers between devices, per_device(): lax.psum_scatter(jnp.dot(activated, down_weight, preferred_element_type=j...  152 us
    all_gather x1, waiting for transfers between devices, per_device(): lax.all_gather(normed, ('ctx', 'req'), axis=0, tiled=True)  80.8 us
    all_gather x1, waiting for transfers between devices, per_device(): lax.all_gather(attended, ('ctx', 'req'), axis=0, tiled=True)  73.1 us
    psum x1, waiting for transfers between devices, per_device(): hidden_total = lax.psum(lifted, 'mp')  47.2 us
    psum x1, waiting for transfers between devices, per_device(): residual_wide = lax.psum(regrouped, 'mp')  43.3 us
    all_gather x2, blocking collectives, joined(): pieces = jax.tree.map(lambda part: lax.all_gather(part, axis), value)  25.8 us
    all_to_all x1, blocking collectives, per_device(): lax.all_to_all(projected + looked_up, ('ctx', 'req'), split_axis=0, conca...  24.7 us
    all_gather x1, blocking collectives, per_device(): gathered = lax.all_gather(queries, 'ctx', axis=0, tiled=True)  13.3 us
  transfers between devices with their start and end apart: 6, of which 5 were waited for; matrix products, arithmetic and copies ran while one was open for 3% of the time, Pallas kernels for 0%

commit v1 on v0

v1 whole, which is shorter than its diff:
```python
import functools
import math

import jax
import jax.numpy as jnp
from jax import lax
from jax.experimental import pallas as pl
from jax.experimental.pallas import tpu as pltpu
from jax.sharding import PartitionSpec as P

LANES = 128
F32 = jnp.float32
BF16 = jnp.bfloat16


def head_lanes(head, tile, head_size):
    first = max(head * head_size - tile * LANES, 0)
    last = min((head + 1) * head_size - tile * LANES, LANES)
    return first, last


def head_tiles(head, head_size):
    return range(head * head_size // LANES, ((head + 1) * head_size - 1) // LANES + 1)


def lane_mask(shape, first, last):
    lane = lax.broadcasted_iota(jnp.int32, shape, len(shape) - 1)
    return (lane >= first) & (lane < last)


def split_three(value):
    high = value.astype(BF16).astype(F32)
    rest = value - high
    middle = rest.astype(BF16).astype(F32)
    low = rest - middle
    return high, middle, low


def prompt_kernel(
    offset_ref, slopes_ref, query_ref, prefix_ref, out_ref, kv_buf, sems, *, heads, head_size
):
    rows, width = query_ref.shape
    keys = kv_buf.shape[2]
    tiles = width // LANES
    copies = {}
    for tile in range(tiles):
        for which in range(2):
            copies[which, tile] = pltpu.make_async_copy(
                prefix_ref.at[which, :, pl.ds(tile * LANES, LANES)],
                kv_buf.at[which, tile],
                sems.at[which, tile],
            )
            copies[which, tile].start()
    scale = 1.0 / math.sqrt(head_size)
    position = (
        lax.broadcasted_iota(jnp.int32, (1, keys), 1) - offset_ref[0]
    ).astype(F32)
    arrived = set()

    def wait(which, tile):
        if (which, tile) not in arrived:
            arrived.add((which, tile))
            copies[which, tile].wait()

    parts = [jnp.zeros((rows, LANES), F32) for _ in range(tiles)]
    stats = jnp.zeros((rows, LANES), F32)
    stat_lane = lax.broadcasted_iota(jnp.int32, (rows, LANES), 1)
    for head in range(heads):
        span = head_tiles(head, head_size)
        for tile in span:
            wait(0, tile)
        query_window = jnp.concatenate(
            [
                jnp.where(
                    lane_mask((rows, LANES), *head_lanes(head, tile, head_size)),
                    query_ref[:, tile * LANES : (tile + 1) * LANES],
                    jnp.zeros((rows, LANES), BF16),
                )
                for tile in span
            ],
            axis=1,
        )
        key_window = jnp.concatenate([kv_buf[0, tile] for tile in span], axis=1)
        scores = lax.dot_general(
            query_window, key_window, (((1,), (1,)), ((), ())), preferred_element_type=F32
        )
        scores = scores * scale + slopes_ref[head] * position
        top = jnp.max(scores, axis=1, keepdims=True)
        weights = jnp.exp(scores - top)
        total = jnp.sum(weights, axis=1, keepdims=True)
        for tile in span:
            wait(1, tile)
        value_window = jnp.concatenate([kv_buf[1, tile] for tile in span], axis=1)
        sums = jnp.dot(weights.astype(BF16), value_window, preferred_element_type=F32)
        sums = sums * (1.0 / total)
        for place, tile in enumerate(span):
            parts[tile] = jnp.where(
                lane_mask((rows, LANES), *head_lanes(head, tile, head_size)),
                sums[:, place * LANES : (place + 1) * LANES],
                parts[tile],
            )
        stats = jnp.where(stat_lane % heads == head, top + jnp.log(total), stats)
    for tile in range(tiles):
        out_ref[:, tile * LANES : (tile + 1) * LANES] = parts[tile].astype(BF16)
    high, middle, low = split_three(stats)
    group = stat_lane // heads
    packed = jnp.where(
        group == 0, high, jnp.where(group == 1, middle, jnp.where(group == 2, low, 0.0))
    )
    out_ref[:, tiles * LANES :] = packed.astype(BF16)


def prompt_part(query_rows, prefix_kv, slopes, offset):
    rows, width = query_rows.shape
    heads = slopes.shape[0]
    keys = prefix_kv.shape[1]
    tiles = width // LANES
    return pl.pallas_call(
        functools.partial(prompt_kernel, heads=heads, head_size=width // heads),
        out_shape=jax.ShapeDtypeStruct((rows, width + LANES), BF16),
        in_specs=[
            pl.BlockSpec(memory_space=pltpu.SMEM),
            pl.BlockSpec(memory_space=pltpu.SMEM),
            pl.BlockSpec(memory_space=pltpu.VMEM),
            pl.BlockSpec(memory_space=pl.ANY),
        ],
        out_specs=pl.BlockSpec(memory_space=pltpu.VMEM),
        scratch_shapes=[
            pltpu.VMEM((2, tiles, keys, LANES), BF16),
            pltpu.SemaphoreType.DMA((2, tiles)),
        ],
        compiler_params=pltpu.CompilerParams(vmem_limit_bytes=40 * 1024 * 1024),
    )(offset, slopes, query_rows, prefix_kv)


def own_kernel(
    length_ref, slopes_ref, query_ref, suffix_ref, draft_ref, out_ref, stats_ref, *, heads, head_size
):
    draft, width = query_ref.shape
    slots = suffix_ref.shape[1]
    rows = heads * draft
    query = query_ref[...]
    masks = [
        lane_mask((draft, width), head * head_size, (head + 1) * head_size)
        for head in range(heads)
    ]
    spread = jnp.concatenate(
        [jnp.where(mask, query, jnp.zeros_like(query)) for mask in masks], axis=0
    )
    row = lax.broadcasted_iota(jnp.int32, (rows, 1), 0)
    slope = jnp.zeros((rows, 1), F32)
    for head in range(heads):
        slope = jnp.where(row // draft == head, slopes_ref[head], slope)
    scale = 1.0 / math.sqrt(head_size)
    length = length_ref[0]
    contract = (((1,), (1,)), ((), ()))
    slot = lax.broadcasted_iota(jnp.int32, (rows, slots), 1)
    suffix_scores = lax.dot_general(spread, suffix_ref[0], contract, preferred_element_type=F32)
    suffix_scores = suffix_scores * scale + slope * slot.astype(F32)
    suffix_scores = jnp.where(slot < length, suffix_scores, -jnp.inf)
    place = lax.broadcasted_iota(jnp.int32, (rows, draft), 1)
    draft_scores = lax.dot_general(spread, draft_ref[0], contract, preferred_element_type=F32)
    draft_scores = draft_scores * scale + slope * (place + length).astype(F32)
    token = lax.broadcasted_iota(jnp.int32, (rows, draft), 0) % draft
    draft_scores = jnp.where(place <= token, draft_scores, -jnp.inf)
    top = jnp.maximum(
        jnp.max(suffix_scores, axis=1, keepdims=True), jnp.max(draft_scores, axis=1, keepdims=True)
    )
    suffix_weights = jnp.exp(suffix_scores - top)
    draft_weights = jnp.exp(draft_scores - top)
    total = jnp.sum(suffix_weights, axis=1, keepdims=True) + jnp.sum(
        draft_weights, axis=1, keepdims=True
    )
    sums = jnp.dot(suffix_weights.astype(BF16), suffix_ref[1], preferred_element_type=F32)
    sums += jnp.dot(draft_weights.astype(BF16), draft_ref[1], preferred_element_type=F32)
    sums = sums * (1.0 / total)
    level = top + jnp.log(total)
    result = jnp.zeros((draft, width), F32)
    stats = jnp.zeros((draft, LANES), F32)
    lane = lax.broadcasted_iota(jnp.int32, (draft, LANES), 1)
    for head in range(heads):
        rows_of = slice(head * draft, (head + 1) * draft)
        result = jnp.where(masks[head], sums[rows_of], result)
        stats = jnp.where(lane == head, level[rows_of], stats)
    out_ref[...] = result
    stats_ref[...] = stats


def own_part(query_rows, suffix_kv, draft_kv, slopes, length):
    draft, width = query_rows.shape
    heads = slopes.shape[0]
    vmem = pl.BlockSpec(memory_space=pltpu.VMEM)
    smem = pl.BlockSpec(memory_space=pltpu.SMEM)
    return pl.pallas_call(
        functools.partial(own_kernel, heads=heads, head_size=width // heads),
        out_shape=(
            jax.ShapeDtypeStruct((draft, width), F32),
            jax.ShapeDtypeStruct((draft, LANES), F32),
        ),
        in_specs=[smem, smem, vmem, vmem, vmem],
        out_specs=(vmem, vmem),
        compiler_params=pltpu.CompilerParams(vmem_limit_bytes=24 * 1024 * 1024),
    )(length, slopes, query_rows, suffix_kv, draft_kv)


def merge_kernel(parts_ref, own_ref, level_ref, out_ref, *, heads, head_size):
    count, draft, _ = parts_ref.shape
    width = own_ref.shape[1]
    tiles = width // LANES
    levels = [level_ref[...]]
    for part in range(count):
        packed = parts_ref[part, :, width:].astype(F32)
        levels.append(
            packed
            + pltpu.roll(packed, LANES - heads, 1)
            + pltpu.roll(packed, LANES - 2 * heads, 1)
        )
    top = functools.reduce(jnp.maximum, levels)
    shares = [jnp.exp(level - top) for level in levels]
    total = functools.reduce(jnp.add, shares)
    shares = [share / total for share in shares]
    for tile in range(tiles):
        lanes = slice(tile * LANES, (tile + 1) * LANES)
        joined = jnp.zeros((draft, LANES), F32)
        for part, share in enumerate(shares):
            factor = jnp.zeros((draft, LANES), F32)
            for head in range(heads):
                first, last = head_lanes(head, tile, head_size)
                if first < last:
                    factor = jnp.where(
                        lane_mask((draft, LANES), first, last), share[:, head : head + 1], factor
                    )
            value = own_ref[:, lanes] if part == 0 else parts_ref[part - 1, :, lanes].astype(F32)
            joined += factor * value
        out_ref[:, lanes] = joined.astype(BF16)


def merge_parts(parts, own, level, heads):
    draft, width = own.shape
    vmem = pl.BlockSpec(memory_space=pltpu.VMEM)
    return pl.pallas_call(
        functools.partial(merge_kernel, heads=heads, head_size=width // heads),
        out_shape=jax.ShapeDtypeStruct((draft, width), BF16),
        in_specs=[vmem, vmem, vmem],
        out_specs=vmem,
    )(parts, own, level)


def residual_kernel(parts_ref, out_ref, sums_ref, *, sources):
    req, mp, pair, draft, columns = parts_ref.shape
    blocks = []
    for half in range(pair):
        for source in range(req):
            block = parts_ref[source, 0, half].astype(F32)
            for piece in range(1, mp):
                block += parts_ref[source, piece, half].astype(F32)
            blocks.append(block)
    residual = jnp.concatenate(blocks, axis=1)
    out_ref[...] = residual
    lane = lax.broadcasted_iota(jnp.int32, (draft, LANES), 1)
    first = jnp.sum(residual, axis=1, keepdims=True)
    second = jnp.sum(residual * residual, axis=1, keepdims=True)
    sums_ref[...] = jnp.where(lane == 0, first, jnp.where(lane == 1, second, 0.0))


def residual_rows(parts):
    req, mp, pair, draft, columns = parts.shape
    vmem = pl.BlockSpec(memory_space=pltpu.VMEM)
    return pl.pallas_call(
        functools.partial(residual_kernel, sources=mp),
        out_shape=(
            jax.ShapeDtypeStruct((draft, req * pair * columns), F32),
            jax.ShapeDtypeStruct((draft, LANES), F32),
        ),
        in_specs=[vmem],
        out_specs=(vmem, vmem),
    )(parts)


def norm_kernel(residual_ref, sums_ref, gain_ref, out_ref, *, model_width):
    sums = sums_ref[0]
    for part in range(1, sums_ref.shape[0]):
        sums += sums_ref[part]
    mean = sums[:, 0:1] / model_width
    mean_square = sums[:, 1:2] / model_width
    factor = lax.rsqrt(mean_square - mean * mean + 1e-05)
    out_ref[...] = ((residual_ref[...] - mean) * factor * gain_ref[...]).astype(BF16)


def norm_rows(residual, sums, gain, model_width):
    vmem = pl.BlockSpec(memory_space=pltpu.VMEM)
    return pl.pallas_call(
        functools.partial(norm_kernel, model_width=model_width),
        out_shape=jax.ShapeDtypeStruct(residual.shape, BF16),
        in_specs=[vmem, vmem, vmem],
        out_specs=vmem,
    )(residual, sums, gain[None, :])


def spread_to_all(value, axis):
    count = lax.axis_size(axis)
    return exchange(jnp.broadcast_to(value[None], (count,) + value.shape), axis)


def exchange(value, axis):
    return lax.all_to_all(value, axis, split_axis=0, concat_axis=0, tiled=True)


def per_device(
    token_ids,
    embed_table,
    queries,
    draft_kv,
    prefix_kv,
    suffix_kv,
    suffix_len,
    slopes,
    out_weight,
    ln_gain,
    up_weight,
    down_weight,
):
    heads = slopes.shape[0]
    _, draft, width = queries.shape
    prompt_local = prefix_kv.shape[1]
    ctx_count = lax.axis_size("ctx")
    req_count = lax.axis_size("req")
    mp_count = lax.axis_size("mp")
    ctx_index = lax.axis_index("ctx")
    model_index = lax.axis_index("mp")
    quarter = ln_gain.shape[0]
    rows = req_count * draft
    columns = out_weight.shape[1]
    hidden = up_weight.shape[1]

    out_all = lax.all_gather(out_weight, "ctx")
    up_all = lax.all_gather(up_weight, "ctx")
    down_all = lax.all_gather(down_weight, "ctx")

    gathered = spread_to_all(queries[0], "ctx").reshape(ctx_count * draft, width)
    own, own_level = own_part(
        queries[0], suffix_kv[:, 0], draft_kv[:, 0], slopes, suffix_len
    )
    vocab_local = embed_table.shape[0]
    shifted = token_ids.reshape(-1) - model_index * vocab_local
    one_hot = (
        shifted[:, None] == jnp.arange(vocab_local, dtype=jnp.int32)[None, :]
    ).astype(BF16)
    looked_up = jnp.dot(one_hot, embed_table, preferred_element_type=F32).astype(BF16)
    embedded = exchange(looked_up.reshape(ctx_count, rows, columns), "ctx")

    offset = (prompt_local * (ctx_count - ctx_index)).astype(jnp.int32).reshape(1)
    parts = prompt_part(gathered, prefix_kv, slopes, offset)
    parts = exchange(parts.reshape(ctx_count, draft, -1), "ctx")
    attended = merge_parts(parts, own, own_level, heads)

    attended_rows = spread_to_all(attended, "req").reshape(rows, width)
    projected = jnp.einsum(
        "mk,ckn->cmn", attended_rows, out_all, preferred_element_type=F32
    ) + embedded.astype(F32)
    pair = ctx_count // mp_count
    message = (
        projected.astype(BF16)
        .reshape(mp_count, pair, req_count, draft, columns)
        .transpose(2, 0, 1, 3, 4)
        .reshape(req_count * mp_count, pair, draft, columns)
    )
    message = exchange(message, ("req", "mp"))
    residual, sums = residual_rows(message.reshape(req_count, mp_count, pair, draft, columns))
    normed = norm_rows(residual, spread_to_all(sums, "mp"), ln_gain, quarter * mp_count)

    normed_rows = spread_to_all(normed, "req").reshape(rows, quarter)
    lifted = jnp.einsum("mk,ckn->cmn", normed_rows, up_all, preferred_element_type=F32)
    share = rows // mp_count
    lifted = exchange(
        lifted.astype(BF16)
        .reshape(ctx_count, mp_count, share, hidden)
        .transpose(1, 0, 2, 3),
        "mp",
    )
    activated = jax.nn.gelu(jnp.sum(lifted.astype(F32), axis=0), approximate=False).astype(BF16)
    activated = (
        spread_to_all(activated, "mp").transpose(1, 0, 2, 3).reshape(ctx_count, rows, hidden)
    )
    lowered = jnp.einsum("cmh,chn->mn", activated, down_all, preferred_element_type=F32)
    lowered = exchange(lowered.astype(BF16).reshape(req_count, draft, quarter), "req")
    layer_out = residual + jnp.sum(lowered.astype(F32), axis=0)
    return residual[None], layer_out[None]


def solution(mesh):
    in_specs = (
        P(),
        P("mp", ("ctx", "req")),
        P(("ctx", "req"), None, "mp"),
        P(None, ("ctx", "req"), None, "mp"),
        P(None, "ctx", "mp"),
        P(None, ("ctx", "req"), None, "mp"),
        P(("ctx", "req")),
        P("mp"),
        P("mp", ("ctx", "req")),
        P("mp"),
        P("mp", ("ctx", "req")),
        P(("ctx", "req"), "mp"),
    )
    out_specs = (P(("ctx", "req"), None, "mp"), P(("ctx", "req"), None, "mp"))
    return jax.shard_map(
        per_device, mesh=mesh, in_specs=in_specs, out_specs=out_specs, check_vma=False
    )
```

time: 559 us -> 193 us (0.35)
  waiting for transfers between devices: 396 us -> 34.1 us
  starting transfers between devices: 0.43 us -> 29.6 us
  local copies, waits for them, and re-layouts: 42 us -> 22 us
  Pallas kernels: 0 us -> 18.5 us
  matrix products: 27.6 us -> 16.1 us
  other arithmetic: 12.2 us -> 2.45 us
  blocking collectives: 63.8 us -> 54.4 us
    all_gather x3, waiting for transfers between devices: 154 us -> 0.04 us  [the longest x1 0.02 us: per_device(): up_all = lax.all_gather(up_weight, 'ctx')]
    reduce_scatter x1 -> x0, waiting for transfers between devices: 152 us -> none  [per_device(): lax.psum_scatter(jnp.dot(activated, down_weight, preferred_element_type=j...]
    psum x2 -> x0, waiting for transfers between devices: 90.4 us -> none  [the longest x1 47.2 us: per_device(): hidden_total = lax.psum(lifted, 'mp')]
    all_gather x3 -> x0, blocking collectives: 39.1 us -> none  [the longest x2 25.8 us: joined(): pieces = jax.tree.map(lambda part: lax.all_gather(part, axis), value)]
    all_to_all x0 -> x6, waiting for transfers between devices: none -> 32 us  [exchange(): return lax.all_to_all(value, axis, split_axis=0, concat_axis=0, tiled=True)]
    all_to_all x1 -> x4, blocking collectives: 24.7 us -> 54.4 us  [exchange(): return lax.all_to_all(value, axis, split_axis=0, concat_axis=0, tiled=True)]
    all_to_all x0 -> x6, starting transfers between devices: none -> 29.5 us  [exchange(): return lax.all_to_all(value, axis, split_axis=0, concat_axis=0, tiled=True)]
    slice x12 -> x0, local copies, waits for them, and re-layouts: 26.3 us -> none  [the longest x2 12.9 us: per_device(): prefix_kv[1][None]]
  transfers between devices with their start and end apart: 6 -> 9, of which waited for: 5 -> 6; matrix products, arithmetic and copies ran while one was open for 3% -> 15% of each run, Pallas kernels for 0% -> 10%
where the time goes in v1:
time: 193 us; the launch traced here: 192 us
  blocking collectives  54.4 us (28%)
  waiting for transfers between devices  34.1 us (18%)
  starting transfers between devices  29.6 us (15%)
  local copies, waits for them, and re-layouts  22 us (11%)
  Pallas kernels  18.5 us (10%)
  matrix products  16.1 us (8%)
  between operations  14.7 us (8%)
  other arithmetic  2.45 us (1%)
    all_to_all x4, blocking collectives, exchange(): return lax.all_to_all(value, axis, split_axis=0, concat_axis=0, tiled=True)  54.4 us
    all_to_all x6, waiting for transfers between devices, exchange(): return lax.all_to_all(value, axis, split_axis=0, concat_axis=0, tiled=True)  32 us
    all_to_all x6, starting transfers between devices, exchange(): return lax.all_to_all(value, axis, split_axis=0, concat_axis=0, tiled=True)  29.5 us
    pallas_call x1, Pallas kernels, prompt_part(): pl.pallas_call(functools.partial(prompt_kernel, heads=heads, head_size=wi...  11.5 us
    unnamed x28, local copies, waits for them, and re-layouts  6.55 us
    unnamed x2, matrix products  6.21 us
    all_gather x1, local copies, waits for them, and re-layouts, per_device(): up_all = lax.all_gather(up_weight, 'ctx')  5.99 us
    dot_general x1, matrix products, per_device(): jnp.dot(one_hot, embed_table, preferred_element_type=F32).astype(BF16)  5.97 us
  transfers between devices with their start and end apart: 9, of which 6 were waited for; matrix products, arithmetic and copies ran while one was open for 15% of the time, Pallas kernels for 10%

profile of v1, /device:TPU:2, one launch (start us, length us, event | category | flops | bytes accessed | tf_op | source)
XLA Modules:
  0.0 191.9 jit_solution(6672642944285823428)
XLA Ops:
  7.3 0.7 all-gather.7.cloned.1.call-update
  8.0 0.7 all-gather.9.cloned.1.call-update
  8.8 0.7 all-gather.11.cloned.1.call-update
  9.4 1.5 broadcast_in_dim.19
  10.9 4.5 %all-to-all-start = ((bf16[8,16,896]{2,1,0:T(8,128)(2,1)}), bf16[8,16,896]{2,1,0:T(8,128)(2,1)S(1)}, u32[]{:S(2)}, u32[]{:S(2)}) async-start(bf16[8,16,896]{2,1,0:T(8,128)(2,1)} %broadcast_in_dim.19), calls=%async_computation | async-start | bytes 458752 | tf_op jit(solution)/shard_map/all_to_all | solution.py:306
  15.4 7.2 %all-to-all-done = bf16[8,16,896]{2,1,0:T(8,128)(2,1)S(1)} async-done(((bf16[8,16,896]{2,1,0:T(8,128)(2,1)}), bf16[8,16,896]{2,1,0:T(8,128)(2,1)S(1)}, u32[]{:S(2)}, u32[]{:S(2)}) %all-to-all-start) | async-done | bytes 229408 | tf_op jit(solution)/shard_map/all_to_all | solution.py:306
  22.6 3.2 %copy-done.1 = bf16[2,2048,896]{2,1,0:T(8,128)(2,1)S(1)} copy-done((bf16[2,2048,896]{2,1,0:T(8,128)(2,1)S(1)}, bf16[2,2048,896]{2,1,0:T(8,128)(2,1)}, u32[]{:S(2)}) %copy-start.1) | copy-done | bytes 7340056
  25.8 0.7 copy-done.7
  26.4 11.5 %shard_map.131 = bf16[128,1024]{1,0:T(8,128)(2,1)} custom-call(s32[1]{0:T(128)} %bitcast.offset_ref, f32[8]{0:T(128)S(1)} %copy-done.7, bf16[128,896]{1,0:T(8,128)(2,1)S(1)} %bitcast.60, bf16[2,2048,896]{2,1,0:T(8,128)(2,1)S(1)} %copy-done.1), custom_call_target="tpu_custom_call" | custom-call | tf_op jit(solution)/shard_map/pallas_call | solution.py:118
  38.0 4.1 %all-to-all-start.1 = ((bf16[8,16,1024]{2,1,0:T(8,128)(2,1)}), bf16[8,16,1024]{2,1,0:T(8,128)(2,1)}, u32[]{:S(2)}, u32[]{:S(2)}) async-start(bf16[8,16,1024]{2,1,0:T(8,128)(2,1)} %bitcast.3), calls=%async_computation.1 | async-start | bytes 524288 | tf_op jit(solution)/shard_map/all_to_all | solution.py:306
  42.9 0.8 copy-done.4
  43.7 1.6 shard_map.132
  45.3 0.6 copy-done.5
  46.0 0.6 copy-done.6
  46.6 3.0 %all-to-all-done.1.parts_ref = bf16[8,16,1024]{2,1,0:T(8,128)(2,1)} async-done(((bf16[8,16,1024]{2,1,0:T(8,128)(2,1)}), bf16[8,16,1024]{2,1,0:T(8,128)(2,1)}, u32[]{:S(2)}, u32[]{:S(2)}) %all-to-all-start.1) | async-done | bytes 262176 | tf_op jit(solution)/shard_map/all_to_all | solution.py:306
  49.6 2.0 %shard_map.133 = bf16[16,896]{1,0:T(8,128)(2,1)} custom-call(bf16[8,16,1024]{2,1,0:T(8,128)(2,1)} %all-to-all-done.1.parts_ref, f32[16,896]{1,0:T(8,128)} %copy-done.5, f32[16,128]{1,0:T(8,128)} %copy-done.6), custom_call_target="tpu_custom_call" | custom-call | tf_op jit(solution)/shard_map/pallas_call | solution.py:241
  51.5 1.5 broadcast_in_dim.20
  53.0 8.5 %all-to-all-start.2 = ((bf16[8,16,896]{2,1,0:T(8,128)(2,1)}), bf16[8,16,896]{2,1,0:T(8,128)(2,1)S(1)}, u32[]{:S(2)}, u32[]{:S(2)}) async-start(bf16[8,16,896]{2,1,0:T(8,128)(2,1)} %broadcast_in_dim.20), calls=%async_computation.2 | async-start | bytes 458752 | tf_op jit(solution)/shard_map/all_to_all | solution.py:306
  61.5 6.0 %fusion.4 = bf16[14,8,8,128]{3,2,1,0:T(8,128)(2,1)S(1)} fusion(bf16[6400,112]{0,1:T(8,128)(2,1)S(1)} %copy-done, s32[1024]{0:T(1024)S(1)} %sub.19), kind=kOutput, calls=%fused_computation.8 | convolution fusion | flops 1474674688 | bytes 1667072 | tf_op jit(solution)/shard_map/dot_general | solution.py:349
  67.5 0.7 copy.49
  68.3 1.6 copy.48
  69.8 2.5 %all-to-all-done.2 = bf16[8,16,896]{2,1,0:T(8,128)(2,1)S(1)} async-done(((bf16[8,16,896]{2,1,0:T(8,128)(2,1)}), bf16[8,16,896]{2,1,0:T(8,128)(2,1)S(1)}, u32[]{:S(2)}, u32[]{:S(2)}) %all-to-all-start.2) | async-done | bytes 229408 | tf_op jit(solution)/shard_map/all_to_all | solution.py:306
  72.3 4.0 %all-to-all-start.3 = ((bf16[8,128,112]{1,2,0:T(8,128)(2,1)}), bf16[8,128,112]{1,2,0:T(8,128)(2,1)}, u32[]{:S(2)}, u32[]{:S(2)}) async-start(bf16[8,128,112]{1,2,0:T(8,128)(2,1)} %bitcast.58), calls=%async_computation.3 | async-start | bytes 458752 | tf_op jit(solution)/shard_map/all_to_all | solution.py:306
  76.4 1.6 fusion.15
  78.0 8.4 %all-to-all-done.3 = bf16[8,128,112]{1,2,0:T(8,128)(2,1)} async-done(((bf16[8,128,112]{1,2,0:T(8,128)(2,1)}), bf16[8,128,112]{1,2,0:T(8,128)(2,1)}, u32[]{:S(2)}, u32[]{:S(2)}) %all-to-all-start.3) | async-done | bytes 229408 | tf_op jit(solution)/shard_map/all_to_all | solution.py:306
  86.4 1.0 add_convert_fusion
  87.3 0.2 copy.33
  87.6 18.7 %all_to_all.50 = bf16[32,2,16,112]{3,2,1,0:T(8,128)(2,1)} all-to-all(bf16[32,2,16,112]{3,2,1,0:T(8,128)(2,1)S(1)} %bitcast.77), channel_id=1, replica_groups=mesh['ctx'=8,'req'=8,'mp'=4] {'req','mp'}, dimensions={0} | all-to-all | bytes 458752 | tf_op jit(solution)/shard_map/all_to_all | solution.py:306
  106.3 1.7 shard_map.134
  108.0 1.3 broadcast_in_dim.22
  109.3 4.9 %all-to-all-start.5 = ((f32[4,16,128]{2,1,0:T(8,128)}), f32[4,16,128]{2,1,0:T(8,128)S(1)}, u32[]{:S(2)}, u32[]{:S(2)}) async-start(f32[4,16,128]{2,1,0:T(8,128)} %broadcast_in_dim.22), calls=%async_computation.5 | async-start | bytes 65536 | tf_op jit(solution)/shard_map/all_to_all | solution.py:306
  114.3 0.6 broadcast_in_dim.23.gain_ref
  114.9 3.4 %all-to-all-done.5.sums_ref = f32[4,16,128]{2,1,0:T(8,128)S(1)} async-done(((f32[4,16,128]{2,1,0:T(8,128)}), f32[4,16,128]{2,1,0:T(8,128)S(1)}, u32[]{:S(2)}, u32[]{:S(2)}) %all-to-all-start.5) | async-done | bytes 32800 | tf_op jit(solution)/shard_map/all_to_all | solution.py:306
  118.3 0.6 copy-done.11
  118.9 1.7 shard_map.135
  120.6 1.6 broadcast_in_dim.48
  122.2 3.5 %all-to-all-start.6 = ((bf16[8,16,1792]{2,1,0:T(8,128)(2,1)}), bf16[8,16,1792]{2,1,0:T(8,128)(2,1)S(1)}, u32[]{:S(2)}, u32[]{:S(2)}) async-start(bf16[8,16,1792]{2,1,0:T(8,128)(2,1)} %broadcast_in_dim.48), calls=%async_computation.6 | async-start | bytes 917504 | tf_op jit(solution)/shard_map/all_to_all | solution.py:306
  125.7 6.0 %copy.47 = bf16[28,8,8,1792]{3,2,0,1:T(8,128)(2,1)} copy(bf16[28,8,8,1792]{3,2,1,0:T(8,128)(2,1)} %bitcast.66) | data formatting | bytes 12845056 | tf_op jit(solution)/shard_map/all_gather | solution.py:337
  131.7 7.5 %all-to-all-done.6 = bf16[8,16,1792]{2,1,0:T(8,128)(2,1)S(1)} async-done(((bf16[8,16,1792]{2,1,0:T(8,128)(2,1)}), bf16[8,16,1792]{2,1,0:T(8,128)(2,1)S(1)}, u32[]{:S(2)}, u32[]{:S(2)}) %all-to-all-start.6) | async-done | bytes 458784 | tf_op jit(solution)/shard_map/all_to_all | solution.py:306
  139.2 4.7 %fusion.16 = f32[128,1792]{0,1:S(1)} fusion(bf16[128,1792]{1,0:T(8,128)(2,1)S(1)} %bitcast.68, bf16[1792,1792]{0,1:T(8,128)(2,1)} %bitcast.64), kind=kOutput, calls=%fused_computation.36 | convolution fusion | flops 822083584 | bytes 7798784
  143.9 0.2 copy.36
  144.2 10.3 %all_to_all.51 = bf16[4,8,32,224]{3,2,1,0:T(8,128)(2,1)S(1)} all-to-all(bf16[4,8,32,224]{3,2,1,0:T(8,128)(2,1)S(1)} %copy.37), channel_id=1, replica_groups=mesh['ctx'=8,'req'=8,'mp'=4] {'mp'}, dimensions={0} | all-to-all | bytes 917504 | tf_op jit(solution)/shard_map/all_to_all | solution.py:306
  154.5 0.1 convert_reduce_fusion
  154.5 0.6 fusion.7
  155.2 10.5 %all_to_all.52 = bf16[4,8,32,224]{3,2,1,0:T(8,128)(2,1)S(1)} all-to-all(bf16[4,8,32,224]{3,2,1,0:T(8,128)(2,1)S(1)} %broadcast_in_dim.49), channel_id=1, replica_groups=mesh['ctx'=8,'req'=8,'mp'=4] {'mp'}, dimensions={0} | all-to-all | bytes 917504 | tf_op jit(solution)/shard_map/all_to_all | solution.py:306
  165.7 3.9 %fusion.2 = bf16[128,1792]{1,0:T(8,128)(2,1)S(1)} fusion(bf16[8,128,224]{2,1,0:T(8,128)(2,1)S(1)} %bitcast.70, bf16[8,224,1792]{2,1,0:T(8,128)(2,1)} %bitcast.65), kind=kOutput, calls=%fused_computation.5 | convolution fusion | flops 822312960 | bytes 7340032 | tf_op jit(solution)/shard_map/cmh,chn->mn/dot_general | solution.py:385
  169.6 15.0 %all_to_all.53 = bf16[8,16,1792]{2,1,0:T(8,128)(2,1)S(1)} all-to-all(bf16[8,16,1792]{2,1,0:T(8,128)(2,1)S(1)} %bitcast.74), channel_id=1, replica_groups=mesh['ctx'=8,'req'=8,'mp'=4] {'req'}, dimensions={0} | all-to-all | bytes 917504 | tf_op jit(solution)/shard_map/all_to_all | solution.py:306
  184.7 0.7 add_bitcast_fusion
  (37 shorter events, 0.6 us)
Async XLA Ops:
  7.2 54.4 %copy-start = (bf16[6400,112]{0,1:T(8,128)(2,1)S(1)}, bf16[6400,112]{0,1:T(8,128)(2,1)}, u32[]{:S(2)}) copy-start(bf16[6400,112]{0,1:T(8,128)(2,1)} %param.13) | copy-start | bytes 4300804
  7.2 35.7 %copy-start.3 = (bf16[1,16,896]{2,1,0:T(8,128)(2,1)S(1)}, bf16[1,16,896]{2,1,0:T(8,128)(2,1)}, u32[]{:S(2)}) copy-start(bf16[1,16,896]{2,1,0:T(8,128)(2,1)} %param.14) | copy-start | bytes 86020
  7.2 35.7 %copy-start.8 = (f32[8]{0:T(128)S(1)}, f32[8]{0:T(128)}, u32[]{:S(2)}) copy-start(f32[8]{0:T(128)} %slopes_ref.3) | copy-start | bytes 100
  7.2 35.5 %copy-start.12 = (s32[64,16]{0,1:T(8,128)S(1)}, s32[64,16]{0,1:T(8,128)}, u32[]{:S(2)}) copy-start(s32[64,16]{0,1:T(8,128)} %param.12) | copy-start | bytes 12292
  7.2 35.7 %copy-start.2 = (bf16[2,1,512,896]{3,2,1,0:T(8,128)(2,1)S(1)}, bf16[2,1,512,896]{3,2,1,0:T(8,128)(2,1)}, u32[]{:S(2)}) copy-start(bf16[2,1,512,896]{3,2,1,0:T(8,128)(2,1)} %param.17) | copy-start | bytes 5505028
  7.2 61.0 %all-gather.7.cloned.1.call-start = ((), (), s32[]{:S(2)}) async-start(), calls=%async_computation.10 | async-start | bytes 1806336 | tf_op jit(solution)/shard_map/all_gather | solution.py:336
  8.0 117.8 %all-gather.9.cloned.1.call-start = ((), (), s32[]{:S(2)}) async-start(), calls=%async_computation.11 | async-start | bytes 7225344 | tf_op jit(solution)/shard_map/all_gather | solution.py:337
  8.7 157.0 %all-gather.11.cloned.1.call-start = ((), (), s32[]{:S(2)}) async-start(), calls=%async_computation.12 | async-start | bytes 7225344 | tf_op jit(solution)/shard_map/all_gather | solution.py:338
  10.9 11.7 %all-to-all-start = ((bf16[8,16,896]{2,1,0:T(8,128)(2,1)}), bf16[8,16,896]{2,1,0:T(8,128)(2,1)S(1)}, u32[]{:S(2)}, u32[]{:S(2)}) async-start(bf16[8,16,896]{2,1,0:T(8,128)(2,1)} %broadcast_in_dim.19), calls=%async_computation | async-start | bytes 458752 | tf_op jit(solution)/shard_map/all_to_all | solution.py:306
  22.6 3.2 %copy-start.1 = (bf16[2,2048,896]{2,1,0:T(8,128)(2,1)S(1)}, bf16[2,2048,896]{2,1,0:T(8,128)(2,1)}, u32[]{:S(2)}) copy-start(bf16[2,2048,896]{2,1,0:T(8,128)(2,1)} %prefix_ref.1) | copy-start | bytes 22020100
  25.8 0.7 copy-start.7
  38.0 11.6 %all-to-all-start.1 = ((bf16[8,16,1024]{2,1,0:T(8,128)(2,1)}), bf16[8,16,1024]{2,1,0:T(8,128)(2,1)}, u32[]{:S(2)}, u32[]{:S(2)}) async-start(bf16[8,16,1024]{2,1,0:T(8,128)(2,1)} %bitcast.3), calls=%async_computation.1 | async-start | bytes 524288 | tf_op jit(solution)/shard_map/all_to_all | solution.py:306
  42.9 0.8 copy-start.4
  45.3 0.6 copy-start.5
  46.0 0.6 copy-start.6
  53.0 19.3 %all-to-all-start.2 = ((bf16[8,16,896]{2,1,0:T(8,128)(2,1)}), bf16[8,16,896]{2,1,0:T(8,128)(2,1)S(1)}, u32[]{:S(2)}, u32[]{:S(2)}) async-start(bf16[8,16,896]{2,1,0:T(8,128)(2,1)} %broadcast_in_dim.20), calls=%async_computation.2 | async-start | bytes 458752 | tf_op jit(solution)/shard_map/all_to_all | solution.py:306
  67.5 46.7 %copy-start.13 = (f32[1792]{0:T(1024)S(1)}, f32[1792]{0:T(1024)}, u32[]{:S(2)}) copy-start(f32[1792]{0:T(1024)} %param.21) | copy-start | bytes 21508
  72.3 4.0 %copy-start.9 = (bf16[8,16,896]{2,1,0:T(8,128)(2,1)}, bf16[8,16,896]{2,1,0:T(8,128)(2,1)S(1)}, u32[]{:S(2)}) copy-start(bf16[8,16,896]{2,1,0:T(8,128)(2,1)S(1)} %all-to-all-done.2) | copy-start | bytes 688132
  72.3 14.0 %all-to-all-start.3 = ((bf16[8,128,112]{1,2,0:T(8,128)(2,1)}), bf16[8,128,112]{1,2,0:T(8,128)(2,1)}, u32[]{:S(2)}, u32[]{:S(2)}) async-start(bf16[8,128,112]{1,2,0:T(8,128)(2,1)} %bitcast.58), calls=%async_computation.3 | async-start | bytes 458752 | tf_op jit(solution)/shard_map/all_to_all | solution.py:306
  109.3 8.9 %all-to-all-start.5 = ((f32[4,16,128]{2,1,0:T(8,128)}), f32[4,16,128]{2,1,0:T(8,128)S(1)}, u32[]{:S(2)}, u32[]{:S(2)}) async-start(f32[4,16,128]{2,1,0:T(8,128)} %broadcast_in_dim.22), calls=%async_computation.5 | async-start | bytes 65536 | tf_op jit(solution)/shard_map/all_to_all | solution.py:306
  118.3 0.6 copy-start.11
  122.2 17.0 %all-to-all-start.6 = ((bf16[8,16,1792]{2,1,0:T(8,128)(2,1)}), bf16[8,16,1792]{2,1,0:T(8,128)(2,1)S(1)}, u32[]{:S(2)}, u32[]{:S(2)}) async-start(bf16[8,16,1792]{2,1,0:T(8,128)(2,1)} %broadcast_in_dim.48), calls=%async_computation.6 | async-start | bytes 917504 | tf_op jit(solution)/shard_map/all_to_all | solution.py:306
  165.7 19.0 %copy-start.10 = (f32[16,1792]{1,0:T(8,128)S(1)}, f32[16,1792]{1,0:T(8,128)}, u32[]{:S(2)}) copy-start(f32[16,1792]{1,0:T(8,128)} %get-tuple-element.8.residual_ref) | copy-start | bytes 344068
Sparse Core Ops, SparseCore 0:
  9.9 30.1 all-gather.6
  42.0 46.4 all-gather.8
  90.3 44.1 all-gather.10

commit v2 on v1

--- a/solution.py
+++ b/solution.py
@@ -11,6 +11,7 @@
 LANES = 128
 F32 = jnp.float32
 BF16 = jnp.bfloat16
+WHOLE_VMEM = 60 * 1024 * 1024
 
 
 def head_lanes(head, tile, head_size):
@@ -122,14 +123,14 @@
             pl.BlockSpec(memory_space=pltpu.SMEM),
             pl.BlockSpec(memory_space=pltpu.SMEM),
             pl.BlockSpec(memory_space=pltpu.VMEM),
-            pl.BlockSpec(memory_space=pl.ANY),
+            pl.BlockSpec(memory_space=pltpu.HBM),
         ],
         out_specs=pl.BlockSpec(memory_space=pltpu.VMEM),
         scratch_shapes=[
             pltpu.VMEM((2, tiles, keys, LANES), BF16),
             pltpu.SemaphoreType.DMA((2, tiles)),
         ],
-        compiler_params=pltpu.CompilerParams(vmem_limit_bytes=40 * 1024 * 1024),
+        compiler_params=pltpu.CompilerParams(vmem_limit_bytes=WHOLE_VMEM),
     )(offset, slopes, query_rows, prefix_kv)
 
 
@@ -232,44 +233,44 @@
                     )
             value = own_ref[:, lanes] if part == 0 else parts_ref[part - 1, :, lanes].astype(F32)
             joined += factor * value
-        out_ref[:, lanes] = joined.astype(BF16)
-
-
-def merge_parts(parts, own, level, heads):
+        joined = joined.astype(BF16)
+        for target in range(out_ref.shape[0]):
+            out_ref[target, :, lanes] = joined
+
+
+def merge_parts(parts, own, level, heads, targets):
     draft, width = own.shape
     vmem = pl.BlockSpec(memory_space=pltpu.VMEM)
     return pl.pallas_call(
         functools.partial(merge_kernel, heads=heads, head_size=width // heads),
-        out_shape=jax.ShapeDtypeStruct((draft, width), BF16),
+        out_shape=jax.ShapeDtypeStruct((targets, draft, width), BF16),
         in_specs=[vmem, vmem, vmem],
         out_specs=vmem,
     )(parts, own, level)
 
 
-def residual_kernel(parts_ref, out_ref, sums_ref, *, sources):
-    req, mp, pair, draft, columns = parts_ref.shape
+def residual_kernel(parts_ref, out_ref, sums_ref):
+    mp, pair, draft, columns = parts_ref.shape
     blocks = []
     for half in range(pair):
-        for source in range(req):
-            block = parts_ref[source, 0, half].astype(F32)
-            for piece in range(1, mp):
-                block += parts_ref[source, piece, half].astype(F32)
-            blocks.append(block)
-    residual = jnp.concatenate(blocks, axis=1)
-    out_ref[...] = residual
+        block = parts_ref[0, half].astype(F32)
+        for piece in range(1, mp):
+            block += parts_ref[piece, half].astype(F32)
+        blocks.append(block)
+        out_ref[:, half * columns : (half + 1) * columns] = block
     lane = lax.broadcasted_iota(jnp.int32, (draft, LANES), 1)
-    first = jnp.sum(residual, axis=1, keepdims=True)
-    second = jnp.sum(residual * residual, axis=1, keepdims=True)
+    first = sum(jnp.sum(block, axis=1, keepdims=True) for block in blocks)
+    second = sum(jnp.sum(block * block, axis=1, keepdims=True) for block in blocks)
     sums_ref[...] = jnp.where(lane == 0, first, jnp.where(lane == 1, second, 0.0))
 
 
 def residual_rows(parts):
-    req, mp, pair, draft, columns = parts.shape
-    vmem = pl.BlockSpec(memory_space=pltpu.VMEM)
-    return pl.pallas_call(
-        functools.partial(residual_kernel, sources=mp),
+    mp, pair, draft, columns = parts.shape
+    vmem = pl.BlockSpec(memory_space=pltpu.VMEM)
+    return pl.pallas_call(
+        residual_kernel,
         out_shape=(
-            jax.ShapeDtypeStruct((draft, req * pair * columns), F32),
+            jax.ShapeDtypeStruct((draft, pair * columns), F32),
             jax.ShapeDtypeStruct((draft, LANES), F32),
         ),
         in_specs=[vmem],
@@ -277,29 +278,146 @@
     )(parts)
 
 
-def norm_kernel(residual_ref, sums_ref, gain_ref, out_ref, *, model_width):
-    sums = sums_ref[0]
-    for part in range(1, sums_ref.shape[0]):
-        sums += sums_ref[part]
+def norm_kernel(residual_ref, gain_ref, *rest, model_width):
+    *sums_refs, out_ref = rest
+    sums = functools.reduce(jnp.add, [ref[...] for ref in sums_refs])
     mean = sums[:, 0:1] / model_width
     mean_square = sums[:, 1:2] / model_width
     factor = lax.rsqrt(mean_square - mean * mean + 1e-05)
-    out_ref[...] = ((residual_ref[...] - mean) * factor * gain_ref[...]).astype(BF16)
-
-
-def norm_rows(residual, sums, gain, model_width):
+    normed = ((residual_ref[...] - mean) * factor * gain_ref[...]).astype(BF16)
+    for target in range(out_ref.shape[0]):
+        out_ref[target] = normed
+
+
+def norm_rows(residual, sums, gain, model_width, targets):
     vmem = pl.BlockSpec(memory_space=pltpu.VMEM)
     return pl.pallas_call(
         functools.partial(norm_kernel, model_width=model_width),
-        out_shape=jax.ShapeDtypeStruct(residual.shape, BF16),
-        in_specs=[vmem, vmem, vmem],
+        out_shape=jax.ShapeDtypeStruct((targets,) + residual.shape, BF16),
+        in_specs=[vmem] * (2 + len(sums)),
         out_specs=vmem,
-    )(residual, sums, gain[None, :])
-
-
-def spread_to_all(value, axis):
+    )(residual, gain[None, :], *sums)
+
+
+def arriving(refs, buf, sems):
+    blocks = refs[0].shape[0]
+    copies = [
+        pltpu.make_async_copy(ref.at[block], buf.at[place * blocks + block], sems.at[place * blocks + block])
+        for place, ref in enumerate(refs)
+        for block in range(blocks)
+    ]
+    for copy in copies:
+        copy.start()
+
+    def block_at(index):
+        copies[index].wait()
+        return buf[index]
+
+    return block_at
+
+
+def lift_kernel(rows_ref, own_ref, other_ref, out_ref, buf, sems):
+    block_at = arriving((own_ref, other_ref), buf, sems)
+    rows = rows_ref[...]
+    shares, blocks, share, _ = out_ref.shape
+    for block in range(blocks):
+        lifted = lax.dot_general(
+            rows, block_at(block), (((1,), (1,)), ((), ())), preferred_element_type=F32
+        ).astype(BF16)
+        for piece in range(shares):
+            out_ref[piece, block] = lifted[piece * share : (piece + 1) * share]
+
+
+def lift_rows(rows, own, other, shares):
+    vmem = pl.BlockSpec(memory_space=pltpu.VMEM)
+    hbm = pl.BlockSpec(memory_space=pltpu.HBM)
+    blocks, hidden, width = own.shape
+    return pl.pallas_call(
+        lift_kernel,
+        out_shape=jax.ShapeDtypeStruct((shares, 2 * blocks, rows.shape[0] // shares, hidden), BF16),
+        in_specs=[vmem, hbm, hbm],
+        out_specs=vmem,
+        scratch_shapes=[
+            pltpu.VMEM((2 * blocks, hidden, width), BF16),
+            pltpu.SemaphoreType.DMA((2 * blocks,)),
+        ],
+        compiler_params=pltpu.CompilerParams(vmem_limit_bytes=WHOLE_VMEM),
+    )(rows, own, other)
+
+
+def gelu_kernel(parts_ref, out_ref):
+    total = parts_ref[0].astype(F32)
+    for piece in range(1, parts_ref.shape[0]):
+        total += parts_ref[piece].astype(F32)
+    activated = (0.5 * total * (1.0 + lax.erf(total * math.sqrt(0.5)))).astype(BF16)
+    for target in range(out_ref.shape[0]):
+        out_ref[target] = activated
+
+
+def activate(parts):
+    vmem = pl.BlockSpec(memory_space=pltpu.VMEM)
+    return pl.pallas_call(
+        gelu_kernel,
+        out_shape=jax.ShapeDtypeStruct(parts.shape, BF16),
+        in_specs=[vmem],
+        out_specs=vmem,
+    )(parts)
+
+
+def lower_kernel(hidden_ref, own_ref, other_ref, out_ref, buf, sems):
+    block_at = arriving((own_ref, other_ref), buf, sems)
+    shares, blocks, share, _ = hidden_ref.shape
+    targets, draft, width = out_ref.shape
+    total = None
+    for block in range(blocks):
+        rows = jnp.concatenate([hidden_ref[piece, block] for piece in range(shares)], axis=0)
+        product = jnp.dot(rows, block_at(block), preferred_element_type=F32)
+        total = product if total is None else total + product
+    out_ref[...] = total.astype(BF16).reshape(targets, draft, width)
+
+
+def lower_rows(hidden, own, other, targets):
+    vmem = pl.BlockSpec(memory_space=pltpu.VMEM)
+    hbm = pl.BlockSpec(memory_space=pltpu.HBM)
+    rows = hidden.shape[0] * hidden.shape[2]
+    blocks, features, width = own.shape
+    return pl.pallas_call(
+        lower_kernel,
+        out_shape=jax.ShapeDtypeStruct((targets, rows // targets, width), BF16),
+        in_specs=[vmem, hbm, hbm],
+        out_specs=vmem,
+        scratch_shapes=[
+            pltpu.VMEM((2 * blocks, features, width), BF16),
+            pltpu.SemaphoreType.DMA((2 * blocks,)),
+        ],
+        compiler_params=pltpu.CompilerParams(vmem_limit_bytes=WHOLE_VMEM),
+    )(hidden, own, other)
+
+
+def finish_kernel(parts_ref, residual_ref, out_ref):
+    total = parts_ref[0].astype(F32)
+    for piece in range(1, parts_ref.shape[0]):
+        total += parts_ref[piece].astype(F32)
+    out_ref[...] = residual_ref[...] + total
+
+
+def finish(parts, residual):
+    vmem = pl.BlockSpec(memory_space=pltpu.VMEM)
+    return pl.pallas_call(
+        finish_kernel,
+        out_shape=jax.ShapeDtypeStruct(residual.shape, F32),
+        in_specs=[vmem, vmem],
+        out_specs=vmem,
+    )(parts, residual)
+
+
+def after(value, earlier):
+    return lax.optimization_barrier((value, earlier))[0]
+
+
+def shifted_by(value, axis, step):
     count = lax.axis_size(axis)
-    return exchange(jnp.broadcast_to(value[None], (count,) + value.shape), axis)
+    return lax.ppermute(value, axis, [(i, (i + step) % count) for i in range(count)])
 
 
 def exchange(value, axis):
@@ -320,90 +438,89 @@
     up_weight,
     down_weight,
 ):
+    ctx = ("y", "core")
     heads = slopes.shape[0]
     _, draft, width = queries.shape
     prompt_local = prefix_kv.shape[1]
-    ctx_count = lax.axis_size("ctx")
+    ctx_count = lax.axis_size(ctx)
     req_count = lax.axis_size("req")
     mp_count = lax.axis_size("mp")
-    ctx_index = lax.axis_index("ctx")
+    ctx_index = lax.axis_index(ctx)
     model_index = lax.axis_index("mp")
     quarter = ln_gain.shape[0]
-    rows = req_count * draft
     columns = out_weight.shape[1]
-    hidden = up_weight.shape[1]
-
-    out_all = lax.all_gather(out_weight, "ctx")
-    up_all = lax.all_gather(up_weight, "ctx")
-    down_all = lax.all_gather(down_weight, "ctx")
-
-    gathered = spread_to_all(queries[0], "ctx").reshape(ctx_count * draft, width)
-    own, own_level = own_part(
-        queries[0], suffix_kv[:, 0], draft_kv[:, 0], slopes, suffix_len
-    )
+
+    copies = jnp.broadcast_to(queries, (ctx_count, draft, width))
+    gathered = exchange(copies, ctx)
+    out_all = lax.all_gather(out_weight.T, "req", tiled=True)
+    up_own = lax.all_gather(after(up_weight, copies).T, "y")
+    down_own = lax.all_gather(after(down_weight, copies), "y")
+
     vocab_local = embed_table.shape[0]
-    shifted = token_ids.reshape(-1) - model_index * vocab_local
+    shifted = (
+        token_ids.reshape(ctx_count, req_count, draft).transpose(1, 0, 2).reshape(-1)
+        - model_index * vocab_local
+    )
     one_hot = (
         shifted[:, None] == jnp.arange(vocab_local, dtype=jnp.int32)[None, :]
     ).astype(BF16)
     looked_up = jnp.dot(one_hot, embed_table, preferred_element_type=F32).astype(BF16)
-    embedded = exchange(looked_up.reshape(ctx_count, rows, columns), "ctx")
+    own, own_level = own_part(queries[0], suffix_kv[:, 0], draft_kv[:, 0], slopes, suffix_len)
+    gathered, looked_up, own = lax.optimization_barrier((gathered, looked_up, own))
+    embedded = exchange(looked_up.reshape(req_count, ctx_count * draft, columns), "req")
 
     offset = (prompt_local * (ctx_count - ctx_index)).astype(jnp.int32).reshape(1)
-    parts = prompt_part(gathered, prefix_kv, slopes, offset)
-    parts = exchange(parts.reshape(ctx_count, draft, -1), "ctx")
-    attended = merge_parts(parts, own, own_level, heads)
-
-    attended_rows = spread_to_all(attended, "req").reshape(rows, width)
-    projected = jnp.einsum(
-        "mk,ckn->cmn", attended_rows, out_all, preferred_element_type=F32
+    parts = prompt_part(gathered.reshape(ctx_count * draft, width), prefix_kv, slopes, offset)
+    parts, embedded = lax.optimization_barrier((parts, embedded))
+    embedded = embedded.transpose(1, 0, 2).reshape(ctx_count * draft, req_count * columns)
+    parts = exchange(parts.reshape(ctx_count, draft, -1), ctx)
+    attended = exchange(merge_parts(parts, own, own_level, heads, ctx_count), ctx)
+
+    projected = lax.dot_general(
+        attended.reshape(ctx_count * draft, width),
+        out_all,
+        (((1,), (1,)), ((), ())),
+        preferred_element_type=F32,
     ) + embedded.astype(F32)
-    pair = ctx_count // mp_count
-    message = (
-        projected.astype(BF16)
-        .reshape(mp_count, pair, req_count, draft, columns)
-        .transpose(2, 0, 1, 3, 4)
-        .reshape(req_count * mp_count, pair, draft, columns)
-    )
-    message = exchange(message, ("req", "mp"))
-    residual, sums = residual_rows(message.reshape(req_count, mp_count, pair, draft, columns))
-    normed = norm_rows(residual, spread_to_all(sums, "mp"), ln_gain, quarter * mp_count)
-
-    normed_rows = spread_to_all(normed, "req").reshape(rows, quarter)
-    lifted = jnp.einsum("mk,ckn->cmn", normed_rows, up_all, preferred_element_type=F32)
-    share = rows // mp_count
+    projected = exchange(projected.astype(BF16).reshape(ctx_count, draft, -1), ctx)
+    up_other = shifted_by(after(up_own, projected), "core", 1)
+    pieces = exchange(projected.reshape(mp_count, ctx_count // mp_count, draft, -1), "mp")
+    residual, sums = residual_rows(pieces)
+    sums = [sums] + [shifted_by(sums, "mp", step) for step in range(1, mp_count)]
+    normed = norm_rows(residual, sums, ln_gain, quarter * mp_count, req_count)
+    down_other = shifted_by(after(down_own, normed), "core", 1)
+    normed = exchange(normed, "req")
+
     lifted = exchange(
-        lifted.astype(BF16)
-        .reshape(ctx_count, mp_count, share, hidden)
-        .transpose(1, 0, 2, 3),
-        "mp",
-    )
-    activated = jax.nn.gelu(jnp.sum(lifted.astype(F32), axis=0), approximate=False).astype(BF16)
-    activated = (
-        spread_to_all(activated, "mp").transpose(1, 0, 2, 3).reshape(ctx_count, rows, hidden)
-    )
-    lowered = jnp.einsum("cmh,chn->mn", activated, down_all, preferred_element_type=F32)
-    lowered = exchange(lowered.astype(BF16).reshape(req_count, draft, quarter), "req")
-    layer_out = residual + jnp.sum(lowered.astype(F32), axis=0)
+        lift_rows(normed.reshape(req_count * draft, quarter), up_own, up_other, mp_count), "mp"
+    )
+    activated = exchange(activate(lifted), "mp")
+    lowered = exchange(lower_rows(activated, down_own, down_other, req_count), "req")
+    layer_out = finish(lowered, residual)
     return residual[None], layer_out[None]
 
 
 def solution(mesh):
+    chips = jax.sharding.Mesh(
+        mesh.devices.reshape((mesh.shape["ctx"] // 2, 2) + mesh.devices.shape[1:]),
+        ("y", "core", "req", "mp"),
+    )
+    rows = ("y", "core", "req")
     in_specs = (
         P(),
-        P("mp", ("ctx", "req")),
-        P(("ctx", "req"), None, "mp"),
-        P(None, ("ctx", "req"), None, "mp"),
-        P(None, "ctx", "mp"),
-        P(None, ("ctx", "req"), None, "mp"),
-        P(("ctx", "req")),
+        P("mp", rows),
+        P(rows, None, "mp"),
+        P(None, rows, None, "mp"),
+        P(None, ("y", "core"), "mp"),
+        P(None, rows, None, "mp"),
+        P(rows),
         P("mp"),
-        P("mp", ("ctx", "req")),
+        P("mp", rows),
         P("mp"),
-        P("mp", ("ctx", "req")),
-        P(("ctx", "req"), "mp"),
-    )
-    out_specs = (P(("ctx", "req"), None, "mp"), P(("ctx", "req"), None, "mp"))
+        P("mp", rows),
+        P(rows, "mp"),
+    )
+    out_specs = (P(rows, None, "mp"), P(rows, None, "mp"))
     return jax.shard_map(
-        per_device, mesh=mesh, in_specs=in_specs, out_specs=out_specs, check_vma=False
-    )
+        per_device, mesh=chips, in_specs=in_specs, out_specs=out_specs, check_vma=False
+    )

time: 193 us -> 239 us (1.24)
  blocking collectives: 54.4 us -> 90.2 us
  waiting for transfers between devices: 34.1 us -> 57 us
  Pallas kernels: 18.5 us -> 35.4 us
  local copies, waits for them, and re-layouts: 22 us -> 6.62 us
  matrix products: 16.1 us -> 7.97 us
  starting transfers between devices: 29.6 us -> 25.5 us
  other arithmetic: 2.45 us -> 0.04 us
    all_to_all x4 -> x6, blocking collectives: 54.4 us -> 90.2 us  [exchange(): return lax.all_to_all(value, axis, split_axis=0, concat_axis=0, tiled=True)]
    all_gather x3, waiting for transfers between devices: 0.04 us -> 35.8 us  [the longest x1 22.3 us: per_device(): down_own = lax.all_gather(after(down_weight, copies), 'y')]
    pallas_call x1 -> x5, Pallas kernels: 1.73 us -> 18.1 us  [the longest x1 7.67 us: lift_rows(): pl.pallas_call(lift_kernel, out_shape=jax.ShapeDtypeStruct((shares, 2 * b...]
    all_to_all x6 -> x4, waiting for transfers between devices: 32 us -> 17.1 us  [exchange(): return lax.all_to_all(value, axis, split_axis=0, concat_axis=0, tiled=True)]
    all_to_all x6 -> x4, starting transfers between devices: 29.5 us -> 21.2 us  [exchange(): return lax.all_to_all(value, axis, split_axis=0, concat_axis=0, tiled=True)]
    all_gather x2 -> x0, local copies, waits for them, and re-layouts: 7.57 us -> none  [the longest x1 5.99 us: per_device(): up_all = lax.all_gather(up_weight, 'ctx')]
    unnamed x2 -> x0, matrix products: 6.21 us -> none
    broadcast_in_dim x5 -> x1, local copies, waits for them, and re-layouts: 5.93 us -> 1.49 us  [per_device(): copies = jnp.broadcast_to(queries, (ctx_count, draft, width))]
  transfers between devices with their start and end apart: 9 -> 12, of which waited for: 6 -> 7; matrix products, arithmetic and copies ran while one was open for 15% -> 5% of each run, Pallas kernels for 10% -> 12%
where the time goes in v2:
time: 239 us; the launch traced here: 237 us
  blocking collectives  90.2 us (38%)
  waiting for transfers between devices  57 us (24%)
  Pallas kernels  35.4 us (15%)
  starting transfers between devices  25.5 us (11%)
  between operations  14.6 us (6%)
  matrix products  7.97 us (3%)
  local copies, waits for them, and re-layouts  6.62 us (3%)
    all_to_all x6, blocking collectives, exchange(): return lax.all_to_all(value, axis, split_axis=0, concat_axis=0, tiled=True)  90.2 us
    all_gather x1, waiting for transfers between devices, per_device(): down_own = lax.all_gather(after(down_weight, copies), 'y')  22.3 us
    all_to_all x4, starting transfers between devices, exchange(): return lax.all_to_all(value, axis, split_axis=0, concat_axis=0, tiled=True)  21.2 us
    all_to_all x4, waiting for transfers between devices, exchange(): return lax.all_to_all(value, axis, split_axis=0, concat_axis=0, tiled=True)  17.1 us
    all_gather x1, waiting for transfers between devices, per_device(): up_own = lax.all_gather(after(up_weight, copies).T, 'y')  13.5 us
    pallas_call x1, Pallas kernels, prompt_part(): pl.pallas_call(functools.partial(prompt_kernel, heads=heads, head_size=wi...  11.7 us
    pallas_call x1, Pallas kernels, lift_rows(): pl.pallas_call(lift_kernel, out_shape=jax.ShapeDtypeStruct((shares, 2 * b...  7.67 us
    dot_general x1, matrix products, per_device(): jnp.dot(one_hot, embed_table, preferred_element_type=F32).astype(BF16)  5.96 us
  transfers between devices with their start and end apart: 12, of which 7 were waited for; matrix products, arithmetic and copies ran while one was open for 5% of the time, Pallas kernels for 12%

profile of v2, /device:TPU:2, one launch (start us, length us, event | category | flops | bytes accessed | tf_op | source)
XLA Modules:
  0.0 237.3 jit_solution(5439148936555673745)
XLA Ops:
  7.2 0.0 all-gather.6.cloned.1.call-start
  7.2 0.7 all-gather.6.cloned.1.call-update
  7.9 0.0 all-gather.8.cloned.1.call-start
  8.0 1.5 broadcast_in_dim.19
  9.4 0.0 all-gather.8.cloned.1.call-update
  9.5 0.0 all-gather.10.cloned.1.call-start
  9.5 0.7 all-gather.10.cloned.1.call-update
  10.2 4.5 %all-to-all-start = ((bf16[8,16,896]{2,1,0:T(8,128)(2,1)}), bf16[8,16,896]{2,1,0:T(8,128)(2,1)S(1)}, u32[]{:S(2)}, u32[]{:S(2)}) async-start(bf16[8,16,896]{2,1,0:T(8,128)(2,1)} %broadcast_in_dim.19), calls=%async_computation | async-start | bytes 458752 | tf_op jit(solution)/shard_map/all_to_all | solution.py:424
  14.7 0.8 copy.15
  15.5 0.1 sub.27
  15.6 6.0 %fusion.2 = bf16[1024,112]{0,1:T(8,128)(2,1)S(1)} fusion(bf16[6400,112]{0,1:T(8,128)(2,1)S(1)} %copy-done, s32[1024]{0:T(1024)S(1)} %sub.27), kind=kOutput, calls=%fused_computation.4 | convolution fusion | flops 1474674688 | bytes 1667072 | tf_op jit(solution)/shard_map/dot_general | solution.py:467
  22.3 1.6 shard_map.131
  23.9 0.6 copy-done.3
  24.5 0.6 copy-done.5
  25.1 0.8 copy_bitcast_fusion
  26.0 8.5 %all-to-all-start.1 = ((bf16[8,128,112]{1,2,0:T(8,128)(2,1)}), bf16[8,128,112]{1,2,0:T(8,128)(2,1)S(1)}, u32[]{:S(2)}, u32[]{:S(2)}) async-start(bf16[8,128,112]{1,2,0:T(8,128)(2,1)} %copy_bitcast_fusion), calls=%async_computation.1 | async-start | bytes 458752 | tf_op jit(solution)/shard_map/all_to_all | solution.py:424
  34.4 11.7 %shard_map.132 = bf16[128,1024]{1,0:T(8,128)(2,1)} custom-call(s32[1]{0:T(128)} %bitcast.offset_ref, f32[8]{0:T(128)} %slopes_ref.3, bf16[128,896]{1,0:T(8,128)(2,1)} %bitcast.45, bf16[2,2048,896]{2,1,0:T(8,128)(2,1)} %prefix_ref.1), custom_call_target="tpu_custom_call" | custom-call | tf_op jit(solution)/shard_map/pallas_call | solution.py:119
  46.1 2.3 all-to-all-done.1
  48.4 12.4 %all_to_all.50.parts_ref = bf16[8,16,1024]{2,1,0:T(8,128)(2,1)} all-to-all(bf16[8,16,1024]{2,1,0:T(8,128)(2,1)} %bitcast.41), channel_id=1, replica_groups=mesh['y'=4,'core'=2,'req'=8,'mp'=4] {'y','core'}, dimensions={0} | all-to-all | bytes 524288 | tf_op jit(solution)/shard_map/all_to_all | solution.py:424
  60.9 2.1 shard_map.133
  62.9 3.4 %all-to-all-start.3 = ((bf16[8,16,896]{2,1,0:T(8,128)(2,1)}), bf16[8,16,896]{2,1,0:T(8,128)(2,1)S(1)}, u32[]{:S(2)}, u32[]{:S(2)}) async-start(bf16[8,16,896]{2,1,0:T(8,128)(2,1)} %shard_map.133), calls=%async_computation.3 | async-start | bytes 458752 | tf_op jit(solution)/shard_map/all_to_all | solution.py:424
  66.4 0.2 copy.18
  66.6 7.6 %all-to-all-done.3 = bf16[8,16,896]{2,1,0:T(8,128)(2,1)S(1)} async-done(((bf16[8,16,896]{2,1,0:T(8,128)(2,1)}), bf16[8,16,896]{2,1,0:T(8,128)(2,1)S(1)}, u32[]{:S(2)}, u32[]{:S(2)}) %all-to-all-start.3) | async-done | bytes 229408 | tf_op jit(solution)/shard_map/all_to_all | solution.py:424
  74.2 2.0 fusion.3
  76.2 12.4 %all_to_all.51 = bf16[8,16,896]{2,1,0:T(8,128)(2,1)S(1)} all-to-all(bf16[8,16,896]{2,1,0:T(8,128)(2,1)S(1)} %bitcast.43), channel_id=1, replica_groups=mesh['y'=4,'core'=2,'req'=8,'mp'=4] {'y','core'}, dimensions={0} | all-to-all | bytes 458752 | tf_op jit(solution)/shard_map/all_to_all | solution.py:424
  88.6 13.5 %all-gather.8.cloned.1.call-done = bf16[896,1792]{1,0:T(8,128)(2,1)} async-done(((bf16[224,1792]{1,0:T(8,128)(2,1)}), bf16[896,1792]{1,0:T(8,128)(2,1)}) %all-gather.8.cloned.1.call-update) | async-done | bytes 3211280 | tf_op jit(solution)/shard_map/all_gather | solution.py:456
  102.1 0.1 collective-permute-start.3
  102.2 10.1 %all_to_all.52.parts_ref = bf16[4,2,16,896]{3,2,1,0:T(8,128)(2,1)} all-to-all(bf16[4,2,16,896]{3,2,1,0:T(8,128)(2,1)S(1)} %bitcast.44), channel_id=1, replica_groups=mesh['y'=4,'core'=2,'req'=8,'mp'=4] {'mp'}, dimensions={0} | all-to-all | bytes 458752 | tf_op jit(solution)/shard_map/all_to_all | solution.py:424
  112.3 1.7 shard_map.134
  114.0 0.3 collective-permute-start
  114.3 3.2 %collective-permute-start.1 = (f32[16,128]{1,0:T(8,128)}, f32[16,128]{1,0:T(8,128)S(1)}, u32[]{:S(2)}, u32[]{:S(2)}) collective-permute-start(f32[16,128]{1,0:T(8,128)} %get-tuple-element.23.rest_0_), channel_id=1, source_target_pairs={{0,2},{1,3},{2,0},{3,1},{4,6},{5,7},{6,4},{7,5},{8,10},{9,11},{10,... | collective-permute-start | bytes 24584 | tf_op jit(solution)/shard_map/ppermute | solution.py:420
  117.5 0.6 collective-permute-start.2
  118.1 0.6 broadcast_in_dim.21.gain_ref
  118.7 1.0 collective-permute-done.1.rest_2_
  119.6 1.7 collective-permute-done.2.rest_3_
  121.4 0.6 copy-done.11
  122.0 1.9 shard_map.135
  123.9 22.3 %all-gather.10.cloned.1.call-done = bf16[896,1792]{1,0:T(8,128)(2,1)} async-done(((bf16[224,1792]{1,0:T(8,128)(2,1)}), bf16[896,1792]{1,0:T(8,128)(2,1)}) %all-gather.10.cloned.1.call-update) | async-done | bytes 3211280 | tf_op jit(solution)/shard_map/all_gather | solution.py:457
  146.1 23.9 %all_to_all.53 = bf16[8,16,1792]{2,1,0:T(8,128)(2,1)} all-to-all(bf16[8,16,1792]{2,1,0:T(8,128)(2,1)} %shard_map.135), channel_id=1, replica_groups=mesh['y'=4,'core'=2,'req'=8,'mp'=4] {'req'}, dimensions={0} | all-to-all | bytes 917504 | tf_op jit(solution)/shard_map/all_to_all | solution.py:424
  170.0 7.7 %shard_map.136 = bf16[4,8,32,224]{3,2,1,0:T(8,128)(2,1)} custom-call(bf16[128,1792]{1,0:T(8,128)(2,1)} %bitcast.39, bf16[4,224,1792]{2,1,0:T(8,128)(2,1)} %bitcast.38, bf16[4,224,1792]{2,1,0:T(8,128)(2,1)} %collective-permute-done.3.other_ref), custom_call_target="tpu_custom_call" | custom-call | tf_op jit(solution)/shard_map/pallas_call | solution.py:335
  177.7 13.3 %all_to_all.54.parts_ref = bf16[4,8,32,224]{3,2,1,0:T(8,128)(2,1)} all-to-all(bf16[4,8,32,224]{3,2,1,0:T(8,128)(2,1)} %shard_map.136), channel_id=1, replica_groups=mesh['y'=4,'core'=2,'req'=8,'mp'=4] {'mp'}, dimensions={0} | all-to-all | bytes 917504 | tf_op jit(solution)/shard_map/all_to_all | solution.py:424
  191.0 2.0 shard_map.137
  192.9 4.9 %all-to-all-start.8 = ((bf16[4,8,32,224]{3,2,1,0:T(8,128)(2,1)}), bf16[4,8,32,224]{3,2,1,0:T(8,128)(2,1)S(1)}, u32[]{:S(2)}, u32[]{:S(2)}) async-start(bf16[4,8,32,224]{3,2,1,0:T(8,128)(2,1)} %shard_map.137), calls=%async_computation.8 | async-start | bytes 1048576 | tf_op jit(solution)/shard_map/all_to_all | solution.py:424
  197.8 7.2 %all-to-all-done.8.hidden_ref = bf16[4,8,32,224]{3,2,1,0:T(8,128)(2,1)S(1)} async-done(((bf16[4,8,32,224]{3,2,1,0:T(8,128)(2,1)}), bf16[4,8,32,224]{3,2,1,0:T(8,128)(2,1)S(1)}, u32[]{:S(2)}, u32[]{:S(2)}) %all-to-all-start.8) | async-done | bytes 458784 | tf_op jit(solution)/shard_map/all_to_all | solution.py:424
  205.0 0.8 copy-done.7
  205.8 5.0 %shard_map.138 = bf16[8,16,1792]{2,1,0:T(8,128)(2,1)} custom-call(bf16[4,8,32,224]{3,2,1,0:T(8,128)(2,1)} %copy-done.7, bf16[4,224,1792]{2,1,0:T(8,128)(2,1)} %bitcast.36, bf16[4,224,1792]{2,1,0:T(8,128)(2,1)} %collective-permute-done.4.other_ref), custom_call_target="tpu_custom_call" | custom-call | tf_op jit(solution)/shard_map/pallas_call | solution.py:384
  210.8 18.2 %all_to_all.55.parts_ref = bf16[8,16,1792]{2,1,0:T(8,128)(2,1)} all-to-all(bf16[8,16,1792]{2,1,0:T(8,128)(2,1)} %shard_map.138), channel_id=1, replica_groups=mesh['y'=4,'core'=2,'req'=8,'mp'=4] {'req'}, dimensions={0} | all-to-all | bytes 917504 | tf_op jit(solution)/shard_map/all_to_all | solution.py:424
  229.0 1.7 shard_map.139
  (31 shorter events, 0.1 us)
Async XLA Ops:
  7.2 8.4 %copy-start = (bf16[6400,112]{0,1:T(8,128)(2,1)S(1)}, bf16[6400,112]{0,1:T(8,128)(2,1)}, u32[]{:S(2)}) copy-start(bf16[6400,112]{0,1:T(8,128)(2,1)} %param.13) | copy-start | bytes 4300804
  7.2 67.0 %all-gather.6.cloned.1.call-start = ((), (), s32[]{:S(2)}) async-start(), calls=%async_computation.10 | async-start | bytes 1806336 | tf_op jit(solution)/shard_map/all_gather | solution.py:455
  7.9 94.2 %all-gather.8.cloned.1.call-start = ((), (), s32[]{:S(2)}) async-start(), calls=%async_computation.11 | async-start | bytes 4014080 | tf_op jit(solution)/shard_map/all_gather | solution.py:456
  9.5 136.7 %all-gather.10.cloned.1.call-start = ((), (), s32[]{:S(2)}) async-start(), calls=%async_computation.12 | async-start | bytes 4014080 | tf_op jit(solution)/shard_map/all_gather | solution.py:457
  10.2 14.9 %all-to-all-start = ((bf16[8,16,896]{2,1,0:T(8,128)(2,1)}), bf16[8,16,896]{2,1,0:T(8,128)(2,1)S(1)}, u32[]{:S(2)}, u32[]{:S(2)}) async-start(bf16[8,16,896]{2,1,0:T(8,128)(2,1)} %broadcast_in_dim.19), calls=%async_computation | async-start | bytes 458752 | tf_op jit(solution)/shard_map/all_to_all | solution.py:424
  15.6 6.7 %copy-start.1 = (bf16[2,1,512,896]{3,2,1,0:T(8,128)(2,1)S(1)}, bf16[2,1,512,896]{3,2,1,0:T(8,128)(2,1)}, u32[]{:S(2)}) copy-start(bf16[2,1,512,896]{3,2,1,0:T(8,128)(2,1)} %param.17) | copy-start | bytes 5505028
  15.6 6.7 %copy-start.2 = (bf16[1,16,896]{2,1,0:T(8,128)(2,1)S(1)}, bf16[1,16,896]{2,1,0:T(8,128)(2,1)}, u32[]{:S(2)}) copy-start(bf16[1,16,896]{2,1,0:T(8,128)(2,1)} %param.14) | copy-start | bytes 86020
  15.6 6.7 %copy-start.4 = (bf16[2,1,16,896]{3,2,1,0:T(8,128)(2,1)S(1)}, bf16[2,1,16,896]{3,2,1,0:T(8,128)(2,1)}, u32[]{:S(2)}) copy-start(bf16[2,1,16,896]{3,2,1,0:T(8,128)(2,1)} %param.15) | copy-start | bytes 172036
  15.6 6.7 %copy-start.6 = (f32[8]{0:T(128)S(1)}, f32[8]{0:T(128)}, u32[]{:S(2)}) copy-start(f32[8]{0:T(128)} %slopes_ref.3) | copy-start | bytes 100
  23.9 0.6 copy-start.3
  24.5 0.6 copy-start.5
  25.1 9.3 %copy-start.8 = (bf16[8,16,896]{2,1,0:T(8,128)(2,1)}, bf16[8,16,896]{2,1,0:T(8,128)(2,1)S(1)}, u32[]{:S(2)}) copy-start(bf16[8,16,896]{2,1,0:T(8,128)(2,1)S(1)} %all-to-all-done) | copy-start | bytes 688132
  26.0 22.5 %all-to-all-start.1 = ((bf16[8,128,112]{1,2,0:T(8,128)(2,1)}), bf16[8,128,112]{1,2,0:T(8,128)(2,1)S(1)}, u32[]{:S(2)}, u32[]{:S(2)}) async-start(bf16[8,128,112]{1,2,0:T(8,128)(2,1)} %copy_bitcast_fusion), calls=%async_computation.1 | async-start | bytes 458752 | tf_op jit(solution)/shard_map/all_to_all | solution.py:424
  60.8 57.2 %copy-start.12 = (f32[1792]{0:T(1024)S(1)}, f32[1792]{0:T(1024)}, u32[]{:S(2)}) copy-start(f32[1792]{0:T(1024)} %param.21) | copy-start | bytes 21508
  62.9 11.3 %all-to-all-start.3 = ((bf16[8,16,896]{2,1,0:T(8,128)(2,1)}), bf16[8,16,896]{2,1,0:T(8,128)(2,1)S(1)}, u32[]{:S(2)}, u32[]{:S(2)}) async-start(bf16[8,16,896]{2,1,0:T(8,128)(2,1)} %shard_map.133), calls=%async_computation.3 | async-start | bytes 458752 | tf_op jit(solution)/shard_map/all_to_all | solution.py:424
  102.1 67.9 %collective-permute-start.3 = (bf16[4,224,1792]{2,1,0:T(8,128)(2,1)}, bf16[4,224,1792]{2,1,0:T(8,128)(2,1)}, u32[]{:S(2)}, u32[]{:S(2)}) collective-permute-start(bf16[4,224,1792]{2,1,0:T(8,128)(2,1)} %bitcast.37), channel_id=1, source_target_pairs={{0,32},{32,0},{1,33},{33,1},{2,34},{34,2},{3,35},{35,3},{4,36},{36... | collective-permute-start | bytes 9633800 | tf_op jit(solution)/shard_map/ppermute | solution.py:420
  114.0 4.7 %collective-permute-start = (f32[16,128]{1,0:T(8,128)}, f32[16,128]{1,0:T(8,128)S(1)}, u32[]{:S(2)}, u32[]{:S(2)}) collective-permute-start(f32[16,128]{1,0:T(8,128)} %get-tuple-element.23.rest_0_), channel_id=1, source_target_pairs={{0,1},{1,2},{2,3},{3,0},{4,5},{5,6},{6,7},{7,4},{8,9},{9,10},{10,1... | collective-permute-start | bytes 24584 | tf_op jit(solution)/shard_map/ppermute | solution.py:420
  114.3 5.4 %collective-permute-start.1 = (f32[16,128]{1,0:T(8,128)}, f32[16,128]{1,0:T(8,128)S(1)}, u32[]{:S(2)}, u32[]{:S(2)}) collective-permute-start(f32[16,128]{1,0:T(8,128)} %get-tuple-element.23.rest_0_), channel_id=1, source_target_pairs={{0,2},{1,3},{2,0},{3,1},{4,6},{5,7},{6,4},{7,5},{8,10},{9,11},{10,... | collective-permute-start | bytes 24584 | tf_op jit(solution)/shard_map/ppermute | solution.py:420
  117.5 3.9 %collective-permute-start.2 = (f32[16,128]{1,0:T(8,128)}, f32[16,128]{1,0:T(8,128)S(1)}, u32[]{:S(2)}, u32[]{:S(2)}) collective-permute-start(f32[16,128]{1,0:T(8,128)} %get-tuple-element.23.rest_0_), channel_id=1, source_target_pairs={{0,3},{1,0},{2,1},{3,2},{4,7},{5,4},{6,5},{7,6},{8,11},{9,8},{10,9... | collective-permute-start | bytes 24584 | tf_op jit(solution)/shard_map/ppermute | solution.py:420
  118.7 2.7 %copy-start.9 = (f32[16,128]{1,0:T(8,128)}, f32[16,128]{1,0:T(8,128)S(1)}, u32[]{:S(2)}) copy-start(f32[16,128]{1,0:T(8,128)S(1)} %collective-permute-done.rest_1_) | copy-start | bytes 24580
  119.6 1.7 copy-start.10
  121.4 0.6 copy-start.11
  146.1 51.7 %collective-permute-start.4 = (bf16[4,224,1792]{2,1,0:T(8,128)(2,1)}, bf16[4,224,1792]{2,1,0:T(8,128)(2,1)}, u32[]{:S(2)}, u32[]{:S(2)}) collective-permute-start(bf16[4,224,1792]{2,1,0:T(8,128)(2,1)} %bitcast.35), channel_id=1, source_target_pairs={{0,32},{32,0},{1,33},{33,1},{2,34},{34,2},{3,35},{35,3},{4,36},{36... | collective-permute-start | bytes 9633800 | tf_op jit(solution)/shard_map/ppermute | solution.py:420
  192.9 12.1 %all-to-all-start.8 = ((bf16[4,8,32,224]{3,2,1,0:T(8,128)(2,1)}), bf16[4,8,32,224]{3,2,1,0:T(8,128)(2,1)S(1)}, u32[]{:S(2)}, u32[]{:S(2)}) async-start(bf16[4,8,32,224]{3,2,1,0:T(8,128)(2,1)} %shard_map.137), calls=%async_computation.8 | async-start | bytes 1048576 | tf_op jit(solution)/shard_map/all_to_all | solution.py:424
  205.0 0.8 copy-start.7
Sparse Core Ops, SparseCore 0:
  9.8 45.9 all-gather.5
  57.6 44.4 all-gather.7
  103.9 42.1 all-gather.9

commit v3 on v2

--- a/solution.py
+++ b/solution.py
@@ -11,7 +11,7 @@
 LANES = 128
 F32 = jnp.float32
 BF16 = jnp.bfloat16
-WHOLE_VMEM = 60 * 1024 * 1024
+WHOLE_VMEM = 58 * 1024 * 1024
 
 
 def head_lanes(head, tile, head_size):
@@ -38,7 +38,7 @@
 
 
 def prompt_kernel(
-    offset_ref, slopes_ref, query_ref, prefix_ref, out_ref, kv_buf, sems, *, heads, head_size
+    offset_ref, slopes_ref, query_ref, looked_ref, prefix_ref, out_ref, kv_buf, sems, *, heads, head_size
 ):
     rows, width = query_ref.shape
     keys = kv_buf.shape[2]
@@ -101,27 +101,39 @@
                 parts[tile],
             )
         stats = jnp.where(stat_lane % heads == head, top + jnp.log(total), stats)
-    for tile in range(tiles):
-        out_ref[:, tile * LANES : (tile + 1) * LANES] = parts[tile].astype(BF16)
     high, middle, low = split_three(stats)
     group = stat_lane // heads
     packed = jnp.where(
         group == 0, high, jnp.where(group == 1, middle, jnp.where(group == 2, low, 0.0))
     )
-    out_ref[:, tiles * LANES :] = packed.astype(BF16)
-
-
-def prompt_part(query_rows, prefix_kv, slopes, offset):
+    targets = out_ref.shape[0]
+    draft = rows // targets
+    for tile, value in enumerate([*parts, packed]):
+        value = value.astype(BF16)
+        for target in range(targets):
+            out_ref[target, tile * draft : (tile + 1) * draft] = value[
+                target * draft : (target + 1) * draft
+            ]
+    for target in range(targets):
+        out_ref[target, (tiles + 1) * draft :] = looked_ref[
+            :, target * LANES : (target + 1) * LANES
+        ]
+
+
+def prompt_part(query_rows, prefix_kv, slopes, offset, looked_up, targets):
     rows, width = query_rows.shape
     heads = slopes.shape[0]
     keys = prefix_kv.shape[1]
     tiles = width // LANES
     return pl.pallas_call(
         functools.partial(prompt_kernel, heads=heads, head_size=width // heads),
-        out_shape=jax.ShapeDtypeStruct((rows, width + LANES), BF16),
+        out_shape=jax.ShapeDtypeStruct(
+            (targets, (tiles + 1) * (rows // targets) + looked_up.shape[0], LANES), BF16
+        ),
         in_specs=[
             pl.BlockSpec(memory_space=pltpu.SMEM),
             pl.BlockSpec(memory_space=pltpu.SMEM),
+            pl.BlockSpec(memory_space=pltpu.VMEM),
             pl.BlockSpec(memory_space=pltpu.VMEM),
             pl.BlockSpec(memory_space=pltpu.HBM),
         ],
@@ -131,7 +143,7 @@
             pltpu.SemaphoreType.DMA((2, tiles)),
         ],
         compiler_params=pltpu.CompilerParams(vmem_limit_bytes=WHOLE_VMEM),
-    )(offset, slopes, query_rows, prefix_kv)
+    )(offset, slopes, query_rows, looked_up, prefix_kv)
 
 
 def own_kernel(
@@ -205,12 +217,12 @@
 
 
 def merge_kernel(parts_ref, own_ref, level_ref, out_ref, *, heads, head_size):
-    count, draft, _ = parts_ref.shape
-    width = own_ref.shape[1]
+    count = parts_ref.shape[0]
+    draft, width = own_ref.shape
     tiles = width // LANES
     levels = [level_ref[...]]
     for part in range(count):
-        packed = parts_ref[part, :, width:].astype(F32)
+        packed = parts_ref[part, tiles * draft : (tiles + 1) * draft].astype(F32)
         levels.append(
             packed
             + pltpu.roll(packed, LANES - heads, 1)
@@ -231,7 +243,10 @@
                     factor = jnp.where(
                         lane_mask((draft, LANES), first, last), share[:, head : head + 1], factor
                     )
-            value = own_ref[:, lanes] if part == 0 else parts_ref[part - 1, :, lanes].astype(F32)
+            if part == 0:
+                value = own_ref[:, lanes]
+            else:
+                value = parts_ref[part - 1, tile * draft : (tile + 1) * draft].astype(F32)
             joined += factor * value
         joined = joined.astype(BF16)
         for target in range(out_ref.shape[0]):
@@ -249,28 +264,64 @@
     )(parts, own, level)
 
 
-def residual_kernel(parts_ref, out_ref, sums_ref):
-    mp, pair, draft, columns = parts_ref.shape
+def project_kernel(rows_ref, weight_ref, parts_ref, out_ref):
+    blocks, columns, _ = weight_ref.shape
+    targets, held, _ = out_ref.shape
+    req, draft, width = rows_ref.shape
+    mp = targets // req
+    pair = held // draft
+    rows = rows_ref[...].reshape(req * draft, width)
+    for block in range(blocks):
+        product = lax.dot_general(
+            rows, weight_ref[block], (((1,), (1,)), ((), ())), preferred_element_type=F32
+        )
+        looked_up = parts_ref[block, parts_ref.shape[1] - columns :].astype(F32)
+        product = (product + jnp.transpose(looked_up)).astype(BF16)
+        piece, half = divmod(block, pair)
+        for target in range(req):
+            out_ref[target * mp + piece, half * draft : (half + 1) * draft] = product[
+                target * draft : (target + 1) * draft
+            ]
+
+
+def project_rows(rows, weight, parts, mp):
+    req, draft, _ = rows.shape
+    blocks, columns, _ = weight.shape
+    vmem = pl.BlockSpec(memory_space=pltpu.VMEM)
+    return pl.pallas_call(
+        project_kernel,
+        out_shape=jax.ShapeDtypeStruct((req * mp, blocks // mp * draft, columns), BF16),
+        in_specs=[vmem, vmem, vmem],
+        out_specs=vmem,
+    )(rows, weight, parts)
+
+
+def residual_kernel(parts_ref, out_ref, sums_ref, *, mp):
+    sources, held, columns = parts_ref.shape
+    draft = out_ref.shape[0]
     blocks = []
-    for half in range(pair):
-        block = parts_ref[0, half].astype(F32)
-        for piece in range(1, mp):
-            block += parts_ref[piece, half].astype(F32)
-        blocks.append(block)
-        out_ref[:, half * columns : (half + 1) * columns] = block
+    for half in range(held // draft):
+        lines = slice(half * draft, (half + 1) * draft)
+        for source in range(sources // mp):
+            block = parts_ref[source * mp, lines].astype(F32)
+            for piece in range(1, mp):
+                block += parts_ref[source * mp + piece, lines].astype(F32)
+            blocks.append(block)
+    residual = jnp.concatenate(blocks, axis=1)
+    out_ref[...] = residual
     lane = lax.broadcasted_iota(jnp.int32, (draft, LANES), 1)
-    first = sum(jnp.sum(block, axis=1, keepdims=True) for block in blocks)
-    second = sum(jnp.sum(block * block, axis=1, keepdims=True) for block in blocks)
+    first = jnp.sum(residual, axis=1, keepdims=True)
+    second = jnp.sum(residual * residual, axis=1, keepdims=True)
     sums_ref[...] = jnp.where(lane == 0, first, jnp.where(lane == 1, second, 0.0))
 
 
-def residual_rows(parts):
-    mp, pair, draft, columns = parts.shape
-    vmem = pl.BlockSpec(memory_space=pltpu.VMEM)
-    return pl.pallas_call(
-        residual_kernel,
+def residual_rows(parts, mp, draft):
+    sources, held, columns = parts.shape
+    vmem = pl.BlockSpec(memory_space=pltpu.VMEM)
+    return pl.pallas_call(
+        functools.partial(residual_kernel, mp=mp),
         out_shape=(
-            jax.ShapeDtypeStruct((draft, pair * columns), F32),
+            jax.ShapeDtypeStruct((draft, sources // mp * held // draft * columns), F32),
             jax.ShapeDtypeStruct((draft, LANES), F32),
         ),
         in_specs=[vmem],
@@ -299,12 +350,10 @@
     )(residual, gain[None, :], *sums)
 
 
-def arriving(refs, buf, sems):
-    blocks = refs[0].shape[0]
+def arriving(ref, buf, sems):
     copies = [
-        pltpu.make_async_copy(ref.at[block], buf.at[place * blocks + block], sems.at[place * blocks + block])
-        for place, ref in enumerate(refs)
-        for block in range(blocks)
+        pltpu.make_async_copy(ref.at[block], buf.at[block], sems.at[block])
+        for block in range(ref.shape[0])
     ]
     for copy in copies:
         copy.start()
@@ -316,33 +365,29 @@
     return block_at
 
 
-def lift_kernel(rows_ref, own_ref, other_ref, out_ref, buf, sems):
-    block_at = arriving((own_ref, other_ref), buf, sems)
+def lift_kernel(rows_ref, weight_ref, out_ref, buf, sems):
+    block_at = arriving(weight_ref, buf, sems)
     rows = rows_ref[...]
-    shares, blocks, share, _ = out_ref.shape
-    for block in range(blocks):
-        lifted = lax.dot_general(
-            rows, block_at(block), (((1,), (1,)), ((), ())), preferred_element_type=F32
+    pair = out_ref.shape[1]
+    for block in range(weight_ref.shape[0]):
+        out_ref[block // pair, block % pair] = lax.dot_general(
+            block_at(block), rows, (((1,), (1,)), ((), ())), preferred_element_type=F32
         ).astype(BF16)
-        for piece in range(shares):
-            out_ref[piece, block] = lifted[piece * share : (piece + 1) * share]
-
-
-def lift_rows(rows, own, other, shares):
-    vmem = pl.BlockSpec(memory_space=pltpu.VMEM)
-    hbm = pl.BlockSpec(memory_space=pltpu.HBM)
-    blocks, hidden, width = own.shape
+
+
+def lift_rows(rows, weight, mp):
+    blocks, hidden, width = weight.shape
     return pl.pallas_call(
         lift_kernel,
-        out_shape=jax.ShapeDtypeStruct((shares, 2 * blocks, rows.shape[0] // shares, hidden), BF16),
-        in_specs=[vmem, hbm, hbm],
-        out_specs=vmem,
+        out_shape=jax.ShapeDtypeStruct((mp, blocks // mp, hidden, rows.shape[0]), BF16),
+        in_specs=[pl.BlockSpec(memory_space=pltpu.VMEM), pl.BlockSpec(memory_space=pltpu.HBM)],
+        out_specs=pl.BlockSpec(memory_space=pltpu.VMEM),
         scratch_shapes=[
-            pltpu.VMEM((2 * blocks, hidden, width), BF16),
-            pltpu.SemaphoreType.DMA((2 * blocks,)),
+            pltpu.VMEM((blocks, hidden, width), BF16),
+            pltpu.SemaphoreType.DMA((blocks,)),
         ],
         compiler_params=pltpu.CompilerParams(vmem_limit_bytes=WHOLE_VMEM),
-    )(rows, own, other)
+    )(rows, weight)
 
 
 def gelu_kernel(parts_ref, out_ref):
@@ -364,34 +409,35 @@
     )(parts)
 
 
-def lower_kernel(hidden_ref, own_ref, other_ref, out_ref, buf, sems):
-    block_at = arriving((own_ref, other_ref), buf, sems)
-    shares, blocks, share, _ = hidden_ref.shape
+def lower_kernel(hidden_ref, weight_ref, out_ref, buf, sems):
+    block_at = arriving(weight_ref, buf, sems)
+    _, pair, _, rows = hidden_ref.shape
     targets, draft, width = out_ref.shape
     total = None
-    for block in range(blocks):
-        rows = jnp.concatenate([hidden_ref[piece, block] for piece in range(shares)], axis=0)
-        product = jnp.dot(rows, block_at(block), preferred_element_type=F32)
+    for block in range(weight_ref.shape[0]):
+        product = lax.dot_general(
+            hidden_ref[block // pair, block % pair],
+            block_at(block),
+            (((0,), (0,)), ((), ())),
+            preferred_element_type=F32,
+        )
         total = product if total is None else total + product
     out_ref[...] = total.astype(BF16).reshape(targets, draft, width)
 
 
-def lower_rows(hidden, own, other, targets):
-    vmem = pl.BlockSpec(memory_space=pltpu.VMEM)
-    hbm = pl.BlockSpec(memory_space=pltpu.HBM)
-    rows = hidden.shape[0] * hidden.shape[2]
-    blocks, features, width = own.shape
+def lower_rows(hidden, weight, targets):
+    blocks, features, width = weight.shape
     return pl.pallas_call(
         lower_kernel,
-        out_shape=jax.ShapeDtypeStruct((targets, rows // targets, width), BF16),
-        in_specs=[vmem, hbm, hbm],
-        out_specs=vmem,
+        out_shape=jax.ShapeDtypeStruct((targets, hidden.shape[3] // targets, width), BF16),
+        in_specs=[pl.BlockSpec(memory_space=pltpu.VMEM), pl.BlockSpec(memory_space=pltpu.HBM)],
+        out_specs=pl.BlockSpec(memory_space=pltpu.VMEM),
         scratch_shapes=[
-            pltpu.VMEM((2 * blocks, features, width), BF16),
-            pltpu.SemaphoreType.DMA((2 * blocks,)),
+            pltpu.VMEM((blocks, features, width), BF16),
+            pltpu.SemaphoreType.DMA((blocks,)),
         ],
         compiler_params=pltpu.CompilerParams(vmem_limit_bytes=WHOLE_VMEM),
-    )(hidden, own, other)
+    )(hidden, weight)
 
 
 def finish_kernel(parts_ref, residual_ref, out_ref):
@@ -438,80 +484,65 @@
     up_weight,
     down_weight,
 ):
-    ctx = ("y", "core")
     heads = slopes.shape[0]
     _, draft, width = queries.shape
     prompt_local = prefix_kv.shape[1]
-    ctx_count = lax.axis_size(ctx)
+    ctx_count = lax.axis_size("ctx")
     req_count = lax.axis_size("req")
     mp_count = lax.axis_size("mp")
-    ctx_index = lax.axis_index(ctx)
+    ctx_index = lax.axis_index("ctx")
     model_index = lax.axis_index("mp")
     quarter = ln_gain.shape[0]
-    columns = out_weight.shape[1]
 
     copies = jnp.broadcast_to(queries, (ctx_count, draft, width))
-    gathered = exchange(copies, ctx)
-    out_all = lax.all_gather(out_weight.T, "req", tiled=True)
-    up_own = lax.all_gather(after(up_weight, copies).T, "y")
-    down_own = lax.all_gather(after(down_weight, copies), "y")
+    gathered = exchange(copies, "ctx")
+    out_all = lax.all_gather(out_weight.T, "ctx")
+    up_all = lax.all_gather(after(up_weight, copies).T, "ctx")
+    down_all = lax.all_gather(after(down_weight, copies), "ctx")
 
     vocab_local = embed_table.shape[0]
-    shifted = (
-        token_ids.reshape(ctx_count, req_count, draft).transpose(1, 0, 2).reshape(-1)
-        - model_index * vocab_local
-    )
+    shifted = token_ids.reshape(-1) - model_index * vocab_local
     one_hot = (
         shifted[:, None] == jnp.arange(vocab_local, dtype=jnp.int32)[None, :]
     ).astype(BF16)
     looked_up = jnp.dot(one_hot, embed_table, preferred_element_type=F32).astype(BF16)
     own, own_level = own_part(queries[0], suffix_kv[:, 0], draft_kv[:, 0], slopes, suffix_len)
     gathered, looked_up, own = lax.optimization_barrier((gathered, looked_up, own))
-    embedded = exchange(looked_up.reshape(req_count, ctx_count * draft, columns), "req")
 
     offset = (prompt_local * (ctx_count - ctx_index)).astype(jnp.int32).reshape(1)
-    parts = prompt_part(gathered.reshape(ctx_count * draft, width), prefix_kv, slopes, offset)
-    parts, embedded = lax.optimization_barrier((parts, embedded))
-    embedded = embedded.transpose(1, 0, 2).reshape(ctx_count * draft, req_count * columns)
-    parts = exchange(parts.reshape(ctx_count, draft, -1), ctx)
-    attended = exchange(merge_parts(parts, own, own_level, heads, ctx_count), ctx)
-
-    projected = lax.dot_general(
-        attended.reshape(ctx_count * draft, width),
-        out_all,
-        (((1,), (1,)), ((), ())),
-        preferred_element_type=F32,
-    ) + embedded.astype(F32)
-    projected = exchange(projected.astype(BF16).reshape(ctx_count, draft, -1), ctx)
-    up_other = shifted_by(after(up_own, projected), "core", 1)
-    pieces = exchange(projected.reshape(mp_count, ctx_count // mp_count, draft, -1), "mp")
-    residual, sums = residual_rows(pieces)
+    parts = prompt_part(
+        gathered.reshape(ctx_count * draft, width),
+        prefix_kv,
+        slopes,
+        offset,
+        looked_up.T,
+        ctx_count,
+    )
+    parts = exchange(parts, "ctx")
+    attended = exchange(merge_parts(parts, own, own_level, heads, req_count), "req")
+
+    pieces = exchange(project_rows(attended, out_all, parts, mp_count), ("req", "mp"))
+    residual, sums = residual_rows(pieces, mp_count, draft)
     sums = [sums] + [shifted_by(sums, "mp", step) for step in range(1, mp_count)]
-    normed = norm_rows(residual, sums, ln_gain, quarter * mp_count, req_count)
-    down_other = shifted_by(after(down_own, normed), "core", 1)
-    normed = exchange(normed, "req")
+    normed = exchange(norm_rows(residual, sums, ln_gain, quarter * mp_count, req_count), "req")
 
     lifted = exchange(
-        lift_rows(normed.reshape(req_count * draft, quarter), up_own, up_other, mp_count), "mp"
+        lift_rows(normed.reshape(req_count * draft, quarter), up_all, mp_count), "mp"
     )
     activated = exchange(activate(lifted), "mp")
-    lowered = exchange(lower_rows(activated, down_own, down_other, req_count), "req")
+    lowered = exchange(lower_rows(activated, down_all, req_count), "req")
     layer_out = finish(lowered, residual)
     return residual[None], layer_out[None]
 
 
 def solution(mesh):
-    chips = jax.sharding.Mesh(
-        mesh.devices.reshape((mesh.shape["ctx"] // 2, 2) + mesh.devices.shape[1:]),
-        ("y", "core", "req", "mp"),
-    )
-    rows = ("y", "core", "req")
+    rows = ("ctx", "req")
     in_specs = (
         P(),
         P("mp", rows),
         P(rows, None, "mp"),
         P(None, rows, None, "mp"),
-        P(None, ("y", "core"), "mp"),
+        P(None, "ctx", "mp"),
         P(None, rows, None, "mp"),
         P(rows),
         P("mp"),
@@ -522,5 +553,5 @@
     )
     out_specs = (P(rows, None, "mp"), P(rows, None, "mp"))
     return jax.shard_map(
-        per_device, mesh=chips, in_specs=in_specs, out_specs=out_specs, check_vma=False
-    )
+        per_device, mesh=mesh, in_specs=in_specs, out_specs=out_specs, check_vma=False
+    )

time: 239 us -> 185 us (0.77)
  waiting for transfers between devices: 57 us -> 10.4 us
  starting transfers between devices: 25.5 us -> 14.3 us
  blocking collectives: 90.2 us -> 94.1 us
  Pallas kernels: 35.4 us -> 38.6 us
    all_gather x3, waiting for transfers between devices: 35.8 us -> 0.01 us  [the longest x1 0.01 us: per_device(): out_all = lax.all_gather(out_weight.T, 'ctx')]
    all_to_all x4 -> x2, starting transfers between devices: 21.2 us -> 9.37 us  [exchange(): return lax.all_to_all(value, axis, split_axis=0, concat_axis=0, tiled=True)]
    all_to_all x4 -> x2, waiting for transfers between devices: 17.1 us -> 6.28 us  [exchange(): return lax.all_to_all(value, axis, split_axis=0, concat_axis=0, tiled=True)]
    all_to_all x6, blocking collectives: 90.2 us -> 94.1 us  [exchange(): return lax.all_to_all(value, axis, split_axis=0, concat_axis=0, tiled=True)]
    pallas_call x3 -> x4, Pallas kernels: 14.4 us -> 17.4 us  [the longest x1 7.5 us: lift_rows(): pl.pallas_call(lift_kernel, out_shape=jax.ShapeDtypeStruct((mp, blocks //...]
    ppermute x5 -> x3, starting transfers between devices: 4.15 us -> 4.8 us  [shifted_by(): lax.ppermute(value, axis, [(i, (i + step) % count) for i in range(count)])]
  transfers between devices with their start and end apart: 12 -> 8, of which waited for: 7 -> 3; matrix products, arithmetic and copies ran while one was open for 5% -> 5% of each run, Pallas kernels for 12% -> 17%
where the time goes in v3:
time: 185 us; the launch traced here: 184 us
  blocking collectives  94.1 us (51%)
  Pallas kernels  38.6 us (21%)
  between operations  14.5 us (8%)
  starting transfers between devices  14.3 us (8%)
  waiting for transfers between devices  10.4 us (6%)
  matrix products  6.61 us (4%)
  local copies, waits for them, and re-layouts  4.83 us (3%)
    all_to_all x6, blocking collectives, exchange(): return lax.all_to_all(value, axis, split_axis=0, concat_axis=0, tiled=True)  94.1 us
    pallas_call x1, Pallas kernels, prompt_part(): pl.pallas_call(functools.partial(prompt_kernel, heads=heads, head_size=wi...  11.9 us
    all_to_all x2, starting transfers between devices, exchange(): return lax.all_to_all(value, axis, split_axis=0, concat_axis=0, tiled=True)  9.37 us
    pallas_call x1, Pallas kernels, lift_rows(): pl.pallas_call(lift_kernel, out_shape=jax.ShapeDtypeStruct((mp, blocks //...  7.5 us
    dot_general x1, matrix products, per_device(): jnp.dot(one_hot, embed_table, preferred_element_type=F32).astype(BF16)  6.61 us
    all_to_all x2, waiting for transfers between devices, exchange(): return lax.all_to_all(value, axis, split_axis=0, concat_axis=0, tiled=True)  6.28 us
    pallas_call x1, Pallas kernels, lower_rows(): pl.pallas_call(lower_kernel, out_shape=jax.ShapeDtypeStruct((targets, hid...  5.07 us
    ppermute x3, starting transfers between devices, shifted_by(): lax.ppermute(value, axis, [(i, (i + step) % count) for i in range(count)])  4.8 us
  transfers between devices with their start and end apart: 8, of which 3 were waited for; matrix products, arithmetic and copies ran while one was open for 5% of the time, Pallas kernels for 17%

profile of v3, /device:TPU:2, one launch (start us, length us, event | category | flops | bytes accessed | tf_op | source)
XLA Modules:
  0.0 184.0 jit_solution(6661064072253266254)
XLA Ops:
  7.2 0.0 copy-start
  7.2 0.0 all-gather.7.cloned.1.call-start
  7.2 0.7 all-gather.7.cloned.1.call-update
  7.9 0.0 all-gather.9.cloned.1.call-start
  8.0 1.5 broadcast_in_dim.19
  9.4 0.0 all-gather.9.cloned.1.call-update
  9.4 0.0 all-gather.11.cloned.1.call-start
  9.5 0.7 all-gather.11.cloned.1.call-update
  10.2 4.5 %all-to-all-start = ((bf16[8,16,896]{2,1,0:T(8,128)(2,1)}), bf16[8,16,896]{2,1,0:T(8,128)(2,1)}, u32[]{:S(2)}, u32[]{:S(2)}) async-start(bf16[8,16,896]{2,1,0:T(8,128)(2,1)} %broadcast_in_dim.19), calls=%async_computation | async-start | bytes 458752 | tf_op jit(solution)/shard_map/all_to_all | solution.py:470
  14.7 0.7 broadcast_subtract_fusion
  15.4 0.1 copy.14
  15.5 0.1 sub.19
  15.5 0.0 copy-done
  15.5 0.0 copy-start.2
  15.6 0.0 copy-start.4
  15.6 0.0 copy-start.6
  15.6 6.6 %fusion.2 = bf16[1024,112]{0,1:T(8,128)(2,1)} fusion(bf16[6400,112]{0,1:T(8,128)(2,1)S(1)} %copy-done, s32[1024]{0:T(1024)S(1)} %sub.19), kind=kOutput, calls=%fused_computation.3 | convolution fusion | flops 1474674688 | bytes 1667072 | tf_op jit(solution)/shard_map/dot_general | solution.py:508
  22.9 1.6 shard_map.131
  24.5 0.0 copy-start.3
  24.5 0.6 copy-done.3
  25.1 0.6 copy-done.5
  25.7 0.0 all-to-all-done
  25.7 11.9 %shard_map.132 = bf16[8,240,128]{2,1,0:T(8,128)(2,1)} custom-call(s32[1]{0:T(128)} %bitcast.offset_ref, f32[8]{0:T(128)} %slopes_ref.3, bf16[128,896]{1,0:T(8,128)(2,1)} %bitcast.4.query_ref, bf16[112,1024]{1,0:T(8,128)(2,1)} %bitcast.25, bf16[2,2048,896]{2,1,0:T(8,128)(2,1)} %prefix_ref.1), custom_call_target="tpu_custom_call" | custom-call | tf_op jit(solution)/shard_map/pallas_call | solution.py:128
  37.6 15.0 %all_to_all.40.parts_ref = bf16[8,240,128]{2,1,0:T(8,128)(2,1)} all-to-all(bf16[8,240,128]{2,1,0:T(8,128)(2,1)} %shard_map.132), channel_id=1, replica_groups=mesh['ctx'=8,'req'=8,'mp'=4] {'ctx'}, dimensions={0} | all-to-all | bytes 983040 | tf_op jit(solution)/shard_map/all_to_all | solution.py:470
  52.6 2.2 %shard_map.133 = bf16[8,16,896]{2,1,0:T(8,128)(2,1)} custom-call(bf16[8,240,128]{2,1,0:T(8,128)(2,1)} %all_to_all.40.parts_ref, f32[16,896]{1,0:T(8,128)} %copy-done.3, f32[16,128]{1,0:T(8,128)} %copy-done.5), custom_call_target="tpu_custom_call" | custom-call | tf_op jit(solution)/shard_map/pallas_call | solution.py:259
  54.8 19.4 %all_to_all.41.rows_ref = bf16[8,16,896]{2,1,0:T(8,128)(2,1)} all-to-all(bf16[8,16,896]{2,1,0:T(8,128)(2,1)} %shard_map.133), channel_id=1, replica_groups=mesh['ctx'=8,'req'=8,'mp'=4] {'req'}, dimensions={0} | all-to-all | bytes 458752 | tf_op jit(solution)/shard_map/all_to_all | solution.py:470
  74.2 3.1 %shard_map.134 = bf16[32,32,112]{2,1,0:T(8,128)(2,1)} custom-call(bf16[8,16,896]{2,1,0:T(8,128)(2,1)} %all_to_all.41.rows_ref, bf16[8,112,896]{2,1,0:T(8,128)(2,1)} %bitcast.22, bf16[8,240,128]{2,1,0:T(8,128)(2,1)} %all_to_all.40.parts_ref), custom_call_target="tpu_custom_call" | custom-call | tf_op jit(solution)/shard_map/pallas_call | solution.py:291
  77.3 15.3 %all_to_all.42.parts_ref = bf16[32,32,112]{2,1,0:T(8,128)(2,1)} all-to-all(bf16[32,32,112]{2,1,0:T(8,128)(2,1)} %shard_map.134), channel_id=1, replica_groups=mesh['ctx'=8,'req'=8,'mp'=4] {'req','mp'}, dimensions={0} | all-to-all | bytes 458752 | tf_op jit(solution)/shard_map/all_to_all | solution.py:470
  92.6 1.7 shard_map.135
  94.4 1.5 collective-permute-start
  95.8 2.8 %collective-permute-start.1 = (f32[16,128]{1,0:T(8,128)}, f32[16,128]{1,0:T(8,128)S(1)}, u32[]{:S(2)}, u32[]{:S(2)}) collective-permute-start(f32[16,128]{1,0:T(8,128)} %get-tuple-element.17.rest_0_), channel_id=1, source_target_pairs={{0,2},{1,3},{2,0},{3,1},{4,6},{5,7},{6,4},{7,5},{8,10},{9,11},{10,... | collective-permute-start | bytes 24584 | tf_op jit(solution)/shard_map/ppermute | solution.py:466
  98.7 0.5 collective-permute-start.2
  99.2 0.6 broadcast_in_dim.21.gain_ref
  99.8 0.0 collective-permute-done.rest_1_
  99.8 1.4 collective-permute-done.1.rest_2_
  101.2 1.3 collective-permute-done.2.rest_3_
  102.5 0.6 copy-done.10
  103.1 1.9 %shard_map.136 = bf16[8,16,1792]{2,1,0:T(8,128)(2,1)} custom-call(f32[16,1792]{1,0:T(8,128)} %get-tuple-element.16.residual_ref, f32[1,1792]{1,0:T(1,128)} %broadcast_in_dim.21.gain_ref, f32[16,128]{1,0:T(8,128)} %get-tuple-element.17.rest_0_, f32[16,128]{1,0:T(8,128)} %copy-done.8, f32[16,128]{1,0:T(8,128)} %copy-done.9, f32[16,128]{1,0:T(8,128)} %copy-done.10), custom_call_target="tpu_custom_call" | custom-call | tf_op jit(solution)/shard_map/pallas_call | solution.py:345
  105.0 16.7 %all_to_all.43 = bf16[8,16,1792]{2,1,0:T(8,128)(2,1)} all-to-all(bf16[8,16,1792]{2,1,0:T(8,128)(2,1)} %shard_map.136), channel_id=1, replica_groups=mesh['ctx'=8,'req'=8,'mp'=4] {'req'}, dimensions={0} | all-to-all | bytes 917504 | tf_op jit(solution)/shard_map/all_to_all | solution.py:470
  121.7 7.5 %shard_map.137 = bf16[4,2,224,128]{3,2,1,0:T(8,128)(2,1)} custom-call(bf16[128,1792]{1,0:T(8,128)(2,1)} %bitcast.21, bf16[8,224,1792]{2,1,0:T(8,128)(2,1)} %bitcast.20), custom_call_target="tpu_custom_call" | custom-call | tf_op jit(solution)/shard_map/pallas_call | solution.py:380
  129.2 11.0 %all_to_all.44.parts_ref = bf16[4,2,224,128]{3,2,1,0:T(8,128)(2,1)} all-to-all(bf16[4,2,224,128]{3,2,1,0:T(8,128)(2,1)} %shard_map.137), channel_id=1, replica_groups=mesh['ctx'=8,'req'=8,'mp'=4] {'mp'}, dimensions={0} | all-to-all | bytes 917504 | tf_op jit(solution)/shard_map/all_to_all | solution.py:470
  140.2 1.9 %shard_map.138 = bf16[4,2,224,128]{3,2,1,0:T(8,128)(2,1)} custom-call(bf16[4,2,224,128]{3,2,1,0:T(8,128)(2,1)} %all_to_all.44.parts_ref), custom_call_target="tpu_custom_call" | custom-call | tf_op jit(solution)/shard_map/pallas_call | solution.py:404
  142.1 4.9 %all-to-all-start.6 = ((bf16[4,2,224,128]{3,2,1,0:T(8,128)(2,1)}), bf16[4,2,224,128]{3,2,1,0:T(8,128)(2,1)S(1)}, u32[]{:S(2)}, u32[]{:S(2)}) async-start(bf16[4,2,224,128]{3,2,1,0:T(8,128)(2,1)} %shard_map.138), calls=%async_computation.6 | async-start | bytes 917504 | tf_op jit(solution)/shard_map/all_to_all | solution.py:470
  147.0 6.3 %all-to-all-done.6.hidden_ref = bf16[4,2,224,128]{3,2,1,0:T(8,128)(2,1)S(1)} async-done(((bf16[4,2,224,128]{3,2,1,0:T(8,128)(2,1)}), bf16[4,2,224,128]{3,2,1,0:T(8,128)(2,1)S(1)}, u32[]{:S(2)}, u32[]{:S(2)}) %all-to-all-start.6) | async-done | bytes 458784 | tf_op jit(solution)/shard_map/all_to_all | solution.py:470
  153.2 0.8 copy-done.7
  154.0 5.1 %shard_map.139 = bf16[8,16,1792]{2,1,0:T(8,128)(2,1)} custom-call(bf16[4,2,224,128]{3,2,1,0:T(8,128)(2,1)} %copy-done.7, bf16[8,224,1792]{2,1,0:T(8,128)(2,1)} %bitcast.19), custom_call_target="tpu_custom_call" | custom-call | tf_op jit(solution)/shard_map/pallas_call | solution.py:430
  159.1 16.7 %all_to_all.45.parts_ref = bf16[8,16,1792]{2,1,0:T(8,128)(2,1)} all-to-all(bf16[8,16,1792]{2,1,0:T(8,128)(2,1)} %shard_map.139), channel_id=1, replica_groups=mesh['ctx'=8,'req'=8,'mp'=4] {'req'}, dimensions={0} | all-to-all | bytes 917504 | tf_op jit(solution)/shard_map/all_to_all | solution.py:470
  175.8 1.7 shard_map.140
  (17 shorter events, 0.0 us)
Async XLA Ops:
  7.2 8.4 %copy-start = (bf16[6400,112]{0,1:T(8,128)(2,1)S(1)}, bf16[6400,112]{0,1:T(8,128)(2,1)}, u32[]{:S(2)}) copy-start(bf16[6400,112]{0,1:T(8,128)(2,1)} %param.13) | copy-start | bytes 4300804
  7.2 67.0 %all-gather.7.cloned.1.call-start = ((), (), s32[]{:S(2)}) async-start(), calls=%async_computation.8 | async-start | bytes 1806336 | tf_op jit(solution)/shard_map/all_gather | solution.py:499
  7.9 113.8 %all-gather.9.cloned.1.call-start = ((), (), s32[]{:S(2)}) async-start(), calls=%async_computation.9 | async-start | bytes 7225344 | tf_op jit(solution)/shard_map/all_gather | solution.py:500
  9.4 137.5 %all-gather.11.cloned.1.call-start = ((), (), s32[]{:S(2)}) async-start(), calls=%async_computation.10 | async-start | bytes 7225344 | tf_op jit(solution)/shard_map/all_gather | solution.py:501
  10.2 15.6 %all-to-all-start = ((bf16[8,16,896]{2,1,0:T(8,128)(2,1)}), bf16[8,16,896]{2,1,0:T(8,128)(2,1)}, u32[]{:S(2)}, u32[]{:S(2)}) async-start(bf16[8,16,896]{2,1,0:T(8,128)(2,1)} %broadcast_in_dim.19), calls=%async_computation | async-start | bytes 458752 | tf_op jit(solution)/shard_map/all_to_all | solution.py:470
  15.5 7.3 %copy-start.1 = (bf16[2,1,512,896]{3,2,1,0:T(8,128)(2,1)S(1)}, bf16[2,1,512,896]{3,2,1,0:T(8,128)(2,1)}, u32[]{:S(2)}) copy-start(bf16[2,1,512,896]{3,2,1,0:T(8,128)(2,1)} %param.17) | copy-start | bytes 5505028
  15.5 7.3 %copy-start.2 = (bf16[1,16,896]{2,1,0:T(8,128)(2,1)S(1)}, bf16[1,16,896]{2,1,0:T(8,128)(2,1)}, u32[]{:S(2)}) copy-start(bf16[1,16,896]{2,1,0:T(8,128)(2,1)} %param.14) | copy-start | bytes 86020
  15.6 7.3 %copy-start.4 = (bf16[2,1,16,896]{3,2,1,0:T(8,128)(2,1)S(1)}, bf16[2,1,16,896]{3,2,1,0:T(8,128)(2,1)}, u32[]{:S(2)}) copy-start(bf16[2,1,16,896]{3,2,1,0:T(8,128)(2,1)} %param.15) | copy-start | bytes 172036
  15.6 7.3 %copy-start.6 = (f32[8]{0:T(128)S(1)}, f32[8]{0:T(128)}, u32[]{:S(2)}) copy-start(f32[8]{0:T(128)} %slopes_ref.3) | copy-start | bytes 100
  24.5 0.6 copy-start.3
  25.1 0.6 copy-start.5
  25.7 73.4 %copy-start.11 = (f32[1792]{0:T(1024)S(1)}, f32[1792]{0:T(1024)}, u32[]{:S(2)}) copy-start(f32[1792]{0:T(1024)} %param.21) | copy-start | bytes 21508
  94.4 5.4 %collective-permute-start = (f32[16,128]{1,0:T(8,128)}, f32[16,128]{1,0:T(8,128)S(1)}, u32[]{:S(2)}, u32[]{:S(2)}) collective-permute-start(f32[16,128]{1,0:T(8,128)} %get-tuple-element.17.rest_0_), channel_id=1, source_target_pairs={{0,1},{1,2},{2,3},{3,0},{4,5},{5,6},{6,7},{7,4},{8,9},{9,10},{10,1... | collective-permute-start | bytes 24584 | tf_op jit(solution)/shard_map/ppermute | solution.py:466
  95.8 5.4 %collective-permute-start.1 = (f32[16,128]{1,0:T(8,128)}, f32[16,128]{1,0:T(8,128)S(1)}, u32[]{:S(2)}, u32[]{:S(2)}) collective-permute-start(f32[16,128]{1,0:T(8,128)} %get-tuple-element.17.rest_0_), channel_id=1, source_target_pairs={{0,2},{1,3},{2,0},{3,1},{4,6},{5,7},{6,4},{7,5},{8,10},{9,11},{10,... | collective-permute-start | bytes 24584 | tf_op jit(solution)/shard_map/ppermute | solution.py:466
  98.7 3.9 %collective-permute-start.2 = (f32[16,128]{1,0:T(8,128)}, f32[16,128]{1,0:T(8,128)S(1)}, u32[]{:S(2)}, u32[]{:S(2)}) collective-permute-start(f32[16,128]{1,0:T(8,128)} %get-tuple-element.17.rest_0_), channel_id=1, source_target_pairs={{0,3},{1,0},{2,1},{3,2},{4,7},{5,4},{6,5},{7,6},{8,11},{9,8},{10,9... | collective-permute-start | bytes 24584 | tf_op jit(solution)/shard_map/ppermute | solution.py:466
  99.8 2.8 %copy-start.8 = (f32[16,128]{1,0:T(8,128)}, f32[16,128]{1,0:T(8,128)S(1)}, u32[]{:S(2)}) copy-start(f32[16,128]{1,0:T(8,128)S(1)} %collective-permute-done.rest_1_) | copy-start | bytes 24580
  101.2 1.3 copy-start.9
  102.5 0.6 copy-start.10
  142.1 11.2 %all-to-all-start.6 = ((bf16[4,2,224,128]{3,2,1,0:T(8,128)(2,1)}), bf16[4,2,224,128]{3,2,1,0:T(8,128)(2,1)S(1)}, u32[]{:S(2)}, u32[]{:S(2)}) async-start(bf16[4,2,224,128]{3,2,1,0:T(8,128)(2,1)} %shard_map.138), calls=%async_computation.6 | async-start | bytes 917504 | tf_op jit(solution)/shard_map/all_to_all | solution.py:470
  153.2 0.8 copy-start.7
Sparse Core Ops, SparseCore 0:
  9.8 30.0 all-gather.6
  41.8 44.0 all-gather.8
  87.7 44.1 all-gather.10

commit v4 on v3

--- a/solution.py
+++ b/solution.py
@@ -11,7 +11,7 @@
 LANES = 128
 F32 = jnp.float32
 BF16 = jnp.bfloat16
-WHOLE_VMEM = 58 * 1024 * 1024
+MIB = 1024 * 1024
 
 
 def head_lanes(head, tile, head_size):
@@ -38,38 +38,21 @@
 
 
 def prompt_kernel(
-    offset_ref, slopes_ref, query_ref, looked_ref, prefix_ref, out_ref, kv_buf, sems, *, heads, head_size
+    offset_ref, slopes_ref, query_ref, looked_ref, prefix_ref, out_ref, *, heads, head_size
 ):
     rows, width = query_ref.shape
-    keys = kv_buf.shape[2]
+    keys = prefix_ref.shape[1]
     tiles = width // LANES
-    copies = {}
-    for tile in range(tiles):
-        for which in range(2):
-            copies[which, tile] = pltpu.make_async_copy(
-                prefix_ref.at[which, :, pl.ds(tile * LANES, LANES)],
-                kv_buf.at[which, tile],
-                sems.at[which, tile],
-            )
-            copies[which, tile].start()
     scale = 1.0 / math.sqrt(head_size)
     position = (
         lax.broadcasted_iota(jnp.int32, (1, keys), 1) - offset_ref[0]
     ).astype(F32)
-    arrived = set()
-
-    def wait(which, tile):
-        if (which, tile) not in arrived:
-            arrived.add((which, tile))
-            copies[which, tile].wait()
-
     parts = [jnp.zeros((rows, LANES), F32) for _ in range(tiles)]
     stats = jnp.zeros((rows, LANES), F32)
     stat_lane = lax.broadcasted_iota(jnp.int32, (rows, LANES), 1)
     for head in range(heads):
         span = head_tiles(head, head_size)
-        for tile in span:
-            wait(0, tile)
+        window = slice(span[0] * LANES, (span[-1] + 1) * LANES)
         query_window = jnp.concatenate(
             [
                 jnp.where(
@@ -81,18 +64,19 @@
             ],
             axis=1,
         )
-        key_window = jnp.concatenate([kv_buf[0, tile] for tile in span], axis=1)
         scores = lax.dot_general(
-            query_window, key_window, (((1,), (1,)), ((), ())), preferred_element_type=F32
+            query_window,
+            prefix_ref[0, :, window],
+            (((1,), (1,)), ((), ())),
+            preferred_element_type=F32,
         )
         scores = scores * scale + slopes_ref[head] * position
         top = jnp.max(scores, axis=1, keepdims=True)
         weights = jnp.exp(scores - top)
         total = jnp.sum(weights, axis=1, keepdims=True)
-        for tile in span:
-            wait(1, tile)
-        value_window = jnp.concatenate([kv_buf[1, tile] for tile in span], axis=1)
-        sums = jnp.dot(weights.astype(BF16), value_window, preferred_element_type=F32)
+        sums = jnp.dot(
+            weights.astype(BF16), prefix_ref[1, :, window], preferred_element_type=F32
+        )
         sums = sums * (1.0 / total)
         for place, tile in enumerate(span):
             parts[tile] = jnp.where(
@@ -123,7 +107,6 @@
 def prompt_part(query_rows, prefix_kv, slopes, offset, looked_up, targets):
     rows, width = query_rows.shape
     heads = slopes.shape[0]
-    keys = prefix_kv.shape[1]
     tiles = width // LANES
     return pl.pallas_call(
         functools.partial(prompt_kernel, heads=heads, head_size=width // heads),
@@ -135,14 +118,10 @@
             pl.BlockSpec(memory_space=pltpu.SMEM),
             pl.BlockSpec(memory_space=pltpu.VMEM),
             pl.BlockSpec(memory_space=pltpu.VMEM),
-            pl.BlockSpec(memory_space=pltpu.HBM),
+            pl.BlockSpec(memory_space=pltpu.VMEM),
         ],
         out_specs=pl.BlockSpec(memory_space=pltpu.VMEM),
-        scratch_shapes=[
-            pltpu.VMEM((2, tiles, keys, LANES), BF16),
-            pltpu.SemaphoreType.DMA((2, tiles)),
-        ],
-        compiler_params=pltpu.CompilerParams(vmem_limit_bytes=WHOLE_VMEM),
+        compiler_params=pltpu.CompilerParams(vmem_limit_bytes=20 * MIB),
     )(offset, slopes, query_rows, looked_up, prefix_kv)
 
 
@@ -212,7 +191,7 @@
         ),
         in_specs=[smem, smem, vmem, vmem, vmem],
         out_specs=(vmem, vmem),
-        compiler_params=pltpu.CompilerParams(vmem_limit_bytes=24 * 1024 * 1024),
+        compiler_params=pltpu.CompilerParams(vmem_limit_bytes=12 * MIB),
     )(length, slopes, query_rows, suffix_kv, draft_kv)
 
 
@@ -264,19 +243,33 @@
     )(parts, own, level)
 
 
+def packed_sums(value, lanes):
+    lane = lax.broadcasted_iota(jnp.int32, (value.shape[0], lanes), 1)
+    packed = jnp.zeros((value.shape[0], lanes), F32)
+    for place, term in enumerate(split_three(value)):
+        packed = jnp.where(lane == place, term, packed)
+    return packed.astype(BF16)
+
+
 def project_kernel(rows_ref, weight_ref, parts_ref, out_ref):
     blocks, columns, _ = weight_ref.shape
-    targets, held, _ = out_ref.shape
+    targets, held, lanes = out_ref.shape
     req, draft, width = rows_ref.shape
     mp = targets // req
     pair = held // draft
     rows = rows_ref[...].reshape(req * draft, width)
+    products = []
     for block in range(blocks):
         product = lax.dot_general(
             rows, weight_ref[block], (((1,), (1,)), ((), ())), preferred_element_type=F32
         )
         looked_up = parts_ref[block, parts_ref.shape[1] - columns :].astype(F32)
-        product = (product + jnp.transpose(looked_up)).astype(BF16)
+        products.append(product + jnp.transpose(looked_up))
+    sums = packed_sums(
+        jnp.sum(functools.reduce(jnp.add, products), axis=1, keepdims=True), lanes - columns
+    )
+    for block, product in enumerate(products):
+        product = jnp.concatenate([product.astype(BF16), sums], axis=1)
         piece, half = divmod(block, pair)
         for target in range(req):
             out_ref[target * mp + piece, half * draft : (half + 1) * draft] = product[
@@ -287,18 +280,19 @@
 def project_rows(rows, weight, parts, mp):
     req, draft, _ = rows.shape
     blocks, columns, _ = weight.shape
+    lanes = -(-(columns + 3) // LANES) * LANES
     vmem = pl.BlockSpec(memory_space=pltpu.VMEM)
     return pl.pallas_call(
         project_kernel,
-        out_shape=jax.ShapeDtypeStruct((req * mp, blocks // mp * draft, columns), BF16),
+        out_shape=jax.ShapeDtypeStruct((req * mp, blocks // mp * draft, lanes), BF16),
         in_specs=[vmem, vmem, vmem],
         out_specs=vmem,
     )(rows, weight, parts)
 
 
-def residual_kernel(parts_ref, out_ref, sums_ref, *, mp):
-    sources, held, columns = parts_ref.shape
-    draft = out_ref.shape[0]
+def residual_kernel(parts_ref, gain_ref, out_ref, centred_ref, *, mp, columns):
+    sources, held, _ = parts_ref.shape
+    draft, width = out_ref.shape
     blocks = []
     for half in range(held // draft):
         lines = slice(half * draft, (half + 1) * draft)
@@ -307,136 +301,105 @@
             for piece in range(1, mp):
                 block += parts_ref[source * mp + piece, lines].astype(F32)
             blocks.append(block)
-    residual = jnp.concatenate(blocks, axis=1)
+    residual = jnp.concatenate([block[:, :columns] for block in blocks], axis=1)
     out_ref[...] = residual
-    lane = lax.broadcasted_iota(jnp.int32, (draft, LANES), 1)
-    first = jnp.sum(residual, axis=1, keepdims=True)
-    second = jnp.sum(residual * residual, axis=1, keepdims=True)
-    sums_ref[...] = jnp.where(lane == 0, first, jnp.where(lane == 1, second, 0.0))
-
-
-def residual_rows(parts, mp, draft):
-    sources, held, columns = parts.shape
-    vmem = pl.BlockSpec(memory_space=pltpu.VMEM)
-    return pl.pallas_call(
-        functools.partial(residual_kernel, mp=mp),
+    sums = functools.reduce(jnp.add, blocks[: sources // mp])
+    mean = sum(sums[:, columns + term : columns + term + 1] for term in range(3)) / (mp * width)
+    centred = residual - mean
+    squares = packed_sums(jnp.sum(centred * centred, axis=1, keepdims=True), LANES)
+    scaled = (centred * gain_ref[...]).astype(BF16)
+    for target in range(centred_ref.shape[0]):
+        centred_ref[target, :, :width] = scaled
+        centred_ref[target, :, width:] = squares
+
+
+def residual_rows(parts, gain, mp, draft, columns, targets):
+    vmem = pl.BlockSpec(memory_space=pltpu.VMEM)
+    width = gain.shape[0]
+    return pl.pallas_call(
+        functools.partial(residual_kernel, mp=mp, columns=columns),
         out_shape=(
-            jax.ShapeDtypeStruct((draft, sources // mp * held // draft * columns), F32),
-            jax.ShapeDtypeStruct((draft, LANES), F32),
+            jax.ShapeDtypeStruct((draft, width), F32),
+            jax.ShapeDtypeStruct((targets, draft, width + LANES), BF16),
         ),
-        in_specs=[vmem],
+        in_specs=[vmem, vmem],
         out_specs=(vmem, vmem),
-    )(parts)
-
-
-def norm_kernel(residual_ref, gain_ref, *rest, model_width):
-    *sums_refs, out_ref = rest
-    sums = functools.reduce(jnp.add, [ref[...] for ref in sums_refs])
-    mean = sums[:, 0:1] / model_width
-    mean_square = sums[:, 1:2] / model_width
-    factor = lax.rsqrt(mean_square - mean * mean + 1e-05)
-    normed = ((residual_ref[...] - mean) * factor * gain_ref[...]).astype(BF16)
-    for target in range(out_ref.shape[0]):
-        out_ref[target] = normed
-
-
-def norm_rows(residual, sums, gain, model_width, targets):
-    vmem = pl.BlockSpec(memory_space=pltpu.VMEM)
-    return pl.pallas_call(
-        functools.partial(norm_kernel, model_width=model_width),
-        out_shape=jax.ShapeDtypeStruct((targets,) + residual.shape, BF16),
-        in_specs=[vmem] * (2 + len(sums)),
+    )(parts, gain[None, :])
+
+
+def lift_kernel(rows_ref, weight_ref, out_ref):
+    blocks, hidden, width = weight_ref.shape
+    mp, height, _ = out_ref.shape
+    pair = blocks // mp
+    rows = rows_ref[:, :width]
+    for block in range(blocks):
+        piece, place = divmod(block, pair)
+        out_ref[piece, place * hidden : (place + 1) * hidden] = lax.dot_general(
+            weight_ref[block], rows, (((1,), (1,)), ((), ())), preferred_element_type=F32
+        ).astype(BF16)
+    squares = jnp.transpose(rows_ref[:, width:].astype(F32)).astype(BF16)
+    for piece in range(mp):
+        out_ref[piece, pair * hidden :] = squares[: height - pair * hidden]
+
+
+def lift_rows(rows, weight, mp):
+    blocks, hidden, _ = weight.shape
+    vmem = pl.BlockSpec(memory_space=pltpu.VMEM)
+    return pl.pallas_call(
+        lift_kernel,
+        out_shape=jax.ShapeDtypeStruct((mp, blocks // mp * hidden + 16, rows.shape[0]), BF16),
+        in_specs=[vmem, vmem],
         out_specs=vmem,
-    )(residual, gain[None, :], *sums)
-
-
-def arriving(ref, buf, sems):
-    copies = [
-        pltpu.make_async_copy(ref.at[block], buf.at[block], sems.at[block])
-        for block in range(ref.shape[0])
-    ]
-    for copy in copies:
-        copy.start()
-
-    def block_at(index):
-        copies[index].wait()
-        return buf[index]
-
-    return block_at
-
-
-def lift_kernel(rows_ref, weight_ref, out_ref, buf, sems):
-    block_at = arriving(weight_ref, buf, sems)
-    rows = rows_ref[...]
-    pair = out_ref.shape[1]
-    for block in range(weight_ref.shape[0]):
-        out_ref[block // pair, block % pair] = lax.dot_general(
-            block_at(block), rows, (((1,), (1,)), ((), ())), preferred_element_type=F32
-        ).astype(BF16)
-
-
-def lift_rows(rows, weight, mp):
-    blocks, hidden, width = weight.shape
-    return pl.pallas_call(
-        lift_kernel,
-        out_shape=jax.ShapeDtypeStruct((mp, blocks // mp, hidden, rows.shape[0]), BF16),
-        in_specs=[pl.BlockSpec(memory_space=pltpu.VMEM), pl.BlockSpec(memory_space=pltpu.HBM)],
-        out_specs=pl.BlockSpec(memory_space=pltpu.VMEM),
-        scratch_shapes=[
-            pltpu.VMEM((blocks, hidden, width), BF16),
-            pltpu.SemaphoreType.DMA((blocks,)),
-        ],
-        compiler_params=pltpu.CompilerParams(vmem_limit_bytes=WHOLE_VMEM),
+        compiler_params=pltpu.CompilerParams(vmem_limit_bytes=20 * MIB),
     )(rows, weight)
 
 
-def gelu_kernel(parts_ref, out_ref):
+def gelu_kernel(parts_ref, out_ref, *, model_width):
+    hidden = out_ref.shape[1]
     total = parts_ref[0].astype(F32)
     for piece in range(1, parts_ref.shape[0]):
         total += parts_ref[piece].astype(F32)
-    activated = (0.5 * total * (1.0 + lax.erf(total * math.sqrt(0.5)))).astype(BF16)
+    squares = sum(total[hidden + term : hidden + term + 1] for term in range(3))
+    lifted = total[:hidden] * lax.rsqrt(squares / model_width + 1e-05)
+    activated = (0.5 * lifted * (1.0 + lax.erf(lifted * math.sqrt(0.5)))).astype(BF16)
     for target in range(out_ref.shape[0]):
         out_ref[target] = activated
 
 
-def activate(parts):
-    vmem = pl.BlockSpec(memory_space=pltpu.VMEM)
-    return pl.pallas_call(
-        gelu_kernel,
-        out_shape=jax.ShapeDtypeStruct(parts.shape, BF16),
+def activate(parts, hidden, model_width):
+    vmem = pl.BlockSpec(memory_space=pltpu.VMEM)
+    return pl.pallas_call(
+        functools.partial(gelu_kernel, model_width=model_width),
+        out_shape=jax.ShapeDtypeStruct((parts.shape[0], hidden, parts.shape[2]), BF16),
         in_specs=[vmem],
         out_specs=vmem,
     )(parts)
 
 
-def lower_kernel(hidden_ref, weight_ref, out_ref, buf, sems):
-    block_at = arriving(weight_ref, buf, sems)
-    _, pair, _, rows = hidden_ref.shape
-    targets, draft, width = out_ref.shape
+def lower_kernel(hidden_ref, weight_ref, out_ref):
+    blocks, features, _ = weight_ref.shape
+    pair = blocks // hidden_ref.shape[0]
     total = None
-    for block in range(weight_ref.shape[0]):
+    for block in range(blocks):
+        piece, place = divmod(block, pair)
         product = lax.dot_general(
-            hidden_ref[block // pair, block % pair],
-            block_at(block),
+            hidden_ref[piece, place * features : (place + 1) * features],
+            weight_ref[block],
             (((0,), (0,)), ((), ())),
             preferred_element_type=F32,
         )
         total = product if total is None else total + product
-    out_ref[...] = total.astype(BF16).reshape(targets, draft, width)
+    out_ref[...] = total.astype(BF16).reshape(out_ref.shape)
 
 
 def lower_rows(hidden, weight, targets):
-    blocks, features, width = weight.shape
+    vmem = pl.BlockSpec(memory_space=pltpu.VMEM)
     return pl.pallas_call(
         lower_kernel,
-        out_shape=jax.ShapeDtypeStruct((targets, hidden.shape[3] // targets, width), BF16),
-        in_specs=[pl.BlockSpec(memory_space=pltpu.VMEM), pl.BlockSpec(memory_space=pltpu.HBM)],
-        out_specs=pl.BlockSpec(memory_space=pltpu.VMEM),
-        scratch_shapes=[
-            pltpu.VMEM((blocks, features, width), BF16),
-            pltpu.SemaphoreType.DMA((blocks,)),
-        ],
-        compiler_params=pltpu.CompilerParams(vmem_limit_bytes=WHOLE_VMEM),
+        out_shape=jax.ShapeDtypeStruct((targets, hidden.shape[2] // targets, weight.shape[2]), BF16),
+        in_specs=[vmem, vmem],
+        out_specs=vmem,
+        compiler_params=pltpu.CompilerParams(vmem_limit_bytes=20 * MIB),
     )(hidden, weight)
 
 
@@ -459,11 +422,6 @@
 
 def after(value, earlier):
     return lax.optimization_barrier((value, earlier))[0]
-
-
-def shifted_by(value, axis, step):
-    count = lax.axis_size(axis)
-    return lax.ppermute(value, axis, [(i, (i + step) % count) for i in range(count)])
 
 
 def exchange(value, axis):
@@ -506,8 +464,7 @@
         shifted[:, None] == jnp.arange(vocab_local, dtype=jnp.int32)[None, :]
     ).astype(BF16)
     looked_up = jnp.dot(one_hot, embed_table, preferred_element_type=F32).astype(BF16)
-    own, own_level = own_part(queries[0], suffix_kv[:, 0], draft_kv[:, 0], slopes, suffix_len)
-    gathered, looked_up, own = lax.optimization_barrier((gathered, looked_up, own))
+    gathered, looked_up = lax.optimization_barrier((gathered, looked_up))
 
     offset = (prompt_local * (ctx_count - ctx_index)).astype(jnp.int32).reshape(1)
     parts = prompt_part(
@@ -518,18 +475,27 @@
         looked_up.T,
         ctx_count,
     )
+    own, own_level = own_part(
+        after(queries[0], parts), suffix_kv[:, 0], draft_kv[:, 0], slopes, suffix_len
+    )
     parts = exchange(parts, "ctx")
     attended = exchange(merge_parts(parts, own, own_level, heads, req_count), "req")
 
     pieces = exchange(project_rows(attended, out_all, parts, mp_count), ("req", "mp"))
-    residual, sums = residual_rows(pieces, mp_count, draft)
-    sums = [sums] + [shifted_by(sums, "mp", step) for step in range(1, mp_count)]
-    normed = exchange(norm_rows(residual, sums, ln_gain, quarter * mp_count, req_count), "req")
-
-    lifted = exchange(
-        lift_rows(normed.reshape(req_count * draft, quarter), up_all, mp_count), "mp"
-    )
-    activated = exchange(activate(lifted), "mp")
+    residual, centred = residual_rows(
+        pieces, ln_gain, mp_count, draft, out_weight.shape[1], req_count
+    )
+    centred, up_all = lax.optimization_barrier((centred, up_all))
+    centred = exchange(centred, "req").reshape(req_count * draft, -1)
+
+    lifted = exchange(lift_rows(centred, up_all, mp_count), "mp")
+    activated, down_all = lax.optimization_barrier(
+        (
+            activate(lifted, ctx_count // mp_count * up_weight.shape[1], quarter * mp_count),
+            down_all,
+        )
+    )
+    activated = exchange(activated, "mp")
     lowered = exchange(lower_rows(activated, down_all, req_count), "req")
     layer_out = finish(lowered, residual)
     return residual[None], layer_out[None]

time: 185 us -> 180 us (0.973)
  Pallas kernels: 38.6 us -> 22.4 us
  waiting for transfers between devices: 10.4 us -> 21.2 us
  local copies, waits for them, and re-layouts: 4.83 us -> 14.9 us
  blocking collectives: 94.1 us -> 84.2 us
    unnamed x24 -> x26, local copies, waits for them, and re-layouts: 2.6 us -> 12.6 us
    all_to_all x6 -> x5, blocking collectives: 94.1 us -> 84.2 us  [exchange(): return lax.all_to_all(value, axis, split_axis=0, concat_axis=0, tiled=True)]
    all_to_all x2 -> x3, waiting for transfers between devices: 6.28 us -> 15.7 us  [exchange(): return lax.all_to_all(value, axis, split_axis=0, concat_axis=0, tiled=True)]
    pallas_call x1, Pallas kernels: 7.5 us -> 1.81 us  [lift_rows(): pl.pallas_call(lift_kernel, out_shape=jax.ShapeDtypeStruct((mp, blocks //...]
    pallas_call x1, Pallas kernels: 11.9 us -> 6.79 us  [prompt_part(): pl.pallas_call(functools.partial(prompt_kernel, heads=heads, head_size=wi...]
    all_to_all x2 -> x3, starting transfers between devices: 9.37 us -> 14.3 us  [exchange(): return lax.all_to_all(value, axis, split_axis=0, concat_axis=0, tiled=True)]
    ppermute x3 -> x0, starting transfers between devices: 4.8 us -> none  [shifted_by(): lax.ppermute(value, axis, [(i, (i + step) % count) for i in range(count)])]
    all_gather x1, waiting for transfers between devices: 0.01 us -> 4.03 us  [per_device(): down_all = lax.all_gather(after(down_weight, copies), 'ctx')]
  transfers between devices with their start and end apart: 8 -> 6, of which waited for: 3 -> 3; matrix products, arithmetic and copies ran while one was open for 5% -> 5% of each run, Pallas kernels for 17% -> 11%
where the time goes in v4:
time: 180 us; the launch traced here: 179 us
  blocking collectives  84.2 us (47%)
  Pallas kernels  22.4 us (12%)
  waiting for transfers between devices  21.2 us (12%)
  local copies, waits for them, and re-layouts  14.9 us (8%)
  between operations  14.5 us (8%)
  starting transfers between devices  14.4 us (8%)
  matrix products  6.59 us (4%)
    all_to_all x5, blocking collectives, exchange(): return lax.all_to_all(value, axis, split_axis=0, concat_axis=0, tiled=True)  84.2 us
    all_to_all x3, waiting for transfers between devices, exchange(): return lax.all_to_all(value, axis, split_axis=0, concat_axis=0, tiled=True)  15.7 us
    all_to_all x3, starting transfers between devices, exchange(): return lax.all_to_all(value, axis, split_axis=0, concat_axis=0, tiled=True)  14.3 us
    unnamed x26, local copies, waits for them, and re-layouts  12.6 us
    pallas_call x1, Pallas kernels, prompt_part(): pl.pallas_call(functools.partial(prompt_kernel, heads=heads, head_size=wi...  6.79 us
    dot_general x1, matrix products, per_device(): jnp.dot(one_hot, embed_table, preferred_element_type=F32).astype(BF16)  6.59 us
    all_gather x1, waiting for transfers between devices, per_device(): down_all = lax.all_gather(after(down_weight, copies), 'ctx')  4.03 us
  transfers between devices with their start and end apart: 6, of which 3 were waited for; matrix products, arithmetic and copies ran while one was open for 5% of the time, Pallas kernels for 11%

profile of v4, /device:TPU:2, one launch (start us, length us, event | category | flops | bytes accessed | tf_op | source)
XLA Modules:
  0.0 178.9 jit_solution(18281407869787361183)
XLA Ops:
  7.2 0.0 copy-start
  7.2 0.0 all-gather.7.cloned.1.call-start
  7.2 0.7 all-gather.7.cloned.1.call-update
  7.9 0.0 all-gather.9.cloned.1.call-start
  8.0 1.5 broadcast_in_dim.19
  9.4 0.0 all-gather.9.cloned.1.call-update
  9.4 0.0 all-gather.11.cloned.1.call-start
  9.5 0.7 all-gather.11.cloned.1.call-update
  10.2 4.5 %all-to-all-start = ((bf16[8,16,896]{2,1,0:T(8,128)(2,1)}), bf16[8,16,896]{2,1,0:T(8,128)(2,1)S(1)}, u32[]{:S(2)}, u32[]{:S(2)}) async-start(bf16[8,16,896]{2,1,0:T(8,128)(2,1)} %broadcast_in_dim.19), calls=%async_computation | async-start | bytes 458752 | tf_op jit(solution)/shard_map/all_to_all | solution.py:428
  14.7 0.7 broadcast_subtract_fusion
  15.4 0.1 copy.14
  15.5 0.1 sub.19
  15.5 0.0 copy-start.4
  15.6 0.0 copy-start.6
  15.6 6.6 %fusion.2 = bf16[1024,112]{0,1:T(8,128)(2,1)} fusion(bf16[6400,112]{0,1:T(8,128)(2,1)S(1)} %copy-done, s32[1024]{0:T(1024)S(1)} %sub.19), kind=kOutput, calls=%fused_computation.3 | convolution fusion | flops 1474674688 | bytes 1667072 | tf_op jit(solution)/shard_map/dot_general | solution.py:466
  22.2 0.0 all-to-all-done
  22.2 3.2 %copy-done.1 = bf16[2,2048,896]{2,1,0:T(8,128)(2,1)S(1)} copy-done((bf16[2,2048,896]{2,1,0:T(8,128)(2,1)S(1)}, bf16[2,2048,896]{2,1,0:T(8,128)(2,1)}, u32[]{:S(2)}) %copy-start.1) | copy-done | bytes 7340056
  25.4 0.9 copy-done.5
  26.3 6.8 %shard_map.131 = bf16[8,240,128]{2,1,0:T(8,128)(2,1)} custom-call(s32[1]{0:T(128)} %bitcast.offset_ref, f32[8]{0:T(128)S(1)} %copy-done.10, bf16[128,896]{1,0:T(8,128)(2,1)S(1)} %bitcast.19, bf16[112,1024]{1,0:T(8,128)(2,1)S(1)} %bitcast.20, bf16[2,2048,896]{2,1,0:T(8,128)(2,1)S(1)} %copy-done.1), custom_call_target="tpu_custom_call" | custom-call | tf_op jit(solution)/shard_map/pallas_call | solution.py:111
  33.1 4.8 %all-to-all-start.1 = ((bf16[8,240,128]{2,1,0:T(8,128)(2,1)}), bf16[8,240,128]{2,1,0:T(8,128)(2,1)}, u32[]{:S(2)}, u32[]{:S(2)}) async-start(bf16[8,240,128]{2,1,0:T(8,128)(2,1)} %shard_map.131), calls=%async_computation.1 | async-start | bytes 983040 | tf_op jit(solution)/shard_map/all_to_all | solution.py:428
  38.6 0.0 copy-done.4
  38.6 0.0 copy-done.6
  38.6 0.0 copy-start.8
  38.6 0.8 copy-done.8
  39.4 1.6 shard_map.132
  41.0 0.0 copy-start.7
  41.1 0.6 copy-done.7
  41.7 0.6 copy-done.9
  42.3 5.8 %all-to-all-done.1.parts_ref = bf16[8,240,128]{2,1,0:T(8,128)(2,1)} async-done(((bf16[8,240,128]{2,1,0:T(8,128)(2,1)}), bf16[8,240,128]{2,1,0:T(8,128)(2,1)}, u32[]{:S(2)}, u32[]{:S(2)}) %all-to-all-start.1) | async-done | bytes 491552 | tf_op jit(solution)/shard_map/all_to_all | solution.py:428
  48.0 2.1 %shard_map.133 = bf16[8,16,896]{2,1,0:T(8,128)(2,1)} custom-call(bf16[8,240,128]{2,1,0:T(8,128)(2,1)} %all-to-all-done.1.parts_ref, f32[16,896]{1,0:T(8,128)} %copy-done.7, f32[16,128]{1,0:T(8,128)} %copy-done.9), custom_call_target="tpu_custom_call" | custom-call | tf_op jit(solution)/shard_map/pallas_call | solution.py:238
  50.2 19.6 %all_to_all.40.rows_ref = bf16[8,16,896]{2,1,0:T(8,128)(2,1)} all-to-all(bf16[8,16,896]{2,1,0:T(8,128)(2,1)} %shard_map.133), channel_id=1, replica_groups=mesh['ctx'=8,'req'=8,'mp'=4] {'req'}, dimensions={0} | all-to-all | bytes 458752 | tf_op jit(solution)/shard_map/all_to_all | solution.py:428
  69.8 3.3 %shard_map.134 = bf16[32,32,128]{2,1,0:T(8,128)(2,1)} custom-call(bf16[8,16,896]{2,1,0:T(8,128)(2,1)} %all_to_all.40.rows_ref, bf16[8,112,896]{2,1,0:T(8,128)(2,1)} %bitcast.24, bf16[8,240,128]{2,1,0:T(8,128)(2,1)} %all-to-all-done.1.parts_ref), custom_call_target="tpu_custom_call" | custom-call | tf_op jit(solution)/shard_map/pallas_call | solution.py:285
  73.0 5.0 %all-to-all-start.3 = ((bf16[32,32,128]{2,1,0:T(8,128)(2,1)}), bf16[32,32,128]{2,1,0:T(8,128)(2,1)S(1)}, u32[]{:S(2)}, u32[]{:S(2)}) async-start(bf16[32,32,128]{2,1,0:T(8,128)(2,1)} %shard_map.134), calls=%async_computation.3 | async-start | bytes 524288 | tf_op jit(solution)/shard_map/all_to_all | solution.py:428
  78.0 0.6 broadcast_in_dim.20.gain_ref
  78.6 10.0 %all-to-all-done.3.parts_ref = bf16[32,32,128]{2,1,0:T(8,128)(2,1)S(1)} async-done(((bf16[32,32,128]{2,1,0:T(8,128)(2,1)}), bf16[32,32,128]{2,1,0:T(8,128)(2,1)S(1)}, u32[]{:S(2)}, u32[]{:S(2)}) %all-to-all-start.3) | async-done | bytes 262176 | tf_op jit(solution)/shard_map/all_to_all | solution.py:428
  88.6 0.7 copy-done.11
  89.3 2.0 %shard_map.135 = (f32[16,1792]{1,0:T(8,128)}, bf16[8,16,1920]{2,1,0:T(8,128)(2,1)}) custom-call(bf16[32,32,128]{2,1,0:T(8,128)(2,1)} %copy-done.11, f32[1,1792]{1,0:T(1,128)} %broadcast_in_dim.20.gain_ref), custom_call_target="tpu_custom_call" | custom-call | tf_op jit(solution)/shard_map/pallas_call | solution.py:319
  91.3 18.8 %all_to_all.41 = bf16[8,16,1920]{2,1,0:T(8,128)(2,1)S(1)} all-to-all(bf16[8,16,1920]{2,1,0:T(8,128)(2,1)} %get-tuple-element.23), channel_id=1, replica_groups=mesh['ctx'=8,'req'=8,'mp'=4] {'req'}, dimensions={0} | all-to-all | bytes 983040 | tf_op jit(solution)/shard_map/all_to_all | solution.py:428
  110.1 2.9 %copy-done.3 = bf16[1792,1792]{1,0:T(8,128)(2,1)S(1)} copy-done((bf16[1792,1792]{1,0:T(8,128)(2,1)S(1)}, bf16[1792,1792]{1,0:T(8,128)(2,1)}, u32[]{:S(2)}) %copy-start.3) | copy-done | bytes 6422552
  113.1 1.8 %shard_map.136 = bf16[4,464,128]{2,1,0:T(8,128)(2,1)S(1)} custom-call(bf16[128,1920]{1,0:T(8,128)(2,1)S(1)} %bitcast.17, bf16[8,224,1792]{2,1,0:T(8,128)(2,1)S(1)} %bitcast.16), custom_call_target="tpu_custom_call" | custom-call | tf_op jit(solution)/shard_map/pallas_call | solution.py:348
  114.9 11.1 %all_to_all.42.parts_ref = bf16[4,464,128]{2,1,0:T(8,128)(2,1)} all-to-all(bf16[4,464,128]{2,1,0:T(8,128)(2,1)S(1)} %shard_map.136), channel_id=1, replica_groups=mesh['ctx'=8,'req'=8,'mp'=4] {'mp'}, dimensions={0} | all-to-all | bytes 950272 | tf_op jit(solution)/shard_map/all_to_all | solution.py:428
  126.0 1.9 %shard_map.137 = bf16[4,448,128]{2,1,0:T(8,128)(2,1)} custom-call(bf16[4,464,128]{2,1,0:T(8,128)(2,1)} %all_to_all.42.parts_ref), custom_call_target="tpu_custom_call" | custom-call | tf_op jit(solution)/shard_map/pallas_call | solution.py:371
  127.9 4.0 %all-gather.11.cloned.1.call-done = bf16[1792,1792]{1,0:T(8,128)(2,1)} async-done(((bf16[224,1792]{1,0:T(8,128)(2,1)}), bf16[1792,1792]{1,0:T(8,128)(2,1)}) %all-gather.11.cloned.1.call-update) | async-done | bytes 6422544 | tf_op jit(solution)/shard_map/all_gather | solution.py:459
  131.9 12.5 %all_to_all.43.hidden_ref = bf16[4,448,128]{2,1,0:T(8,128)(2,1)S(1)} all-to-all(bf16[4,448,128]{2,1,0:T(8,128)(2,1)} %shard_map.137), channel_id=1, replica_groups=mesh['ctx'=8,'req'=8,'mp'=4] {'mp'}, dimensions={0} | all-to-all | bytes 917504 | tf_op jit(solution)/shard_map/all_to_all | solution.py:428
  144.4 2.8 %copy-done.2 = bf16[1792,1792]{1,0:T(8,128)(2,1)S(1)} copy-done((bf16[1792,1792]{1,0:T(8,128)(2,1)S(1)}, bf16[1792,1792]{1,0:T(8,128)(2,1)}, u32[]{:S(2)}) %copy-start.2) | copy-done | bytes 6422552
  147.3 1.2 shard_map.138
  148.4 22.2 %all_to_all.44.parts_ref = bf16[8,16,1792]{2,1,0:T(8,128)(2,1)} all-to-all(bf16[8,16,1792]{2,1,0:T(8,128)(2,1)S(1)} %shard_map.138), channel_id=1, replica_groups=mesh['ctx'=8,'req'=8,'mp'=4] {'req'}, dimensions={0} | all-to-all | bytes 917504 | tf_op jit(solution)/shard_map/all_to_all | solution.py:428
  170.6 1.7 shard_map.139
  (13 shorter events, 0.0 us)
Async XLA Ops:
  7.2 8.4 %copy-start = (bf16[6400,112]{0,1:T(8,128)(2,1)S(1)}, bf16[6400,112]{0,1:T(8,128)(2,1)}, u32[]{:S(2)}) copy-start(bf16[6400,112]{0,1:T(8,128)(2,1)} %param.13) | copy-start | bytes 4300804
  7.2 62.6 %all-gather.7.cloned.1.call-start = ((), (), s32[]{:S(2)}) async-start(), calls=%async_computation.8 | async-start | bytes 1806336 | tf_op jit(solution)/shard_map/all_gather | solution.py:457
  7.9 83.4 %all-gather.9.cloned.1.call-start = ((), (), s32[]{:S(2)}) async-start(), calls=%async_computation.9 | async-start | bytes 7225344 | tf_op jit(solution)/shard_map/all_gather | solution.py:458
  9.4 122.5 %all-gather.11.cloned.1.call-start = ((), (), s32[]{:S(2)}) async-start(), calls=%async_computation.10 | async-start | bytes 7225344 | tf_op jit(solution)/shard_map/all_gather | solution.py:459
  10.2 12.0 %all-to-all-start = ((bf16[8,16,896]{2,1,0:T(8,128)(2,1)}), bf16[8,16,896]{2,1,0:T(8,128)(2,1)S(1)}, u32[]{:S(2)}, u32[]{:S(2)}) async-start(bf16[8,16,896]{2,1,0:T(8,128)(2,1)} %broadcast_in_dim.19), calls=%async_computation | async-start | bytes 458752 | tf_op jit(solution)/shard_map/all_to_all | solution.py:428
  15.5 6.6 %copy-start.10 = (f32[8]{0:T(128)S(1)}, f32[8]{0:T(128)}, u32[]{:S(2)}) copy-start(f32[8]{0:T(128)} %slopes_ref.3) | copy-start | bytes 100
  15.5 23.0 %copy-start.4 = (bf16[2,1,512,896]{3,2,1,0:T(8,128)(2,1)S(1)}, bf16[2,1,512,896]{3,2,1,0:T(8,128)(2,1)}, u32[]{:S(2)}) copy-start(bf16[2,1,512,896]{3,2,1,0:T(8,128)(2,1)} %param.17) | copy-start | bytes 5505028
  15.6 23.0 %copy-start.6 = (bf16[1,16,896]{2,1,0:T(8,128)(2,1)S(1)}, bf16[1,16,896]{2,1,0:T(8,128)(2,1)}, u32[]{:S(2)}) copy-start(bf16[1,16,896]{2,1,0:T(8,128)(2,1)} %param.14) | copy-start | bytes 86020
  22.2 3.2 %copy-start.1 = (bf16[2,2048,896]{2,1,0:T(8,128)(2,1)S(1)}, bf16[2,2048,896]{2,1,0:T(8,128)(2,1)}, u32[]{:S(2)}) copy-start(bf16[2,2048,896]{2,1,0:T(8,128)(2,1)} %prefix_ref.1) | copy-start | bytes 22020100
  25.4 0.9 copy-start.5
  26.3 51.7 %copy-start.12 = (f32[1792]{0:T(1024)S(1)}, f32[1792]{0:T(1024)}, u32[]{:S(2)}) copy-start(f32[1792]{0:T(1024)} %param.21) | copy-start | bytes 21508
  33.1 14.9 %all-to-all-start.1 = ((bf16[8,240,128]{2,1,0:T(8,128)(2,1)}), bf16[8,240,128]{2,1,0:T(8,128)(2,1)}, u32[]{:S(2)}, u32[]{:S(2)}) async-start(bf16[8,240,128]{2,1,0:T(8,128)(2,1)} %shard_map.131), calls=%async_computation.1 | async-start | bytes 983040 | tf_op jit(solution)/shard_map/all_to_all | solution.py:428
  38.6 0.8 copy-start.8
  41.0 0.6 copy-start.7
  41.7 0.6 copy-start.9
  73.0 15.6 %all-to-all-start.3 = ((bf16[32,32,128]{2,1,0:T(8,128)(2,1)}), bf16[32,32,128]{2,1,0:T(8,128)(2,1)S(1)}, u32[]{:S(2)}, u32[]{:S(2)}) async-start(bf16[32,32,128]{2,1,0:T(8,128)(2,1)} %shard_map.134), calls=%async_computation.3 | async-start | bytes 524288 | tf_op jit(solution)/shard_map/all_to_all | solution.py:428
  88.6 0.7 copy-start.11
  110.1 2.9 %copy-start.3 = (bf16[1792,1792]{1,0:T(8,128)(2,1)S(1)}, bf16[1792,1792]{1,0:T(8,128)(2,1)}, u32[]{:S(2)}) copy-start(bf16[1792,1792]{1,0:T(8,128)(2,1)} %all-gather.9.cloned.1.call-done) | copy-start | bytes 19267588
  144.4 2.8 %copy-start.2 = (bf16[1792,1792]{1,0:T(8,128)(2,1)S(1)}, bf16[1792,1792]{1,0:T(8,128)(2,1)}, u32[]{:S(2)}) copy-start(bf16[1792,1792]{1,0:T(8,128)(2,1)} %all-gather.11.cloned.1.call-done) | copy-start | bytes 19267588
Sparse Core Ops, SparseCore 0:
  9.8 29.8 all-gather.6
  41.6 44.2 all-gather.8
  87.7 44.1 all-gather.10

commit v5 on v4

--- a/solution.py
+++ b/solution.py
@@ -125,6 +125,30 @@
     )(offset, slopes, query_rows, looked_up, prefix_kv)
 
 
+def lookup_kernel(ids_ref, table_ref, out_ref):
+    count = ids_ref.shape[1]
+    features, vocab = table_ref.shape
+    step = math.gcd(vocab, 2 * LANES)
+    ids = ids_ref[...]
+    place = lax.broadcasted_iota(jnp.int32, (step, count), 0)
+    total = jnp.zeros((features, count), F32)
+    for first in range(0, vocab, step):
+        chosen = jnp.where(place == ids - first, 1.0, 0.0).astype(BF16)
+        total += jnp.dot(table_ref[:, first : first + step], chosen, preferred_element_type=F32)
+    out_ref[...] = total.astype(BF16)
+
+
+def look_up(ids, table):
+    vmem = pl.BlockSpec(memory_space=pltpu.VMEM)
+    return pl.pallas_call(
+        lookup_kernel,
+        out_shape=jax.ShapeDtypeStruct((table.shape[0], ids.shape[1]), BF16),
+        in_specs=[vmem, vmem],
+        out_specs=vmem,
+        compiler_params=pltpu.CompilerParams(vmem_limit_bytes=12 * MIB),
+    )(ids, table)
+
+
 def own_kernel(
     length_ref, slopes_ref, query_ref, suffix_ref, draft_ref, out_ref, stats_ref, *, heads, head_size
 ):
@@ -240,6 +264,7 @@
         out_shape=jax.ShapeDtypeStruct((targets, draft, width), BF16),
         in_specs=[vmem, vmem, vmem],
         out_specs=vmem,
+        compiler_params=pltpu.CompilerParams(vmem_limit_bytes=10 * MIB),
     )(parts, own, level)
 
 
@@ -287,6 +312,7 @@
         out_shape=jax.ShapeDtypeStruct((req * mp, blocks // mp * draft, lanes), BF16),
         in_specs=[vmem, vmem, vmem],
         out_specs=vmem,
+        compiler_params=pltpu.CompilerParams(vmem_limit_bytes=10 * MIB),
     )(rows, weight, parts)
 
 
@@ -324,29 +350,33 @@
         ),
         in_specs=[vmem, vmem],
         out_specs=(vmem, vmem),
+        compiler_params=pltpu.CompilerParams(vmem_limit_bytes=10 * MIB),
     )(parts, gain[None, :])
 
 
-def lift_kernel(rows_ref, weight_ref, out_ref):
-    blocks, hidden, width = weight_ref.shape
+def lift_kernel(rows_ref, weight_ref, out_ref, *, hidden):
+    blocks, _, width = weight_ref.shape
     mp, height, _ = out_ref.shape
     pair = blocks // mp
     rows = rows_ref[:, :width]
     for block in range(blocks):
         piece, place = divmod(block, pair)
         out_ref[piece, place * hidden : (place + 1) * hidden] = lax.dot_general(
-            weight_ref[block], rows, (((1,), (1,)), ((), ())), preferred_element_type=F32
+            weight_ref[block, weight_ref.shape[1] - hidden :],
+            rows,
+            (((1,), (1,)), ((), ())),
+            preferred_element_type=F32,
         ).astype(BF16)
     squares = jnp.transpose(rows_ref[:, width:].astype(F32)).astype(BF16)
     for piece in range(mp):
         out_ref[piece, pair * hidden :] = squares[: height - pair * hidden]
 
 
-def lift_rows(rows, weight, mp):
-    blocks, hidden, _ = weight.shape
-    vmem = pl.BlockSpec(memory_space=pltpu.VMEM)
-    return pl.pallas_call(
-        lift_kernel,
+def lift_rows(rows, weight, hidden, mp):
+    blocks = weight.shape[0]
+    vmem = pl.BlockSpec(memory_space=pltpu.VMEM)
+    return pl.pallas_call(
+        functools.partial(lift_kernel, hidden=hidden),
         out_shape=jax.ShapeDtypeStruct((mp, blocks // mp * hidden + 16, rows.shape[0]), BF16),
         in_specs=[vmem, vmem],
         out_specs=vmem,
@@ -373,6 +403,7 @@
         out_shape=jax.ShapeDtypeStruct((parts.shape[0], hidden, parts.shape[2]), BF16),
         in_specs=[vmem],
         out_specs=vmem,
+        compiler_params=pltpu.CompilerParams(vmem_limit_bytes=10 * MIB),
     )(parts)
 
 
@@ -417,6 +448,7 @@
         out_shape=jax.ShapeDtypeStruct(residual.shape, F32),
         in_specs=[vmem, vmem],
         out_specs=vmem,
+        compiler_params=pltpu.CompilerParams(vmem_limit_bytes=10 * MIB),
     )(parts, residual)
 
 
@@ -454,16 +486,17 @@
 
     copies = jnp.broadcast_to(queries, (ctx_count, draft, width))
     gathered = exchange(copies, "ctx")
-    out_all = lax.all_gather(out_weight.T, "ctx")
-    up_all = lax.all_gather(after(up_weight, copies).T, "ctx")
+    columns, hidden = out_weight.shape[1], up_weight.shape[1]
+    upper = -(-columns // 32) * 16
+    first, second = out_weight.T[:upper], out_weight.T[upper:]
+    second = jnp.pad(second, ((0, 2 * upper - columns), (0, 0)))
+    both = jnp.concatenate([jnp.concatenate([first, second], axis=1), up_weight.T], axis=0)
+    both = lax.all_gather(both, "ctx")
     down_all = lax.all_gather(after(down_weight, copies), "ctx")
 
     vocab_local = embed_table.shape[0]
-    shifted = token_ids.reshape(-1) - model_index * vocab_local
-    one_hot = (
-        shifted[:, None] == jnp.arange(vocab_local, dtype=jnp.int32)[None, :]
-    ).astype(BF16)
-    looked_up = jnp.dot(one_hot, embed_table, preferred_element_type=F32).astype(BF16)
+    shifted = token_ids.reshape(1, -1) - model_index * vocab_local
+    looked_up = look_up(shifted, embed_table.T)
     gathered, looked_up = lax.optimization_barrier((gathered, looked_up))
 
     offset = (prompt_local * (ctx_count - ctx_index)).astype(jnp.int32).reshape(1)
@@ -472,7 +505,7 @@
         prefix_kv,
         slopes,
         offset,
-        looked_up.T,
+        looked_up,
         ctx_count,
     )
     own, own_level = own_part(
@@ -481,17 +514,19 @@
     parts = exchange(parts, "ctx")
     attended = exchange(merge_parts(parts, own, own_level, heads, req_count), "req")
 
+    out_all = jnp.concatenate(
+        [both[:, :upper, :width], both[:, : columns - upper, width:]], axis=1
+    )
     pieces = exchange(project_rows(attended, out_all, parts, mp_count), ("req", "mp"))
     residual, centred = residual_rows(
-        pieces, ln_gain, mp_count, draft, out_weight.shape[1], req_count
-    )
-    centred, up_all = lax.optimization_barrier((centred, up_all))
+        pieces, ln_gain, mp_count, draft, columns, req_count
+    )
     centred = exchange(centred, "req").reshape(req_count * draft, -1)
 
-    lifted = exchange(lift_rows(centred, up_all, mp_count), "mp")
+    lifted = exchange(lift_rows(centred, both, hidden, mp_count), "mp")
     activated, down_all = lax.optimization_barrier(
         (
-            activate(lifted, ctx_count // mp_count * up_weight.shape[1], quarter * mp_count),
+            activate(lifted, ctx_count // mp_count * hidden, quarter * mp_count),
             down_all,
         )
     )

time: 180 us -> 171 us (0.950)
  blocking collectives: 84.2 us -> 55.1 us
  waiting for transfers between devices: 21.2 us -> 37.5 us
  starting transfers between devices: 14.4 us -> 26.9 us
  matrix products: 6.59 us -> 0 us
  Pallas kernels: 22.4 us -> 17.1 us
    all_to_all x5 -> x4, blocking collectives: 84.2 us -> 55.1 us  [exchange(): return lax.all_to_all(value, axis, split_axis=0, concat_axis=0, tiled=True)]
    all_to_all x3 -> x4, waiting for transfers between devices: 15.7 us -> 28.4 us  [exchange(): return lax.all_to_all(value, axis, split_axis=0, concat_axis=0, tiled=True)]
    all_to_all x3 -> x4, starting transfers between devices: 14.3 us -> 26.9 us  [exchange(): return lax.all_to_all(value, axis, split_axis=0, concat_axis=0, tiled=True)]
    all_gather x2 -> x1, waiting for transfers between devices: 0.01 us -> 9.02 us  [per_device(): both = lax.all_gather(both, 'ctx')]
    dot_general x1 -> x0, matrix products: 6.59 us -> none  [per_device(): jnp.dot(one_hot, embed_table, preferred_element_type=F32).astype(BF16)]
    slice x0 -> x4, local copies, waits for them, and re-layouts: none -> 4.24 us  [the longest x2 1.81 us: per_device(): first, second = (out_weight.T[:upper], out_weight.T[upper:])]
    all_gather x1, waiting for transfers between devices: 4.03 us -> 0.02 us  [per_device(): down_all = lax.all_gather(after(down_weight, copies), 'ctx')]
    concatenate x0 -> x2, other arithmetic: none -> 2.45 us  [the longest x1 2.32 us: per_device(): jnp.concatenate([jnp.concatenate([first, second], axis=1), up_weight.T],...]
  transfers between devices with their start and end apart: 6 -> 6, of which waited for: 3 -> 4; matrix products, arithmetic and copies ran while one was open for 5% -> 2% of each run, Pallas kernels for 11% -> 9%
where the time goes in v5:
time: 171 us; the launch traced here: 170 us
  blocking collectives  55.1 us (32%)
  waiting for transfers between devices  37.5 us (22%)
  starting transfers between devices  26.9 us (16%)
  Pallas kernels  17.1 us (10%)
  local copies, waits for them, and re-layouts  16.3 us (10%)
  between operations  14.9 us (9%)
  other arithmetic  2.45 us (1%)
    all_to_all x4, blocking collectives, exchange(): return lax.all_to_all(value, axis, split_axis=0, concat_axis=0, tiled=True)  55.1 us
    all_to_all x4, waiting for transfers between devices, exchange(): return lax.all_to_all(value, axis, split_axis=0, concat_axis=0, tiled=True)  28.4 us
    all_to_all x4, starting transfers between devices, exchange(): return lax.all_to_all(value, axis, split_axis=0, concat_axis=0, tiled=True)  26.9 us
    unnamed x22, local copies, waits for them, and re-layouts  11.2 us
    all_gather x1, waiting for transfers between devices, per_device(): both = lax.all_gather(both, 'ctx')  9.02 us
    pallas_call x1, Pallas kernels, prompt_part(): pl.pallas_call(functools.partial(prompt_kernel, heads=heads, head_size=wi...  6.39 us
  transfers between devices with their start and end apart: 6, of which 4 were waited for; matrix products, arithmetic and copies ran while one was open for 2% of the time, Pallas kernels for 9%

profile of v5, /device:TPU:2, one launch (start us, length us, event | category | flops | bytes accessed | tf_op | source)
XLA Modules:
  0.0 170.2 jit_solution(7785132444909605383)
XLA Ops:
  7.2 0.0 copy-start.5
  7.2 0.0 all-gather.5.cloned.1.call-start
  7.2 0.9 slice.16
  8.1 0.9 slice.17
  9.0 0.0 copy-start.4
  9.1 2.3 %fusion.4 = bf16[288,1792]{1,0:T(8,128)(2,1)} fusion(bf16[48,896]{1,0:T(8,128)(2,1)S(1)} %slice.17, bf16[224,1792]{1,0:T(8,128)(2,1)} %bitcast.25, bf16[64,896]{1,0:T(8,128)(2,1)S(1)} %slice.16), kind=kLoop, calls=%fused_computation.7 | loop fusion | flops 5677056 | bytes 2035712 | tf_op jit(solution)/shard_map/concatenate | solution.py:493
  11.4 0.0 all-gather.5.cloned.1.call-update
  11.4 0.0 all-gather.7.cloned.1.call-start
  11.4 0.0 copy-done.5
  11.5 0.7 broadcast_in_dim.17
  12.2 0.0 all-gather.7.cloned.1.call-update
  12.2 4.5 %all-to-all-start = ((bf16[8,16,896]{2,1,0:T(8,128)(2,1)}), bf16[8,16,896]{2,1,0:T(8,128)(2,1)S(1)}, u32[]{:S(2)}, u32[]{:S(2)}) async-start(bf16[8,16,896]{2,1,0:T(8,128)(2,1)} %broadcast_in_dim.17), calls=%async_computation | async-start | bytes 458752 | tf_op jit(solution)/shard_map/all_to_all | solution.py:460
  16.7 0.1 copy.15
  16.8 0.1 sub.14.ids_ref
  16.9 1.9 %shard_map.131.looked_ref = bf16[112,1024]{1,0:T(8,128)(2,1)S(1)} custom-call(s32[1,1024]{1,0:T(1,128)S(1)} %sub.14.ids_ref, bf16[112,6400]{1,0:T(8,128)(2,1)S(1)} %bitcast.19), custom_call_target="tpu_custom_call" | custom-call | tf_op jit(solution)/shard_map/pallas_call | solution.py:143
  18.7 5.1 %all-to-all-done = bf16[8,16,896]{2,1,0:T(8,128)(2,1)S(1)} async-done(((bf16[8,16,896]{2,1,0:T(8,128)(2,1)}), bf16[8,16,896]{2,1,0:T(8,128)(2,1)S(1)}, u32[]{:S(2)}, u32[]{:S(2)}) %all-to-all-start) | async-done | bytes 229408 | tf_op jit(solution)/shard_map/all_to_all | solution.py:460
  23.8 0.0 copy-done.8
  23.9 3.5 %copy-done.1 = bf16[2,2048,896]{2,1,0:T(8,128)(2,1)S(1)} copy-done((bf16[2,2048,896]{2,1,0:T(8,128)(2,1)S(1)}, bf16[2,2048,896]{2,1,0:T(8,128)(2,1)}, u32[]{:S(2)}) %copy-start.1) | copy-done | bytes 7340056
  27.3 6.4 %shard_map.132 = bf16[8,240,128]{2,1,0:T(8,128)(2,1)} custom-call(s32[1]{0:T(128)} %bitcast.offset_ref, f32[8]{0:T(128)S(1)} %copy-done.8, bf16[128,896]{1,0:T(8,128)(2,1)S(1)} %bitcast.20, bf16[112,1024]{1,0:T(8,128)(2,1)S(1)} %shard_map.131.looked_ref, bf16[2,2048,896]{2,1,0:T(8,128)(2,1)S(1)} %copy-done.1), custom_call_target="tpu_custom_call" | custom-call | tf_op jit(solution)/shard_map/pallas_call | solution.py:111
  33.7 3.5 %all-to-all-start.1 = ((bf16[8,240,128]{2,1,0:T(8,128)(2,1)}), bf16[8,240,128]{2,1,0:T(8,128)(2,1)S(1)}, u32[]{:S(2)}, u32[]{:S(2)}) async-start(bf16[8,240,128]{2,1,0:T(8,128)(2,1)} %shard_map.132), calls=%async_computation.1 | async-start | bytes 983040 | tf_op jit(solution)/shard_map/all_to_all | solution.py:460
  37.9 0.0 copy-start.3
  37.9 1.5 copy-done.3
  39.4 1.6 shard_map.133
  41.0 11.7 %all-to-all-done.1.parts_ref = bf16[8,240,128]{2,1,0:T(8,128)(2,1)S(1)} async-done(((bf16[8,240,128]{2,1,0:T(8,128)(2,1)}), bf16[8,240,128]{2,1,0:T(8,128)(2,1)S(1)}, u32[]{:S(2)}, u32[]{:S(2)}) %all-to-all-start.1) | async-done | bytes 491552 | tf_op jit(solution)/shard_map/all_to_all | solution.py:460
  52.7 1.0 shard_map.134
  53.7 8.7 %all-to-all-start.2 = ((bf16[8,16,896]{2,1,0:T(8,128)(2,1)}), bf16[8,16,896]{2,1,0:T(8,128)(2,1)S(1)}, u32[]{:S(2)}, u32[]{:S(2)}) async-start(bf16[8,16,896]{2,1,0:T(8,128)(2,1)} %shard_map.134), calls=%async_computation.2 | async-start | bytes 458752 | tf_op jit(solution)/shard_map/all_to_all | solution.py:460
  62.5 9.0 %all-gather.5.cloned.1.call-done = bf16[2304,1792]{1,0:T(8,128)(2,1)} async-done(((bf16[288,1792]{1,0:T(8,128)(2,1)}), bf16[2304,1792]{1,0:T(8,128)(2,1)}) %all-gather.5.cloned.1.call-update) | async-done | bytes 8257552 | tf_op jit(solution)/shard_map/all_gather | solution.py:494
  71.5 1.3 slice.18
  72.8 1.2 slice.19
  73.9 0.1 pad_maximum_fusion.weight_ref
  74.1 0.0 copy-start.10
  74.1 0.0 all-to-all-done.2.rows_ref
  74.1 1.6 shard_map.135
  75.7 10.2 %all-to-all-start.3 = ((bf16[32,32,128]{2,1,0:T(8,128)(2,1)}), bf16[32,32,128]{2,1,0:T(8,128)(2,1)S(1)}, u32[]{:S(2)}, u32[]{:S(2)}) async-start(bf16[32,32,128]{2,1,0:T(8,128)(2,1)} %shard_map.135), calls=%async_computation.3 | async-start | bytes 524288 | tf_op jit(solution)/shard_map/all_to_all | solution.py:460
  85.8 0.0 copy-done.10
  85.8 11.6 %all-to-all-done.3.parts_ref = bf16[32,32,128]{2,1,0:T(8,128)(2,1)S(1)} async-done(((bf16[32,32,128]{2,1,0:T(8,128)(2,1)}), bf16[32,32,128]{2,1,0:T(8,128)(2,1)S(1)}, u32[]{:S(2)}, u32[]{:S(2)}) %all-to-all-start.3) | async-done | bytes 262176 | tf_op jit(solution)/shard_map/all_to_all | solution.py:460
  97.5 0.8 shard_map.136
  98.3 18.5 %all_to_all.40 = bf16[8,16,1920]{2,1,0:T(8,128)(2,1)S(1)} all-to-all(bf16[8,16,1920]{2,1,0:T(8,128)(2,1)S(1)} %get-tuple-element.18), channel_id=1, replica_groups=mesh['ctx'=8,'req'=8,'mp'=4] {'req'}, dimensions={0} | all-to-all | bytes 983040 | tf_op jit(solution)/shard_map/all_to_all | solution.py:460
  116.8 3.3 %copy-done = bf16[2304,1792]{1,0:T(8,128)(2,1)S(1)} copy-done((bf16[2304,1792]{1,0:T(8,128)(2,1)S(1)}, bf16[2304,1792]{1,0:T(8,128)(2,1)}, u32[]{:S(2)}) %copy-start) | copy-done | bytes 8257560
  120.1 1.8 %shard_map.137 = bf16[4,464,128]{2,1,0:T(8,128)(2,1)S(1)} custom-call(bf16[128,1920]{1,0:T(8,128)(2,1)S(1)} %bitcast.17, bf16[8,288,1792]{2,1,0:T(8,128)(2,1)S(1)} %bitcast.15), custom_call_target="tpu_custom_call" | custom-call | tf_op jit(solution)/shard_map/pallas_call | solution.py:378
  122.0 10.9 %all_to_all.41.parts_ref = bf16[4,464,128]{2,1,0:T(8,128)(2,1)S(1)} all-to-all(bf16[4,464,128]{2,1,0:T(8,128)(2,1)S(1)} %shard_map.137), channel_id=1, replica_groups=mesh['ctx'=8,'req'=8,'mp'=4] {'mp'}, dimensions={0} | all-to-all | bytes 950272 | tf_op jit(solution)/shard_map/all_to_all | solution.py:460
  132.9 0.1 shard_map.138
  133.0 0.0 all-gather.7.cloned.1.call-done
  133.0 10.1 %all_to_all.42.hidden_ref = bf16[4,448,128]{2,1,0:T(8,128)(2,1)S(1)} all-to-all(bf16[4,448,128]{2,1,0:T(8,128)(2,1)S(1)} %shard_map.138), channel_id=1, replica_groups=mesh['ctx'=8,'req'=8,'mp'=4] {'mp'}, dimensions={0} | all-to-all | bytes 917504 | tf_op jit(solution)/shard_map/all_to_all | solution.py:460
  143.1 2.8 %copy-done.2 = bf16[1792,1792]{1,0:T(8,128)(2,1)S(1)} copy-done((bf16[1792,1792]{1,0:T(8,128)(2,1)S(1)}, bf16[1792,1792]{1,0:T(8,128)(2,1)}, u32[]{:S(2)}) %copy-start.2) | copy-done | bytes 6422552
  146.0 1.2 shard_map.139
  147.1 15.5 %all_to_all.43.parts_ref = bf16[8,16,1792]{2,1,0:T(8,128)(2,1)S(1)} all-to-all(bf16[8,16,1792]{2,1,0:T(8,128)(2,1)S(1)} %shard_map.139), channel_id=1, replica_groups=mesh['ctx'=8,'req'=8,'mp'=4] {'req'}, dimensions={0} | all-to-all | bytes 917504 | tf_op jit(solution)/shard_map/all_to_all | solution.py:460
  162.7 0.7 shard_map.140
  (13 shorter events, 0.0 us)
Async XLA Ops:
  7.2 4.3 %copy-start.5 = (bf16[1,16,896]{2,1,0:T(8,128)(2,1)S(1)}, bf16[1,16,896]{2,1,0:T(8,128)(2,1)}, u32[]{:S(2)}) copy-start(bf16[1,16,896]{2,1,0:T(8,128)(2,1)} %param.14) | copy-start | bytes 86020
  7.2 64.3 %all-gather.5.cloned.1.call-start = ((), (), s32[]{:S(2)}) async-start(), calls=%async_computation.8 | async-start | bytes 9289728 | tf_op jit(solution)/shard_map/all_gather | solution.py:494
  9.0 7.6 %copy-start.9 = (s32[64,16]{0,1:T(8,128)S(1)}, s32[64,16]{0,1:T(8,128)}, u32[]{:S(2)}) copy-start(s32[64,16]{0,1:T(8,128)} %param.12) | copy-start | bytes 12292
  9.0 7.8 %copy-start.4 = (bf16[6400,112]{0,1:T(8,128)(2,1)S(1)}, bf16[6400,112]{0,1:T(8,128)(2,1)}, u32[]{:S(2)}) copy-start(bf16[6400,112]{0,1:T(8,128)(2,1)} %param.13) | copy-start | bytes 4300804
  11.4 12.5 %copy-start.8 = (f32[8]{0:T(128)S(1)}, f32[8]{0:T(128)}, u32[]{:S(2)}) copy-start(f32[8]{0:T(128)} %slopes_ref.3) | copy-start | bytes 100
  11.4 121.6 %all-gather.7.cloned.1.call-start = ((), (), s32[]{:S(2)}) async-start(), calls=%async_computation.9 | async-start | bytes 7225344 | tf_op jit(solution)/shard_map/all_gather | solution.py:495
  12.2 11.7 %all-to-all-start = ((bf16[8,16,896]{2,1,0:T(8,128)(2,1)}), bf16[8,16,896]{2,1,0:T(8,128)(2,1)S(1)}, u32[]{:S(2)}, u32[]{:S(2)}) async-start(bf16[8,16,896]{2,1,0:T(8,128)(2,1)} %broadcast_in_dim.17), calls=%async_computation | async-start | bytes 458752 | tf_op jit(solution)/shard_map/all_to_all | solution.py:460
  23.9 3.5 %copy-start.1 = (bf16[2,2048,896]{2,1,0:T(8,128)(2,1)S(1)}, bf16[2,2048,896]{2,1,0:T(8,128)(2,1)}, u32[]{:S(2)}) copy-start(bf16[2,2048,896]{2,1,0:T(8,128)(2,1)} %prefix_ref.1) | copy-start | bytes 22020100
  27.3 10.5 %copy-start.7 = (bf16[2,1,16,896]{3,2,1,0:T(8,128)(2,1)S(1)}, bf16[2,1,16,896]{3,2,1,0:T(8,128)(2,1)}, u32[]{:S(2)}) copy-start(bf16[2,1,16,896]{3,2,1,0:T(8,128)(2,1)} %param.15) | copy-start | bytes 172036
  33.7 19.0 %all-to-all-start.1 = ((bf16[8,240,128]{2,1,0:T(8,128)(2,1)}), bf16[8,240,128]{2,1,0:T(8,128)(2,1)S(1)}, u32[]{:S(2)}, u32[]{:S(2)}) async-start(bf16[8,240,128]{2,1,0:T(8,128)(2,1)} %shard_map.132), calls=%async_computation.1 | async-start | bytes 983040 | tf_op jit(solution)/shard_map/all_to_all | solution.py:460
  37.9 1.5 copy-start.3
  53.7 20.3 %all-to-all-start.2 = ((bf16[8,16,896]{2,1,0:T(8,128)(2,1)}), bf16[8,16,896]{2,1,0:T(8,128)(2,1)S(1)}, u32[]{:S(2)}, u32[]{:S(2)}) async-start(bf16[8,16,896]{2,1,0:T(8,128)(2,1)} %shard_map.134), calls=%async_computation.2 | async-start | bytes 458752 | tf_op jit(solution)/shard_map/all_to_all | solution.py:460
  74.1 11.7 %copy-start.10 = (f32[1792]{0:T(1024)S(1)}, f32[1792]{0:T(1024)}, u32[]{:S(2)}) copy-start(f32[1792]{0:T(1024)} %param.21) | copy-start | bytes 21508
  75.7 21.8 %all-to-all-start.3 = ((bf16[32,32,128]{2,1,0:T(8,128)(2,1)}), bf16[32,32,128]{2,1,0:T(8,128)(2,1)S(1)}, u32[]{:S(2)}, u32[]{:S(2)}) async-start(bf16[32,32,128]{2,1,0:T(8,128)(2,1)} %shard_map.135), calls=%async_computation.3 | async-start | bytes 524288 | tf_op jit(solution)/shard_map/all_to_all | solution.py:460
  116.8 3.3 %copy-start = (bf16[2304,1792]{1,0:T(8,128)(2,1)S(1)}, bf16[2304,1792]{1,0:T(8,128)(2,1)}, u32[]{:S(2)}) copy-start(bf16[2304,1792]{1,0:T(8,128)(2,1)} %all-gather.5.cloned.1.call-done) | copy-start | bytes 24772612
  143.1 2.8 %copy-start.2 = (bf16[1792,1792]{1,0:T(8,128)(2,1)S(1)}, bf16[1792,1792]{1,0:T(8,128)(2,1)}, u32[]{:S(2)}) copy-start(bf16[1792,1792]{1,0:T(8,128)(2,1)} %all-gather.7.cloned.1.call-done) | copy-start | bytes 19267588
  146.0 16.7 %copy-start.6 = (f32[16,1792]{1,0:T(8,128)S(1)}, f32[16,1792]{1,0:T(8,128)}, u32[]{:S(2)}) copy-start(f32[16,1792]{1,0:T(8,128)} %get-tuple-element.17.residual_ref) | copy-start | bytes 344068
Sparse Core Ops, SparseCore 0:
  11.5 59.9 all-gather.4
  73.3 44.2 all-gather.6

commit v6 on v5

--- a/solution.py
+++ b/solution.py
@@ -276,56 +276,54 @@
     return packed.astype(BF16)
 
 
-def project_kernel(rows_ref, weight_ref, parts_ref, out_ref):
-    blocks, columns, _ = weight_ref.shape
-    targets, held, lanes = out_ref.shape
-    req, draft, width = rows_ref.shape
-    mp = targets // req
-    pair = held // draft
+def project_kernel(ctx_ref, rows_ref, parts_ref, *refs, mp):
+    *weight_refs, out_ref = refs
+    columns = weight_refs[0].shape[0]
+    blocks = len(weight_refs)
+    _, pair, draft, lanes = out_ref.shape
+    req, _, width = rows_ref.shape
     rows = rows_ref[...].reshape(req * draft, width)
     products = []
-    for block in range(blocks):
+    for place, weight_ref in enumerate(weight_refs):
+        beside, back = divmod(place, blocks // pair)
+        block = lax.rem(ctx_ref[0] + blocks - pair * back, blocks) ^ beside
         product = lax.dot_general(
-            rows, weight_ref[block], (((1,), (1,)), ((), ())), preferred_element_type=F32
+            rows, weight_ref[...], (((1,), (1,)), ((), ())), preferred_element_type=F32
         )
         looked_up = parts_ref[block, parts_ref.shape[1] - columns :].astype(F32)
-        products.append(product + jnp.transpose(looked_up))
-    sums = packed_sums(
-        jnp.sum(functools.reduce(jnp.add, products), axis=1, keepdims=True), lanes - columns
-    )
-    for block, product in enumerate(products):
+        products.append((block, product + jnp.transpose(looked_up)))
+    total = functools.reduce(jnp.add, [product for _, product in products])
+    sums = packed_sums(jnp.sum(total, axis=1, keepdims=True), lanes - columns)
+    for block, product in products:
         product = jnp.concatenate([product.astype(BF16), sums], axis=1)
-        piece, half = divmod(block, pair)
+        piece, half = lax.shift_right_logical(block, 1), block & 1
         for target in range(req):
-            out_ref[target * mp + piece, half * draft : (half + 1) * draft] = product[
-                target * draft : (target + 1) * draft
-            ]
-
-
-def project_rows(rows, weight, parts, mp):
+            out_ref[target * mp + piece, half] = product[target * draft : (target + 1) * draft]
+
+
+def project_rows(rows, weights, parts, ctx_index, mp):
     req, draft, _ = rows.shape
-    blocks, columns, _ = weight.shape
+    columns = weights[0].shape[0]
     lanes = -(-(columns + 3) // LANES) * LANES
     vmem = pl.BlockSpec(memory_space=pltpu.VMEM)
     return pl.pallas_call(
-        project_kernel,
-        out_shape=jax.ShapeDtypeStruct((req * mp, blocks // mp * draft, lanes), BF16),
-        in_specs=[vmem, vmem, vmem],
+        functools.partial(project_kernel, mp=mp),
+        out_shape=jax.ShapeDtypeStruct((req * mp, len(weights) // mp, draft, lanes), BF16),
+        in_specs=[pl.BlockSpec(memory_space=pltpu.SMEM)] + [vmem] * (2 + len(weights)),
         out_specs=vmem,
         compiler_params=pltpu.CompilerParams(vmem_limit_bytes=10 * MIB),
-    )(rows, weight, parts)
+    )(ctx_index, rows, parts, *weights)
 
 
 def residual_kernel(parts_ref, gain_ref, out_ref, centred_ref, *, mp, columns):
-    sources, held, _ = parts_ref.shape
-    draft, width = out_ref.shape
+    sources, pair, _, _ = parts_ref.shape
+    _, width = out_ref.shape
     blocks = []
-    for half in range(held // draft):
-        lines = slice(half * draft, (half + 1) * draft)
+    for half in range(pair):
         for source in range(sources // mp):
-            block = parts_ref[source * mp, lines].astype(F32)
+            block = parts_ref[source * mp, half].astype(F32)
             for piece in range(1, mp):
-                block += parts_ref[source * mp + piece, lines].astype(F32)
+                block += parts_ref[source * mp + piece, half].astype(F32)
             blocks.append(block)
     residual = jnp.concatenate([block[:, :columns] for block in blocks], axis=1)
     out_ref[...] = residual
@@ -486,18 +484,19 @@
 
     copies = jnp.broadcast_to(queries, (ctx_count, draft, width))
     gathered = exchange(copies, "ctx")
-    columns, hidden = out_weight.shape[1], up_weight.shape[1]
-    upper = -(-columns // 32) * 16
-    first, second = out_weight.T[:upper], out_weight.T[upper:]
-    second = jnp.pad(second, ((0, 2 * upper - columns), (0, 0)))
-    both = jnp.concatenate([jnp.concatenate([first, second], axis=1), up_weight.T], axis=0)
-    both = lax.all_gather(both, "ctx")
+    up_all = lax.all_gather(after(up_weight, copies).T, "ctx")
     down_all = lax.all_gather(after(down_weight, copies), "ctx")
 
     vocab_local = embed_table.shape[0]
     shifted = token_ids.reshape(1, -1) - model_index * vocab_local
     looked_up = look_up(shifted, embed_table.T)
     gathered, looked_up = lax.optimization_barrier((gathered, looked_up))
+
+    out_blocks = [after(out_weight.T, looked_up)]
+    out_blocks += [
+        lax.ppermute(out_blocks[0], "ctx", [(i, (i + step) % ctx_count) for i in range(ctx_count)])
+        for step in range(2, ctx_count, 2)
+    ]
 
     offset = (prompt_local * (ctx_count - ctx_index)).astype(jnp.int32).reshape(1)
     parts = prompt_part(
@@ -512,24 +511,26 @@
         after(queries[0], parts), suffix_kv[:, 0], draft_kv[:, 0], slopes, suffix_len
     )
     parts = exchange(parts, "ctx")
+    out_blocks += [
+        lax.ppermute(after(block, own), "ctx", [(i, i ^ 1) for i in range(ctx_count)])
+        for block in out_blocks
+    ]
     attended = exchange(merge_parts(parts, own, own_level, heads, req_count), "req")
 
-    out_all = jnp.concatenate(
-        [both[:, :upper, :width], both[:, : columns - upper, width:]], axis=1
-    )
-    pieces = exchange(project_rows(attended, out_all, parts, mp_count), ("req", "mp"))
+    pieces = exchange(
+        project_rows(
+            attended, out_blocks, parts, ctx_index.astype(jnp.int32).reshape(1), mp_count
+        ),
+        ("req", "mp"),
+    )
     residual, centred = residual_rows(
-        pieces, ln_gain, mp_count, draft, columns, req_count
+        pieces, ln_gain, mp_count, draft, out_weight.shape[1], req_count
     )
     centred = exchange(centred, "req").reshape(req_count * draft, -1)
 
-    lifted = exchange(lift_rows(centred, both, hidden, mp_count), "mp")
-    activated, down_all = lax.optimization_barrier(
-        (
-            activate(lifted, ctx_count // mp_count * hidden, quarter * mp_count),
-            down_all,
-        )
-    )
+    hidden = up_weight.shape[1]
+    lifted = exchange(lift_rows(centred, up_all, hidden, mp_count), "mp")
+    activated = activate(lifted, ctx_count // mp_count * hidden, quarter * mp_count)
     activated = exchange(activated, "mp")
     lowered = exchange(lower_rows(activated, down_all, req_count), "req")
     layer_out = finish(lowered, residual)

time: 171 us -> 169 us (0.988)
  starting transfers between devices: 26.9 us -> 38.5 us
  blocking collectives: 55.1 us -> 45 us
  local copies, waits for them, and re-layouts: 16.3 us -> 12.5 us
  other arithmetic: 2.45 us -> 0.7 us
    all_to_all x4 -> x3, blocking collectives: 55.1 us -> 45 us  [exchange(): return lax.all_to_all(value, axis, split_axis=0, concat_axis=0, tiled=True)]
    all_gather x1, waiting for transfers between devices: 9.02 us -> 0.01 us  [per_device(): up_all = lax.all_gather(after(up_weight, copies).T, 'ctx')]
    ppermute x0 -> x7, waiting for transfers between devices: none -> 7.78 us  [the longest x3 6.56 us: per_device(): lax.ppermute(out_blocks[0], 'ctx', [(i, (i + step) % ctx_count) for i in...]
    ppermute x0 -> x7, starting transfers between devices: none -> 7.16 us  [the longest x3 6.16 us: per_device(): lax.ppermute(out_blocks[0], 'ctx', [(i, (i + step) % ctx_count) for i in...]
    all_to_all x4 -> x5, starting transfers between devices: 26.9 us -> 31.2 us  [exchange(): return lax.all_to_all(value, axis, split_axis=0, concat_axis=0, tiled=True)]
    slice x4 -> x0, local copies, waits for them, and re-layouts: 4.24 us -> none  [the longest x2 1.81 us: per_device(): first, second = (out_weight.T[:upper], out_weight.T[upper:])]
    concatenate x2 -> x0, other arithmetic: 2.45 us -> none  [the longest x1 2.32 us: per_device(): jnp.concatenate([jnp.concatenate([first, second], axis=1), up_weight.T],...]
    all_to_all x4 -> x5, waiting for transfers between devices: 28.4 us -> 30 us  [exchange(): return lax.all_to_all(value, axis, split_axis=0, concat_axis=0, tiled=True)]
  transfers between devices with their start and end apart: 6 -> 14, of which waited for: 4 -> 8; matrix products, arithmetic and copies ran while one was open for 2% -> 1% of each run, Pallas kernels for 9% -> 10%
where the time goes in v6:
time: 169 us
  blocking collectives  45 us (27%)
  starting transfers between devices  38.5 us (23%)
  waiting for transfers between devices  38.5 us (23%)
  Pallas kernels  18.5 us (11%)
  between operations  14.8 us (9%)
  local copies, waits for them, and re-layouts  12.5 us (7%)
    all_to_all x3, blocking collectives, exchange(): return lax.all_to_all(value, axis, split_axis=0, concat_axis=0, tiled=True)  45 us
    all_to_all x5, starting transfers between devices, exchange(): return lax.all_to_all(value, axis, split_axis=0, concat_axis=0, tiled=True)  31.2 us
    all_to_all x5, waiting for transfers between devices, exchange(): return lax.all_to_all(value, axis, split_axis=0, concat_axis=0, tiled=True)  30 us
    unnamed x24, local copies, waits for them, and re-layouts  10.9 us
    pallas_call x1, Pallas kernels, prompt_part(): pl.pallas_call(functools.partial(prompt_kernel, heads=heads, head_size=wi...  6.79 us
    ppermute x3, waiting for transfers between devices, per_device(): lax.ppermute(out_blocks[0], 'ctx', [(i, (i + step) % ctx_count) for i in...  6.56 us
    ppermute x3, starting transfers between devices, per_device(): lax.ppermute(out_blocks[0], 'ctx', [(i, (i + step) % ctx_count) for i in...  6.16 us
  transfers between devices with their start and end apart: 14, of which 8 were waited for; matrix products, arithmetic and copies ran while one was open for 1% of the time, Pallas kernels for 10%

profile of v6, /device:TPU:2, one launch (start us, length us, event | category | flops | bytes accessed | tf_op | source)
XLA Modules:
  0.0 168.5 jit_solution(1683342257282508671)
XLA Ops:
  7.2 0.0 all-gather.5.cloned.1.call-start
  7.2 1.5 broadcast_in_dim.17
  8.7 0.0 copy-start.10
  8.7 0.0 all-gather.5.cloned.1.call-update
  8.7 0.0 all-gather.7.cloned.1.call-start
  8.8 0.7 all-gather.7.cloned.1.call-update
  9.5 4.5 %all-to-all-start = ((bf16[8,16,896]{2,1,0:T(8,128)(2,1)}), bf16[8,16,896]{2,1,0:T(8,128)(2,1)S(1)}, u32[]{:S(2)}, u32[]{:S(2)}) async-start(bf16[8,16,896]{2,1,0:T(8,128)(2,1)} %broadcast_in_dim.17), calls=%async_computation | async-start | bytes 458752 | tf_op jit(solution)/shard_map/all_to_all | solution.py:458
  14.0 0.7 broadcast_subtract_fusion
  14.7 0.1 copy.15
  14.7 0.1 sub.14.ids_ref
  14.8 1.4 copy-done.4
  16.2 2.0 %shard_map.131.looked_ref = bf16[112,1024]{1,0:T(8,128)(2,1)S(1)} custom-call(s32[1,1024]{1,0:T(1,128)S(1)} %sub.14.ids_ref, bf16[112,6400]{1,0:T(8,128)(2,1)S(1)} %bitcast.18), custom_call_target="tpu_custom_call" | custom-call | tf_op jit(solution)/shard_map/pallas_call | solution.py:143
  18.1 3.0 %all-to-all-done = bf16[8,16,896]{2,1,0:T(8,128)(2,1)S(1)} async-done(((bf16[8,16,896]{2,1,0:T(8,128)(2,1)}), bf16[8,16,896]{2,1,0:T(8,128)(2,1)S(1)}, u32[]{:S(2)}, u32[]{:S(2)}) %all-to-all-start) | async-done | bytes 229408 | tf_op jit(solution)/shard_map/all_to_all | solution.py:458
  21.1 3.1 %copy-done = bf16[2,2048,896]{2,1,0:T(8,128)(2,1)S(1)} copy-done((bf16[2,2048,896]{2,1,0:T(8,128)(2,1)S(1)}, bf16[2,2048,896]{2,1,0:T(8,128)(2,1)}, u32[]{:S(2)}) %copy-start) | copy-done | bytes 7340056
  24.3 0.7 copy-done.9
  24.9 6.8 %shard_map.132 = bf16[8,240,128]{2,1,0:T(8,128)(2,1)} custom-call(s32[1]{0:T(128)} %bitcast.1.offset_ref, f32[8]{0:T(128)S(1)} %copy-done.9, bf16[128,896]{1,0:T(8,128)(2,1)S(1)} %bitcast.19, bf16[112,1024]{1,0:T(8,128)(2,1)S(1)} %shard_map.131.looked_ref, bf16[2,2048,896]{2,1,0:T(8,128)(2,1)S(1)} %copy-done), custom_call_target="tpu_custom_call" | custom-call | tf_op jit(solution)/shard_map/pallas_call | solution.py:111
  31.7 3.5 %all-to-all-start.1 = ((bf16[8,240,128]{2,1,0:T(8,128)(2,1)}), bf16[8,240,128]{2,1,0:T(8,128)(2,1)S(1)}, u32[]{:S(2)}, u32[]{:S(2)}) async-start(bf16[8,240,128]{2,1,0:T(8,128)(2,1)} %shard_map.132), calls=%async_computation.1 | async-start | bytes 983040 | tf_op jit(solution)/shard_map/all_to_all | solution.py:458
  35.9 2.0 %collective-permute-start = (bf16[112,896]{1,0:T(8,128)(2,1)S(1)}, bf16[112,896]{1,0:T(8,128)(2,1)S(1)}, u32[]{:S(2)}, u32[]{:S(2)}) collective-permute-start(bf16[112,896]{1,0:T(8,128)(2,1)S(1)} %bitcast.20), channel_id=1, source_target_pairs={{0,64},{32,96},{64,128},{96,160},{128,192},{160,224},{192,0},{224,... | collective-permute-start | bytes 602120 | tf_op jit(solution)/shard_map/ppermute | solution.py:497
  37.9 2.7 %collective-permute-start.1 = (bf16[112,896]{1,0:T(8,128)(2,1)S(1)}, bf16[112,896]{1,0:T(8,128)(2,1)S(1)}, u32[]{:S(2)}, u32[]{:S(2)}) collective-permute-start(bf16[112,896]{1,0:T(8,128)(2,1)S(1)} %bitcast.21), channel_id=1, source_target_pairs={{0,128},{32,160},{64,192},{96,224},{128,0},{160,32},{192,64},{224,... | collective-permute-start | bytes 602120 | tf_op jit(solution)/shard_map/ppermute | solution.py:497
  40.6 1.4 collective-permute-start.2
  42.0 1.6 shard_map.133
  43.7 7.2 %all-to-all-done.1.parts_ref = bf16[8,240,128]{2,1,0:T(8,128)(2,1)S(1)} async-done(((bf16[8,240,128]{2,1,0:T(8,128)(2,1)}), bf16[8,240,128]{2,1,0:T(8,128)(2,1)S(1)}, u32[]{:S(2)}, u32[]{:S(2)}) %all-to-all-start.1) | async-done | bytes 491552 | tf_op jit(solution)/shard_map/all_to_all | solution.py:458
  50.9 1.1 shard_map.134
  52.0 8.9 %all-to-all-start.2 = ((bf16[8,16,896]{2,1,0:T(8,128)(2,1)}), bf16[8,16,896]{2,1,0:T(8,128)(2,1)S(1)}, u32[]{:S(2)}, u32[]{:S(2)}) async-start(bf16[8,16,896]{2,1,0:T(8,128)(2,1)} %shard_map.134), calls=%async_computation.2 | async-start | bytes 458752 | tf_op jit(solution)/shard_map/all_to_all | solution.py:458
  60.9 0.0 collective-permute-done.refs_1_
  60.9 0.5 collective-permute-start.4
  61.4 6.6 %collective-permute-done.1.refs_2_ = bf16[112,896]{1,0:T(8,128)(2,1)S(1)} collective-permute-done((bf16[112,896]{1,0:T(8,128)(2,1)S(1)}, bf16[112,896]{1,0:T(8,128)(2,1)S(1)}, u32[]{:S(2)}, u32[]{:S(2)}) %collective-permute-start.1) | collective-permute-done | bytes 200736 | tf_op jit(solution)/shard_map/ppermute | solution.py:497
  67.9 0.0 collective-permute-done.2.refs_3_
  67.9 0.5 collective-permute-start.6
  68.4 0.9 collective-permute-done.5.refs_6_
  69.4 0.3 collective-permute-done.6.refs_7_
  69.7 1.9 %all-to-all-done.2.rows_ref = bf16[8,16,896]{2,1,0:T(8,128)(2,1)S(1)} async-done(((bf16[8,16,896]{2,1,0:T(8,128)(2,1)}), bf16[8,16,896]{2,1,0:T(8,128)(2,1)S(1)}, u32[]{:S(2)}, u32[]{:S(2)}) %all-to-all-start.2) | async-done | bytes 229408 | tf_op jit(solution)/shard_map/all_to_all | solution.py:458
  71.6 1.6 shard_map.135
  73.2 9.5 %all-to-all-start.3 = ((bf16[32,2,16,128]{3,2,1,0:T(8,128)(2,1)}), bf16[32,2,16,128]{3,2,1,0:T(8,128)(2,1)S(1)}, u32[]{:S(2)}, u32[]{:S(2)}) async-start(bf16[32,2,16,128]{3,2,1,0:T(8,128)(2,1)} %shard_map.135), calls=%async_computation.3 | async-start | bytes 524288 | tf_op jit(solution)/shard_map/all_to_all | solution.py:458
  82.8 11.6 %all-to-all-done.3.parts_ref = bf16[32,2,16,128]{3,2,1,0:T(8,128)(2,1)S(1)} async-done(((bf16[32,2,16,128]{3,2,1,0:T(8,128)(2,1)}), bf16[32,2,16,128]{3,2,1,0:T(8,128)(2,1)S(1)}, u32[]{:S(2)}, u32[]{:S(2)}) %all-to-all-start.3) | async-done | bytes 262176 | tf_op jit(solution)/shard_map/all_to_all | solution.py:458
  94.4 0.8 shard_map.136
  95.2 18.4 %all_to_all.40 = bf16[8,16,1920]{2,1,0:T(8,128)(2,1)S(1)} all-to-all(bf16[8,16,1920]{2,1,0:T(8,128)(2,1)S(1)} %get-tuple-element.27), channel_id=1, replica_groups=mesh['ctx'=8,'req'=8,'mp'=4] {'req'}, dimensions={0} | all-to-all | bytes 983040 | tf_op jit(solution)/shard_map/all_to_all | solution.py:458
  113.6 2.9 %copy-done.2 = bf16[1792,1792]{1,0:T(8,128)(2,1)S(1)} copy-done((bf16[1792,1792]{1,0:T(8,128)(2,1)S(1)}, bf16[1792,1792]{1,0:T(8,128)(2,1)}, u32[]{:S(2)}) %copy-start.2) | copy-done | bytes 6422552
  116.5 1.8 %shard_map.137 = bf16[4,464,128]{2,1,0:T(8,128)(2,1)S(1)} custom-call(bf16[128,1920]{1,0:T(8,128)(2,1)S(1)} %bitcast.16, bf16[8,224,1792]{2,1,0:T(8,128)(2,1)S(1)} %bitcast.15), custom_call_target="tpu_custom_call" | custom-call | tf_op jit(solution)/shard_map/pallas_call | solution.py:376
  118.3 0.0 copy-start.7
  118.3 11.1 %all_to_all.41.parts_ref = bf16[4,464,128]{2,1,0:T(8,128)(2,1)S(1)} all-to-all(bf16[4,464,128]{2,1,0:T(8,128)(2,1)S(1)} %shard_map.137), channel_id=1, replica_groups=mesh['ctx'=8,'req'=8,'mp'=4] {'mp'}, dimensions={0} | all-to-all | bytes 950272 | tf_op jit(solution)/shard_map/all_to_all | solution.py:458
  129.4 0.9 shard_map.138
  130.3 4.9 %all-to-all-start.6 = ((bf16[4,448,128]{2,1,0:T(8,128)(2,1)}), bf16[4,448,128]{2,1,0:T(8,128)(2,1)S(1)}, u32[]{:S(2)}, u32[]{:S(2)}) async-start(bf16[4,448,128]{2,1,0:T(8,128)(2,1)} %shard_map.138), calls=%async_computation.6 | async-start | bytes 917504 | tf_op jit(solution)/shard_map/all_to_all | solution.py:458
  135.2 6.3 %all-to-all-done.6.hidden_ref = bf16[4,448,128]{2,1,0:T(8,128)(2,1)S(1)} async-done(((bf16[4,448,128]{2,1,0:T(8,128)(2,1)}), bf16[4,448,128]{2,1,0:T(8,128)(2,1)S(1)}, u32[]{:S(2)}, u32[]{:S(2)}) %all-to-all-start.6) | async-done | bytes 458784 | tf_op jit(solution)/shard_map/all_to_all | solution.py:458
  141.5 2.8 %copy-done.1 = bf16[1792,1792]{1,0:T(8,128)(2,1)S(1)} copy-done((bf16[1792,1792]{1,0:T(8,128)(2,1)S(1)}, bf16[1792,1792]{1,0:T(8,128)(2,1)}, u32[]{:S(2)}) %copy-start.1) | copy-done | bytes 6422552
  144.3 1.2 shard_map.139
  145.5 15.5 %all_to_all.42.parts_ref = bf16[8,16,1792]{2,1,0:T(8,128)(2,1)S(1)} all-to-all(bf16[8,16,1792]{2,1,0:T(8,128)(2,1)S(1)} %shard_map.139), channel_id=1, replica_groups=mesh['ctx'=8,'req'=8,'mp'=4] {'req'}, dimensions={0} | all-to-all | bytes 917504 | tf_op jit(solution)/shard_map/all_to_all | solution.py:458
  161.0 0.7 shard_map.140
  (24 shorter events, 0.1 us)
Async XLA Ops:
  7.2 106.5 %all-gather.5.cloned.1.call-start = ((), (), s32[]{:S(2)}) async-start(), calls=%async_computation.8 | async-start | bytes 7225344 | tf_op jit(solution)/shard_map/all_gather | solution.py:487
  8.7 27.2 %copy-start.5 = (bf16[896,112]{0,1:T(8,128)(2,1)S(1)}, bf16[896,112]{0,1:T(8,128)(2,1)}, u32[]{:S(2)}) copy-start(bf16[896,112]{0,1:T(8,128)(2,1)} %param.20) | copy-start | bytes 602116
  8.7 33.4 %copy-start.3 = (bf16[2,1,512,896]{3,2,1,0:T(8,128)(2,1)S(1)}, bf16[2,1,512,896]{3,2,1,0:T(8,128)(2,1)}, u32[]{:S(2)}) copy-start(bf16[2,1,512,896]{3,2,1,0:T(8,128)(2,1)} %param.17) | copy-start | bytes 5505028
  8.7 33.4 %copy-start.6 = (bf16[1,16,896]{2,1,0:T(8,128)(2,1)S(1)}, bf16[1,16,896]{2,1,0:T(8,128)(2,1)}, u32[]{:S(2)}) copy-start(bf16[1,16,896]{2,1,0:T(8,128)(2,1)} %param.14) | copy-start | bytes 86020
  8.7 33.4 %copy-start.8 = (bf16[2,1,16,896]{3,2,1,0:T(8,128)(2,1)S(1)}, bf16[2,1,16,896]{3,2,1,0:T(8,128)(2,1)}, u32[]{:S(2)}) copy-start(bf16[2,1,16,896]{3,2,1,0:T(8,128)(2,1)} %param.15) | copy-start | bytes 172036
  8.7 33.4 %copy-start.10 = (f32[8]{0:T(128)S(1)}, f32[8]{0:T(128)}, u32[]{:S(2)}) copy-start(f32[8]{0:T(128)} %slopes_ref.3) | copy-start | bytes 100
  8.7 126.5 %all-gather.7.cloned.1.call-start = ((), (), s32[]{:S(2)}) async-start(), calls=%async_computation.9 | async-start | bytes 7225344 | tf_op jit(solution)/shard_map/all_gather | solution.py:488
  9.5 11.7 %all-to-all-start = ((bf16[8,16,896]{2,1,0:T(8,128)(2,1)}), bf16[8,16,896]{2,1,0:T(8,128)(2,1)S(1)}, u32[]{:S(2)}, u32[]{:S(2)}) async-start(bf16[8,16,896]{2,1,0:T(8,128)(2,1)} %broadcast_in_dim.17), calls=%async_computation | async-start | bytes 458752 | tf_op jit(solution)/shard_map/all_to_all | solution.py:458
  14.8 1.4 copy-start.4
  21.1 3.1 %copy-start = (bf16[2,2048,896]{2,1,0:T(8,128)(2,1)S(1)}, bf16[2,2048,896]{2,1,0:T(8,128)(2,1)}, u32[]{:S(2)}) copy-start(bf16[2,2048,896]{2,1,0:T(8,128)(2,1)} %prefix_ref.1) | copy-start | bytes 22020100
  24.3 0.7 copy-start.9
  24.9 57.8 %copy-start.11 = (f32[1792]{0:T(1024)S(1)}, f32[1792]{0:T(1024)}, u32[]{:S(2)}) copy-start(f32[1792]{0:T(1024)} %param.21) | copy-start | bytes 21508
  31.7 19.2 %all-to-all-start.1 = ((bf16[8,240,128]{2,1,0:T(8,128)(2,1)}), bf16[8,240,128]{2,1,0:T(8,128)(2,1)S(1)}, u32[]{:S(2)}, u32[]{:S(2)}) async-start(bf16[8,240,128]{2,1,0:T(8,128)(2,1)} %shard_map.132), calls=%async_computation.1 | async-start | bytes 983040 | tf_op jit(solution)/shard_map/all_to_all | solution.py:458
  35.9 25.0 %collective-permute-start = (bf16[112,896]{1,0:T(8,128)(2,1)S(1)}, bf16[112,896]{1,0:T(8,128)(2,1)S(1)}, u32[]{:S(2)}, u32[]{:S(2)}) collective-permute-start(bf16[112,896]{1,0:T(8,128)(2,1)S(1)} %bitcast.20), channel_id=1, source_target_pairs={{0,64},{32,96},{64,128},{96,160},{128,192},{160,224},{192,0},{224,... | collective-permute-start | bytes 602120 | tf_op jit(solution)/shard_map/ppermute | solution.py:497
  37.9 30.0 %collective-permute-start.1 = (bf16[112,896]{1,0:T(8,128)(2,1)S(1)}, bf16[112,896]{1,0:T(8,128)(2,1)S(1)}, u32[]{:S(2)}, u32[]{:S(2)}) collective-permute-start(bf16[112,896]{1,0:T(8,128)(2,1)S(1)} %bitcast.21), channel_id=1, source_target_pairs={{0,128},{32,160},{64,192},{96,224},{128,0},{160,32},{192,64},{224,... | collective-permute-start | bytes 602120 | tf_op jit(solution)/shard_map/ppermute | solution.py:497
  40.6 27.3 %collective-permute-start.2 = (bf16[112,896]{1,0:T(8,128)(2,1)S(1)}, bf16[112,896]{1,0:T(8,128)(2,1)S(1)}, u32[]{:S(2)}, u32[]{:S(2)}) collective-permute-start(bf16[112,896]{1,0:T(8,128)(2,1)S(1)} %bitcast.22), channel_id=1, source_target_pairs={{0,192},{32,224},{64,0},{96,32},{128,64},{160,96},{192,128},{224,1... | collective-permute-start | bytes 602120 | tf_op jit(solution)/shard_map/ppermute | solution.py:497
  52.0 19.6 %all-to-all-start.2 = ((bf16[8,16,896]{2,1,0:T(8,128)(2,1)}), bf16[8,16,896]{2,1,0:T(8,128)(2,1)S(1)}, u32[]{:S(2)}, u32[]{:S(2)}) async-start(bf16[8,16,896]{2,1,0:T(8,128)(2,1)} %shard_map.134), calls=%async_computation.2 | async-start | bytes 458752 | tf_op jit(solution)/shard_map/all_to_all | solution.py:458
  60.9 7.6 %collective-permute-start.3 = (bf16[112,896]{1,0:T(8,128)(2,1)S(1)}, bf16[112,896]{1,0:T(8,128)(2,1)S(1)}, u32[]{:S(2)}, u32[]{:S(2)}) collective-permute-start(bf16[112,896]{1,0:T(8,128)(2,1)S(1)} %bitcast.23), channel_id=1, source_target_pairs={{0,32},{32,0},{64,96},{96,64},{128,160},{160,128},{192,224},{224,1... | collective-permute-start | bytes 602120 | tf_op jit(solution)/shard_map/ppermute | solution.py:515
  60.9 7.6 %collective-permute-start.4 = (bf16[112,896]{1,0:T(8,128)(2,1)S(1)}, bf16[112,896]{1,0:T(8,128)(2,1)S(1)}, u32[]{:S(2)}, u32[]{:S(2)}) collective-permute-start(bf16[112,896]{1,0:T(8,128)(2,1)S(1)} %collective-permute-done.refs_1_), channel_id=1, source_target_pairs={{0,32},{32,0},{64,96},{96,64},{128,160},{160,128},{192,224},{224,1... | collective-permute-start | bytes 602120 | tf_op jit(solution)/shard_map/ppermute | solution.py:515
  67.9 1.4 collective-permute-start.5
  67.9 1.7 %collective-permute-start.6 = (bf16[112,896]{1,0:T(8,128)(2,1)S(1)}, bf16[112,896]{1,0:T(8,128)(2,1)S(1)}, u32[]{:S(2)}, u32[]{:S(2)}) collective-permute-start(bf16[112,896]{1,0:T(8,128)(2,1)S(1)} %collective-permute-done.2.refs_3_), channel_id=1, source_target_pairs={{0,32},{32,0},{64,96},{96,64},{128,160},{160,128},{192,224},{224,1... | collective-permute-start | bytes 602120 | tf_op jit(solution)/shard_map/ppermute | solution.py:515
  73.2 21.1 %all-to-all-start.3 = ((bf16[32,2,16,128]{3,2,1,0:T(8,128)(2,1)}), bf16[32,2,16,128]{3,2,1,0:T(8,128)(2,1)S(1)}, u32[]{:S(2)}, u32[]{:S(2)}) async-start(bf16[32,2,16,128]{3,2,1,0:T(8,128)(2,1)} %shard_map.135), calls=%async_computation.3 | async-start | bytes 524288 | tf_op jit(solution)/shard_map/all_to_all | solution.py:458
  113.6 2.9 %copy-start.2 = (bf16[1792,1792]{1,0:T(8,128)(2,1)S(1)}, bf16[1792,1792]{1,0:T(8,128)(2,1)}, u32[]{:S(2)}) copy-start(bf16[1792,1792]{1,0:T(8,128)(2,1)} %all-gather.5.cloned.1.call-done) | copy-start | bytes 19267588
  118.3 42.6 %copy-start.7 = (f32[16,1792]{1,0:T(8,128)S(1)}, f32[16,1792]{1,0:T(8,128)}, u32[]{:S(2)}) copy-start(f32[16,1792]{1,0:T(8,128)} %get-tuple-element.26.residual_ref) | copy-start | bytes 344068
  130.3 11.2 %all-to-all-start.6 = ((bf16[4,448,128]{2,1,0:T(8,128)(2,1)}), bf16[4,448,128]{2,1,0:T(8,128)(2,1)S(1)}, u32[]{:S(2)}, u32[]{:S(2)}) async-start(bf16[4,448,128]{2,1,0:T(8,128)(2,1)} %shard_map.138), calls=%async_computation.6 | async-start | bytes 917504 | tf_op jit(solution)/shard_map/all_to_all | solution.py:458
  141.5 2.8 %copy-start.1 = (bf16[1792,1792]{1,0:T(8,128)(2,1)S(1)}, bf16[1792,1792]{1,0:T(8,128)(2,1)}, u32[]{:S(2)}) copy-start(bf16[1792,1792]{1,0:T(8,128)(2,1)} %all-gather.7.cloned.1.call-done) | copy-start | bytes 19267588
Sparse Core Ops, SparseCore 0:
  9.8 60.8 all-gather.4
  72.5 44.0 all-gather.6

commit v7 on v6

--- a/solution.py
+++ b/solution.py
@@ -70,7 +70,7 @@
             (((1,), (1,)), ((), ())),
             preferred_element_type=F32,
         )
-        scores = scores * scale + slopes_ref[head] * position
+        scores = scores * scale + slopes_ref[:, head : head + 1] * position
         top = jnp.max(scores, axis=1, keepdims=True)
         weights = jnp.exp(scores - top)
         total = jnp.sum(weights, axis=1, keepdims=True)
@@ -115,14 +115,14 @@
         ),
         in_specs=[
             pl.BlockSpec(memory_space=pltpu.SMEM),
-            pl.BlockSpec(memory_space=pltpu.SMEM),
+            pl.BlockSpec(memory_space=pltpu.VMEM),
             pl.BlockSpec(memory_space=pltpu.VMEM),
             pl.BlockSpec(memory_space=pltpu.VMEM),
             pl.BlockSpec(memory_space=pltpu.VMEM),
         ],
         out_specs=pl.BlockSpec(memory_space=pltpu.VMEM),
         compiler_params=pltpu.CompilerParams(vmem_limit_bytes=20 * MIB),
-    )(offset, slopes, query_rows, looked_up, prefix_kv)
+    )(offset, slopes[None, :], query_rows, looked_up, prefix_kv)
 
 
 def lookup_kernel(ids_ref, table_ref, out_ref):
@@ -166,7 +166,7 @@
     row = lax.broadcasted_iota(jnp.int32, (rows, 1), 0)
     slope = jnp.zeros((rows, 1), F32)
     for head in range(heads):
-        slope = jnp.where(row // draft == head, slopes_ref[head], slope)
+        slope = jnp.where(row // draft == head, slopes_ref[:, head : head + 1], slope)
     scale = 1.0 / math.sqrt(head_size)
     length = length_ref[0]
     contract = (((1,), (1,)), ((), ()))
@@ -213,10 +213,10 @@
             jax.ShapeDtypeStruct((draft, width), F32),
             jax.ShapeDtypeStruct((draft, LANES), F32),
         ),
-        in_specs=[smem, smem, vmem, vmem, vmem],
+        in_specs=[smem, vmem, vmem, vmem, vmem],
         out_specs=(vmem, vmem),
         compiler_params=pltpu.CompilerParams(vmem_limit_bytes=12 * MIB),
-    )(length, slopes, query_rows, suffix_kv, draft_kv)
+    )(length, slopes[None, :], query_rows, suffix_kv, draft_kv)
 
 
 def merge_kernel(parts_ref, own_ref, level_ref, out_ref, *, heads, head_size):
@@ -484,13 +484,12 @@
 
     copies = jnp.broadcast_to(queries, (ctx_count, draft, width))
     gathered = exchange(copies, "ctx")
-    up_all = lax.all_gather(after(up_weight, copies).T, "ctx")
-    down_all = lax.all_gather(after(down_weight, copies), "ctx")
-
     vocab_local = embed_table.shape[0]
     shifted = token_ids.reshape(1, -1) - model_index * vocab_local
     looked_up = look_up(shifted, embed_table.T)
     gathered, looked_up = lax.optimization_barrier((gathered, looked_up))
+    up_all = lax.all_gather(after(up_weight, gathered).T, "ctx")
+    down_all = lax.all_gather(after(down_weight, gathered), "ctx")
 
     out_blocks = [after(out_weight.T, looked_up)]
     out_blocks += [
@@ -507,12 +506,13 @@
         looked_up,
         ctx_count,
     )
+    parts, *out_blocks = lax.optimization_barrier((parts, *out_blocks))
     own, own_level = own_part(
         after(queries[0], parts), suffix_kv[:, 0], draft_kv[:, 0], slopes, suffix_len
     )
     parts = exchange(parts, "ctx")
     out_blocks += [
-        lax.ppermute(after(block, own), "ctx", [(i, i ^ 1) for i in range(ctx_count)])
+        lax.ppermute(block, "ctx", [(i, i ^ 1) for i in range(ctx_count)])
         for block in out_blocks
     ]
     attended = exchange(merge_parts(parts, own, own_level, heads, req_count), "req")

time: 169 us -> 166 us (0.982)
  starting transfers between devices: 38.5 us -> 31.7 us
  waiting for transfers between devices: 38.5 us -> 44.1 us
    all_to_all x5, waiting for transfers between devices: 30 us -> 41.8 us  [exchange(): return lax.all_to_all(value, axis, split_axis=0, concat_axis=0, tiled=True)]
    ppermute x3, waiting for transfers between devices: 6.56 us -> 0.01 us  [per_device(): lax.ppermute(out_blocks[0], 'ctx', [(i, (i + step) % ctx_count) for i in...]
    all_to_all x5, starting transfers between devices: 31.2 us -> 27.1 us  [exchange(): return lax.all_to_all(value, axis, split_axis=0, concat_axis=0, tiled=True)]
    ppermute x3, starting transfers between devices: 6.16 us -> 3.42 us  [per_device(): lax.ppermute(out_blocks[0], 'ctx', [(i, (i + step) % ctx_count) for i in...]
  transfers between devices with their start and end apart: 14 -> 14, of which waited for: 8 -> 9; matrix products, arithmetic and copies ran while one was open for 1% -> 1% of each run, Pallas kernels for 10% -> 9%
where the time goes in v7:
time: 166 us; the launch traced here: 165 us
  waiting for transfers between devices  44.1 us (27%)
  blocking collectives  44 us (27%)
  starting transfers between devices  31.7 us (19%)
  Pallas kernels  17.5 us (11%)
  between operations  14.8 us (9%)
  local copies, waits for them, and re-layouts  12.5 us (8%)
    all_to_all x3, blocking collectives, exchange(): return lax.all_to_all(value, axis, split_axis=0, concat_axis=0, tiled=True)  44 us
    all_to_all x5, waiting for transfers between devices, exchange(): return lax.all_to_all(value, axis, split_axis=0, concat_axis=0, tiled=True)  41.8 us
    all_to_all x5, starting transfers between devices, exchange(): return lax.all_to_all(value, axis, split_axis=0, concat_axis=0, tiled=True)  27.1 us
    unnamed x24, local copies, waits for them, and re-layouts  10.8 us
    pallas_call x1, Pallas kernels, prompt_part(): pl.pallas_call(functools.partial(prompt_kernel, heads=heads, head_size=wi...  6.36 us
    ppermute x3, starting transfers between devices, per_device(): lax.ppermute(out_blocks[0], 'ctx', [(i, (i + step) % ctx_count) for i in...  3.42 us
  transfers between devices with their start and end apart: 14, of which 9 were waited for; matrix products, arithmetic and copies ran while one was open for 1% of the time, Pallas kernels for 9%

profile of v7, /device:TPU:2, one launch (start us, length us, event | category | flops | bytes accessed | tf_op | source)
XLA Modules:
  0.0 165.4 jit_solution(9310917020470315958)
XLA Ops:
  7.2 1.5 broadcast_in_dim.22
  8.6 4.6 %all-to-all-start = ((bf16[8,16,896]{2,1,0:T(8,128)(2,1)}), bf16[8,16,896]{2,1,0:T(8,128)(2,1)S(1)}, u32[]{:S(2)}, u32[]{:S(2)}) async-start(bf16[8,16,896]{2,1,0:T(8,128)(2,1)} %broadcast_in_dim.22), calls=%async_computation | async-start | bytes 458752 | tf_op jit(solution)/shard_map/all_to_all | solution.py:458
  13.2 0.0 all-gather.5.cloned.1.call-start
  13.3 0.8 broadcast_subtract_fusion
  14.1 0.1 copy.15
  14.2 0.1 sub.14.ids_ref
  14.3 1.4 copy-done.4
  15.6 1.9 %shard_map.131.looked_ref = bf16[112,1024]{1,0:T(8,128)(2,1)S(1)} custom-call(s32[1,1024]{1,0:T(1,128)S(1)} %sub.14.ids_ref, bf16[112,6400]{1,0:T(8,128)(2,1)S(1)} %bitcast.19), custom_call_target="tpu_custom_call" | custom-call | tf_op jit(solution)/shard_map/pallas_call | solution.py:143
  17.6 2.9 %all-to-all-done = bf16[8,16,896]{2,1,0:T(8,128)(2,1)S(1)} async-done(((bf16[8,16,896]{2,1,0:T(8,128)(2,1)}), bf16[8,16,896]{2,1,0:T(8,128)(2,1)S(1)}, u32[]{:S(2)}, u32[]{:S(2)}) %all-to-all-start) | async-done | bytes 229408 | tf_op jit(solution)/shard_map/all_to_all | solution.py:458
  20.4 0.0 all-gather.5.cloned.1.call-update
  20.4 0.0 all-gather.7.cloned.1.call-start
  20.5 0.7 all-gather.7.cloned.1.call-update
  21.2 0.6 collective-permute-start
  21.8 2.1 %collective-permute-start.1 = (bf16[112,896]{1,0:T(8,128)(2,1)}, bf16[112,896]{1,0:T(8,128)(2,1)S(1)}, u32[]{:S(2)}, u32[]{:S(2)}) collective-permute-start(bf16[112,896]{1,0:T(8,128)(2,1)} %bitcast.22), channel_id=1, source_target_pairs={{0,128},{32,160},{64,192},{96,224},{128,0},{160,32},{192,64},{224,... | collective-permute-start | bytes 602120 | tf_op jit(solution)/shard_map/ppermute | solution.py:496
  23.9 0.7 collective-permute-start.2
  24.6 3.1 %copy-done = bf16[2,2048,896]{2,1,0:T(8,128)(2,1)S(1)} copy-done((bf16[2,2048,896]{2,1,0:T(8,128)(2,1)S(1)}, bf16[2,2048,896]{2,1,0:T(8,128)(2,1)}, u32[]{:S(2)}) %copy-start) | copy-done | bytes 7340056
  27.7 0.7 copy-done.9
  28.4 6.4 %shard_map.132 = bf16[8,240,128]{2,1,0:T(8,128)(2,1)} custom-call(s32[1]{0:T(128)} %bitcast.1.offset_ref, f32[1,8]{1,0:T(1,128)S(1)} %bitcast.30, bf16[128,896]{1,0:T(8,128)(2,1)S(1)} %bitcast.20, bf16[112,1024]{1,0:T(8,128)(2,1)S(1)} %shard_map.131.looked_ref, bf16[2,2048,896]{2,1,0:T(8,128)(2,1)S(1)} %copy-done), custom_call_target="tpu_custom_call" | custom-call | tf_op jit(solution)/shard_map/pallas_call | solution.py:111
  34.7 4.1 %all-to-all-start.1 = ((bf16[8,240,128]{2,1,0:T(8,128)(2,1)}), bf16[8,240,128]{2,1,0:T(8,128)(2,1)S(1)}, u32[]{:S(2)}, u32[]{:S(2)}) async-start(bf16[8,240,128]{2,1,0:T(8,128)(2,1)} %shard_map.132), calls=%async_computation.1 | async-start | bytes 983040 | tf_op jit(solution)/shard_map/all_to_all | solution.py:458
  39.5 1.1 shard_map.133
  40.7 13.8 %all-to-all-done.1.parts_ref = bf16[8,240,128]{2,1,0:T(8,128)(2,1)S(1)} async-done(((bf16[8,240,128]{2,1,0:T(8,128)(2,1)}), bf16[8,240,128]{2,1,0:T(8,128)(2,1)S(1)}, u32[]{:S(2)}, u32[]{:S(2)}) %all-to-all-start.1) | async-done | bytes 491552 | tf_op jit(solution)/shard_map/all_to_all | solution.py:458
  54.4 1.1 shard_map.134
  55.5 8.5 %all-to-all-start.2 = ((bf16[8,16,896]{2,1,0:T(8,128)(2,1)}), bf16[8,16,896]{2,1,0:T(8,128)(2,1)S(1)}, u32[]{:S(2)}, u32[]{:S(2)}) async-start(bf16[8,16,896]{2,1,0:T(8,128)(2,1)} %shard_map.134), calls=%async_computation.2 | async-start | bytes 458752 | tf_op jit(solution)/shard_map/all_to_all | solution.py:458
  64.0 0.1 collective-permute-start.3
  64.1 0.5 collective-permute-start.4
  64.6 0.1 collective-permute-start.5
  64.7 0.4 collective-permute-start.6
  65.1 0.4 collective-permute-done.3.refs_4_
  65.5 0.3 collective-permute-done.4.refs_5_
  65.8 0.6 collective-permute-done.5.refs_6_
  66.4 0.3 collective-permute-done.6.refs_7_
  66.6 8.2 %all-to-all-done.2.rows_ref = bf16[8,16,896]{2,1,0:T(8,128)(2,1)S(1)} async-done(((bf16[8,16,896]{2,1,0:T(8,128)(2,1)}), bf16[8,16,896]{2,1,0:T(8,128)(2,1)S(1)}, u32[]{:S(2)}, u32[]{:S(2)}) %all-to-all-start.2) | async-done | bytes 229408 | tf_op jit(solution)/shard_map/all_to_all | solution.py:458
  74.9 1.6 shard_map.135
  76.5 5.0 %all-to-all-start.3 = ((bf16[32,2,16,128]{3,2,1,0:T(8,128)(2,1)}), bf16[32,2,16,128]{3,2,1,0:T(8,128)(2,1)S(1)}, u32[]{:S(2)}, u32[]{:S(2)}) async-start(bf16[32,2,16,128]{3,2,1,0:T(8,128)(2,1)} %shard_map.135), calls=%async_computation.3 | async-start | bytes 524288 | tf_op jit(solution)/shard_map/all_to_all | solution.py:458
  81.5 10.7 %all-to-all-done.3.parts_ref = bf16[32,2,16,128]{3,2,1,0:T(8,128)(2,1)S(1)} async-done(((bf16[32,2,16,128]{3,2,1,0:T(8,128)(2,1)}), bf16[32,2,16,128]{3,2,1,0:T(8,128)(2,1)S(1)}, u32[]{:S(2)}, u32[]{:S(2)}) %all-to-all-start.3) | async-done | bytes 262176 | tf_op jit(solution)/shard_map/all_to_all | solution.py:458
  92.2 0.8 shard_map.136
  93.1 18.0 %all_to_all.40 = bf16[8,16,1920]{2,1,0:T(8,128)(2,1)S(1)} all-to-all(bf16[8,16,1920]{2,1,0:T(8,128)(2,1)S(1)} %get-tuple-element.29), channel_id=1, replica_groups=mesh['ctx'=8,'req'=8,'mp'=4] {'req'}, dimensions={0} | all-to-all | bytes 983040 | tf_op jit(solution)/shard_map/all_to_all | solution.py:458
  111.1 2.9 %copy-done.2 = bf16[1792,1792]{1,0:T(8,128)(2,1)S(1)} copy-done((bf16[1792,1792]{1,0:T(8,128)(2,1)S(1)}, bf16[1792,1792]{1,0:T(8,128)(2,1)}, u32[]{:S(2)}) %copy-start.2) | copy-done | bytes 6422552
  114.0 1.8 %shard_map.137 = bf16[4,464,128]{2,1,0:T(8,128)(2,1)S(1)} custom-call(bf16[128,1920]{1,0:T(8,128)(2,1)S(1)} %bitcast.17, bf16[8,224,1792]{2,1,0:T(8,128)(2,1)S(1)} %bitcast.16), custom_call_target="tpu_custom_call" | custom-call | tf_op jit(solution)/shard_map/pallas_call | solution.py:376
  115.8 0.0 copy-start.7
  115.8 11.0 %all_to_all.41.parts_ref = bf16[4,464,128]{2,1,0:T(8,128)(2,1)S(1)} all-to-all(bf16[4,464,128]{2,1,0:T(8,128)(2,1)S(1)} %shard_map.137), channel_id=1, replica_groups=mesh['ctx'=8,'req'=8,'mp'=4] {'mp'}, dimensions={0} | all-to-all | bytes 950272 | tf_op jit(solution)/shard_map/all_to_all | solution.py:458
  126.8 0.9 shard_map.138
  127.7 4.9 %all-to-all-start.6 = ((bf16[4,448,128]{2,1,0:T(8,128)(2,1)}), bf16[4,448,128]{2,1,0:T(8,128)(2,1)S(1)}, u32[]{:S(2)}, u32[]{:S(2)}) async-start(bf16[4,448,128]{2,1,0:T(8,128)(2,1)} %shard_map.138), calls=%async_computation.6 | async-start | bytes 917504 | tf_op jit(solution)/shard_map/all_to_all | solution.py:458
  132.6 6.3 %all-to-all-done.6.hidden_ref = bf16[4,448,128]{2,1,0:T(8,128)(2,1)S(1)} async-done(((bf16[4,448,128]{2,1,0:T(8,128)(2,1)}), bf16[4,448,128]{2,1,0:T(8,128)(2,1)S(1)}, u32[]{:S(2)}, u32[]{:S(2)}) %all-to-all-start.6) | async-done | bytes 458784 | tf_op jit(solution)/shard_map/all_to_all | solution.py:458
  138.9 2.8 %copy-done.1 = bf16[1792,1792]{1,0:T(8,128)(2,1)S(1)} copy-done((bf16[1792,1792]{1,0:T(8,128)(2,1)S(1)}, bf16[1792,1792]{1,0:T(8,128)(2,1)}, u32[]{:S(2)}) %copy-start.1) | copy-done | bytes 6422552
  141.7 1.2 shard_map.139
  142.9 15.0 %all_to_all.42.parts_ref = bf16[8,16,1792]{2,1,0:T(8,128)(2,1)S(1)} all-to-all(bf16[8,16,1792]{2,1,0:T(8,128)(2,1)S(1)} %shard_map.139), channel_id=1, replica_groups=mesh['ctx'=8,'req'=8,'mp'=4] {'req'}, dimensions={0} | all-to-all | bytes 917504 | tf_op jit(solution)/shard_map/all_to_all | solution.py:458
  157.9 0.7 shard_map.140
  (24 shorter events, 0.1 us)
Async XLA Ops:
  8.6 30.9 %copy-start.6 = (bf16[1,16,896]{2,1,0:T(8,128)(2,1)S(1)}, bf16[1,16,896]{2,1,0:T(8,128)(2,1)}, u32[]{:S(2)}) copy-start(bf16[1,16,896]{2,1,0:T(8,128)(2,1)} %param.14) | copy-start | bytes 86020
  8.6 30.9 %copy-start.8 = (bf16[2,1,16,896]{3,2,1,0:T(8,128)(2,1)S(1)}, bf16[2,1,16,896]{3,2,1,0:T(8,128)(2,1)}, u32[]{:S(2)}) copy-start(bf16[2,1,16,896]{3,2,1,0:T(8,128)(2,1)} %param.15) | copy-start | bytes 172036
  8.6 30.9 %copy-start.10 = (f32[8]{0:T(128)S(1)}, f32[8]{0:T(128)}, u32[]{:S(2)}) copy-start(f32[8]{0:T(128)} %param.19) | copy-start | bytes 100
  8.6 11.8 %all-to-all-start = ((bf16[8,16,896]{2,1,0:T(8,128)(2,1)}), bf16[8,16,896]{2,1,0:T(8,128)(2,1)S(1)}, u32[]{:S(2)}, u32[]{:S(2)}) async-start(bf16[8,16,896]{2,1,0:T(8,128)(2,1)} %broadcast_in_dim.22), calls=%async_computation | async-start | bytes 458752 | tf_op jit(solution)/shard_map/all_to_all | solution.py:458
  13.2 26.3 %copy-start.3 = (bf16[2,1,512,896]{3,2,1,0:T(8,128)(2,1)S(1)}, bf16[2,1,512,896]{3,2,1,0:T(8,128)(2,1)}, u32[]{:S(2)}) copy-start(bf16[2,1,512,896]{3,2,1,0:T(8,128)(2,1)} %param.17) | copy-start | bytes 5505028
  13.2 97.8 %all-gather.5.cloned.1.call-start = ((), (), s32[]{:S(2)}) async-start(), calls=%async_computation.8 | async-start | bytes 7225344 | tf_op jit(solution)/shard_map/all_gather | solution.py:491
  14.3 1.4 copy-start.4
  20.4 112.2 %all-gather.7.cloned.1.call-start = ((), (), s32[]{:S(2)}) async-start(), calls=%async_computation.9 | async-start | bytes 7225344 | tf_op jit(solution)/shard_map/all_gather | solution.py:492
  20.5 43.5 %copy-start.5 = (bf16[896,112]{0,1:T(8,128)(2,1)S(1)}, bf16[896,112]{0,1:T(8,128)(2,1)}, u32[]{:S(2)}) copy-start(bf16[896,112]{0,1:T(8,128)(2,1)} %param.20) | copy-start | bytes 602116
  21.2 13.5 %collective-permute-start = (bf16[112,896]{1,0:T(8,128)(2,1)}, bf16[112,896]{1,0:T(8,128)(2,1)S(1)}, u32[]{:S(2)}, u32[]{:S(2)}) collective-permute-start(bf16[112,896]{1,0:T(8,128)(2,1)} %bitcast.21), channel_id=1, source_target_pairs={{0,64},{32,96},{64,128},{96,160},{128,192},{160,224},{192,0},{224,... | collective-permute-start | bytes 602120 | tf_op jit(solution)/shard_map/ppermute | solution.py:496
  21.8 12.9 %collective-permute-start.1 = (bf16[112,896]{1,0:T(8,128)(2,1)}, bf16[112,896]{1,0:T(8,128)(2,1)S(1)}, u32[]{:S(2)}, u32[]{:S(2)}) collective-permute-start(bf16[112,896]{1,0:T(8,128)(2,1)} %bitcast.22), channel_id=1, source_target_pairs={{0,128},{32,160},{64,192},{96,224},{128,0},{160,32},{192,64},{224,... | collective-permute-start | bytes 602120 | tf_op jit(solution)/shard_map/ppermute | solution.py:496
  23.9 10.8 %collective-permute-start.2 = (bf16[112,896]{1,0:T(8,128)(2,1)}, bf16[112,896]{1,0:T(8,128)(2,1)S(1)}, u32[]{:S(2)}, u32[]{:S(2)}) collective-permute-start(bf16[112,896]{1,0:T(8,128)(2,1)} %bitcast.23), channel_id=1, source_target_pairs={{0,192},{32,224},{64,0},{96,32},{128,64},{160,96},{192,128},{224,1... | collective-permute-start | bytes 602120 | tf_op jit(solution)/shard_map/ppermute | solution.py:496
  24.6 3.1 %copy-start = (bf16[2,2048,896]{2,1,0:T(8,128)(2,1)S(1)}, bf16[2,2048,896]{2,1,0:T(8,128)(2,1)}, u32[]{:S(2)}) copy-start(bf16[2,2048,896]{2,1,0:T(8,128)(2,1)} %prefix_ref.1) | copy-start | bytes 22020100
  27.7 0.7 copy-start.9
  28.3 53.2 %copy-start.11 = (f32[1792]{0:T(1024)S(1)}, f32[1792]{0:T(1024)}, u32[]{:S(2)}) copy-start(f32[1792]{0:T(1024)} %param.21) | copy-start | bytes 21508
  34.7 19.7 %all-to-all-start.1 = ((bf16[8,240,128]{2,1,0:T(8,128)(2,1)}), bf16[8,240,128]{2,1,0:T(8,128)(2,1)S(1)}, u32[]{:S(2)}, u32[]{:S(2)}) async-start(bf16[8,240,128]{2,1,0:T(8,128)(2,1)} %shard_map.132), calls=%async_computation.1 | async-start | bytes 983040 | tf_op jit(solution)/shard_map/all_to_all | solution.py:458
  55.5 19.4 %all-to-all-start.2 = ((bf16[8,16,896]{2,1,0:T(8,128)(2,1)}), bf16[8,16,896]{2,1,0:T(8,128)(2,1)S(1)}, u32[]{:S(2)}, u32[]{:S(2)}) async-start(bf16[8,16,896]{2,1,0:T(8,128)(2,1)} %shard_map.134), calls=%async_computation.2 | async-start | bytes 458752 | tf_op jit(solution)/shard_map/all_to_all | solution.py:458
  64.0 1.5 collective-permute-start.3
  64.1 1.7 %collective-permute-start.4 = (bf16[112,896]{1,0:T(8,128)(2,1)S(1)}, bf16[112,896]{1,0:T(8,128)(2,1)S(1)}, u32[]{:S(2)}, u32[]{:S(2)}) collective-permute-start(bf16[112,896]{1,0:T(8,128)(2,1)S(1)} %collective-permute-done.refs_1_), channel_id=1, source_target_pairs={{0,32},{32,0},{64,96},{96,64},{128,160},{160,128},{192,224},{224,1... | collective-permute-start | bytes 602120 | tf_op jit(solution)/shard_map/ppermute | solution.py:515
  64.6 1.8 %collective-permute-start.5 = (bf16[112,896]{1,0:T(8,128)(2,1)S(1)}, bf16[112,896]{1,0:T(8,128)(2,1)S(1)}, u32[]{:S(2)}, u32[]{:S(2)}) collective-permute-start(bf16[112,896]{1,0:T(8,128)(2,1)S(1)} %collective-permute-done.1.refs_2_), channel_id=1, source_target_pairs={{0,32},{32,0},{64,96},{96,64},{128,160},{160,128},{192,224},{224,1... | collective-permute-start | bytes 602120 | tf_op jit(solution)/shard_map/ppermute | solution.py:515
  64.7 2.0 %collective-permute-start.6 = (bf16[112,896]{1,0:T(8,128)(2,1)S(1)}, bf16[112,896]{1,0:T(8,128)(2,1)S(1)}, u32[]{:S(2)}, u32[]{:S(2)}) collective-permute-start(bf16[112,896]{1,0:T(8,128)(2,1)S(1)} %collective-permute-done.2.refs_3_), channel_id=1, source_target_pairs={{0,32},{32,0},{64,96},{96,64},{128,160},{160,128},{192,224},{224,1... | collective-permute-start | bytes 602120 | tf_op jit(solution)/shard_map/ppermute | solution.py:515
  76.5 15.7 %all-to-all-start.3 = ((bf16[32,2,16,128]{3,2,1,0:T(8,128)(2,1)}), bf16[32,2,16,128]{3,2,1,0:T(8,128)(2,1)S(1)}, u32[]{:S(2)}, u32[]{:S(2)}) async-start(bf16[32,2,16,128]{3,2,1,0:T(8,128)(2,1)} %shard_map.135), calls=%async_computation.3 | async-start | bytes 524288 | tf_op jit(solution)/shard_map/all_to_all | solution.py:458
  111.1 2.9 %copy-start.2 = (bf16[1792,1792]{1,0:T(8,128)(2,1)S(1)}, bf16[1792,1792]{1,0:T(8,128)(2,1)}, u32[]{:S(2)}) copy-start(bf16[1792,1792]{1,0:T(8,128)(2,1)} %all-gather.5.cloned.1.call-done) | copy-start | bytes 19267588
  115.8 42.1 %copy-start.7 = (f32[16,1792]{1,0:T(8,128)S(1)}, f32[16,1792]{1,0:T(8,128)}, u32[]{:S(2)}) copy-start(f32[16,1792]{1,0:T(8,128)} %get-tuple-element.28.residual_ref) | copy-start | bytes 344068
  127.7 11.2 %all-to-all-start.6 = ((bf16[4,448,128]{2,1,0:T(8,128)(2,1)}), bf16[4,448,128]{2,1,0:T(8,128)(2,1)S(1)}, u32[]{:S(2)}, u32[]{:S(2)}) async-start(bf16[4,448,128]{2,1,0:T(8,128)(2,1)} %shard_map.138), calls=%async_computation.6 | async-start | bytes 917504 | tf_op jit(solution)/shard_map/all_to_all | solution.py:458
  138.9 2.8 %copy-start.1 = (bf16[1792,1792]{1,0:T(8,128)(2,1)S(1)}, bf16[1792,1792]{1,0:T(8,128)(2,1)}, u32[]{:S(2)}) copy-start(bf16[1792,1792]{1,0:T(8,128)(2,1)} %all-gather.7.cloned.1.call-done) | copy-start | bytes 19267588
Sparse Core Ops, SparseCore 0:
  20.6 50.2 all-gather.4
  72.6 44.1 all-gather.6

commit v8 on v7

--- a/solution.py
+++ b/solution.py
@@ -352,34 +352,34 @@
     )(parts, gain[None, :])
 
 
-def lift_kernel(rows_ref, weight_ref, out_ref, *, hidden):
-    blocks, _, width = weight_ref.shape
+def lift_kernel(rows_ref, *refs):
+    *weight_refs, out_ref = refs
+    width = weight_refs[0].shape[1]
     mp, height, _ = out_ref.shape
-    pair = blocks // mp
+    held = sum(ref.shape[0] for ref in weight_refs) // mp
     rows = rows_ref[:, :width]
-    for block in range(blocks):
-        piece, place = divmod(block, pair)
-        out_ref[piece, place * hidden : (place + 1) * hidden] = lax.dot_general(
-            weight_ref[block, weight_ref.shape[1] - hidden :],
-            rows,
-            (((1,), (1,)), ((), ())),
-            preferred_element_type=F32,
+    first = 0
+    for ref in weight_refs:
+        piece, place = divmod(first, held)
+        out_ref[piece, place : place + ref.shape[0]] = lax.dot_general(
+            ref[...], rows, (((1,), (1,)), ((), ())), preferred_element_type=F32
         ).astype(BF16)
+        first += ref.shape[0]
     squares = jnp.transpose(rows_ref[:, width:].astype(F32)).astype(BF16)
     for piece in range(mp):
-        out_ref[piece, pair * hidden :] = squares[: height - pair * hidden]
-
-
-def lift_rows(rows, weight, hidden, mp):
-    blocks = weight.shape[0]
-    vmem = pl.BlockSpec(memory_space=pltpu.VMEM)
-    return pl.pallas_call(
-        functools.partial(lift_kernel, hidden=hidden),
-        out_shape=jax.ShapeDtypeStruct((mp, blocks // mp * hidden + 16, rows.shape[0]), BF16),
-        in_specs=[vmem, vmem],
+        out_ref[piece, held:] = squares[: height - held]
+
+
+def lift_rows(rows, weights, mp):
+    held = sum(weight.shape[0] for weight in weights) // mp
+    vmem = pl.BlockSpec(memory_space=pltpu.VMEM)
+    return pl.pallas_call(
+        lift_kernel,
+        out_shape=jax.ShapeDtypeStruct((mp, held + 16, rows.shape[0]), BF16),
+        in_specs=[vmem] * (1 + len(weights)),
         out_specs=vmem,
         compiler_params=pltpu.CompilerParams(vmem_limit_bytes=20 * MIB),
-    )(rows, weight)
+    )(rows, *weights)
 
 
 def gelu_kernel(parts_ref, out_ref, *, model_width):
@@ -405,31 +405,35 @@
     )(parts)
 
 
-def lower_kernel(hidden_ref, weight_ref, out_ref):
-    blocks, features, _ = weight_ref.shape
-    pair = blocks // hidden_ref.shape[0]
+def lower_kernel(hidden_ref, *refs):
+    *weight_refs, out_ref = refs
+    held = hidden_ref.shape[1]
     total = None
-    for block in range(blocks):
-        piece, place = divmod(block, pair)
+    first = 0
+    for ref in weight_refs:
+        piece, place = divmod(first, held)
         product = lax.dot_general(
-            hidden_ref[piece, place * features : (place + 1) * features],
-            weight_ref[block],
+            hidden_ref[piece, place : place + ref.shape[0]],
+            ref[...],
             (((0,), (0,)), ((), ())),
             preferred_element_type=F32,
         )
         total = product if total is None else total + product
+        first += ref.shape[0]
     out_ref[...] = total.astype(BF16).reshape(out_ref.shape)
 
 
-def lower_rows(hidden, weight, targets):
+def lower_rows(hidden, weights, targets):
     vmem = pl.BlockSpec(memory_space=pltpu.VMEM)
     return pl.pallas_call(
         lower_kernel,
-        out_shape=jax.ShapeDtypeStruct((targets, hidden.shape[2] // targets, weight.shape[2]), BF16),
-        in_specs=[vmem, vmem],
+        out_shape=jax.ShapeDtypeStruct(
+            (targets, hidden.shape[2] // targets, weights[0].shape[1]), BF16
+        ),
+        in_specs=[vmem] * (1 + len(weights)),
         out_specs=vmem,
         compiler_params=pltpu.CompilerParams(vmem_limit_bytes=20 * MIB),
-    )(hidden, weight)
+    )(hidden, *weights)
 
 
 def finish_kernel(parts_ref, residual_ref, out_ref):
@@ -452,6 +456,26 @@
 
 def after(value, earlier):
     return lax.optimization_barrier((value, earlier))[0]
+
+
+def shifted_by(block, step):
+    count = lax.axis_size("ctx")
+    return lax.ppermute(block, "ctx", [(i, (i + step) % count) for i in range(count)])
+
+
+def beside(blocks):
+    count = lax.axis_size("ctx")
+    return [lax.ppermute(block, "ctx", [(i, i ^ 1) for i in range(count)]) for block in blocks]
+
+
+def nearest(block):
+    return [block, shifted_by(block, 2), shifted_by(block, -2)]
+
+
+def farthest(blocks):
+    _, back, on = blocks
+    half = back.shape[0] // 2
+    return [shifted_by(back[:half], 2), shifted_by(on[half:], -2)]
 
 
 def exchange(value, axis):
@@ -488,14 +512,9 @@
     shifted = token_ids.reshape(1, -1) - model_index * vocab_local
     looked_up = look_up(shifted, embed_table.T)
     gathered, looked_up = lax.optimization_barrier((gathered, looked_up))
-    up_all = lax.all_gather(after(up_weight, gathered).T, "ctx")
-    down_all = lax.all_gather(after(down_weight, gathered), "ctx")
-
     out_blocks = [after(out_weight.T, looked_up)]
-    out_blocks += [
-        lax.ppermute(out_blocks[0], "ctx", [(i, (i + step) % ctx_count) for i in range(ctx_count)])
-        for step in range(2, ctx_count, 2)
-    ]
+    out_blocks += [shifted_by(out_blocks[0], step) for step in range(2, ctx_count, 2)]
+    up_blocks = nearest(after(up_weight.T, looked_up))
 
     offset = (prompt_local * (ctx_count - ctx_index)).astype(jnp.int32).reshape(1)
     parts = prompt_part(
@@ -511,28 +530,33 @@
         after(queries[0], parts), suffix_kv[:, 0], draft_kv[:, 0], slopes, suffix_len
     )
     parts = exchange(parts, "ctx")
-    out_blocks += [
-        lax.ppermute(block, "ctx", [(i, i ^ 1) for i in range(ctx_count)])
-        for block in out_blocks
-    ]
-    attended = exchange(merge_parts(parts, own, own_level, heads, req_count), "req")
-
-    pieces = exchange(
-        project_rows(
-            attended, out_blocks, parts, ctx_index.astype(jnp.int32).reshape(1), mp_count
-        ),
-        ("req", "mp"),
-    )
+    out_blocks += beside(out_blocks)
+    merged = merge_parts(parts, own, own_level, heads, req_count)
+    merged, *up_blocks = lax.optimization_barrier((merged, *up_blocks))
+    attended = exchange(merged, "req")
+    up_blocks += farthest(up_blocks)
+    down_blocks = nearest(after(down_weight, merged))
+
+    pieces = project_rows(
+        attended, out_blocks, parts, ctx_index.astype(jnp.int32).reshape(1), mp_count
+    )
+    pieces, *up_blocks = lax.optimization_barrier((pieces, *up_blocks))
+    pieces = exchange(pieces, ("req", "mp"))
+    up_blocks += beside(up_blocks)
     residual, centred = residual_rows(
         pieces, ln_gain, mp_count, draft, out_weight.shape[1], req_count
     )
+    centred, *down_blocks = lax.optimization_barrier((centred, *down_blocks))
     centred = exchange(centred, "req").reshape(req_count * draft, -1)
-
-    hidden = up_weight.shape[1]
-    lifted = exchange(lift_rows(centred, up_all, hidden, mp_count), "mp")
-    activated = activate(lifted, ctx_count // mp_count * hidden, quarter * mp_count)
-    activated = exchange(activated, "mp")
-    lowered = exchange(lower_rows(activated, down_all, req_count), "req")
+    down_blocks += farthest(down_blocks)
+
+    lifted = lift_rows(centred, up_blocks, mp_count)
+    lifted, *down_blocks = lax.optimization_barrier((lifted, *down_blocks))
+    lifted = exchange(lifted, "mp")
+    down_blocks += beside(down_blocks)
+    hidden = up_weight.shape[1] * ctx_count // mp_count
+    activated = exchange(activate(lifted, hidden, quarter * mp_count), "mp")
+    lowered = exchange(lower_rows(activated, down_blocks, req_count), "req")
     layer_out = finish(lowered, residual)
     return residual[None], layer_out[None]
 

time: 166 us -> 187 us (1.13)
  starting transfers between devices: 31.7 us -> 60.7 us
  blocking collectives: 44 us -> 19.1 us
  between operations: 14.8 us -> 1.45 us
  waiting for transfers between devices: 44.1 us -> 57.4 us
  local copies, waits for them, and re-layouts: 12.5 us -> 23.1 us
  Pallas kernels: 17.5 us -> 23.3 us
    all_to_all x3 -> x1, blocking collectives: 44 us -> 19.1 us  [exchange(): return lax.all_to_all(value, axis, split_axis=0, concat_axis=0, tiled=True)]
    ppermute x7 -> x25, waiting for transfers between devices: 1.58 us -> 18.2 us  [the longest x11 13.5 us: shifted_by(): lax.ppermute(block, 'ctx', [(i, (i + step) % count) for i in range(count)])]
    ppermute x7 -> x25, starting transfers between devices: 4.52 us -> 19.9 us  [the longest x11 16.2 us: shifted_by(): lax.ppermute(block, 'ctx', [(i, (i + step) % count) for i in range(count)])]
    all_to_all x5 -> x7, starting transfers between devices: 27.1 us -> 40.9 us  [exchange(): return lax.all_to_all(value, axis, split_axis=0, concat_axis=0, tiled=True)]
    unnamed x24 -> x46, local copies, waits for them, and re-layouts: 10.8 us -> 17.4 us
    slice x0 -> x4, local copies, waits for them, and re-layouts: none -> 4.1 us  [farthest(): return [shifted_by(back[:half], 2), shifted_by(on[half:], -2)]]
    all_to_all x5 -> x7, waiting for transfers between devices: 41.8 us -> 39.2 us  [exchange(): return lax.all_to_all(value, axis, split_axis=0, concat_axis=0, tiled=True)]
    pallas_call x1, Pallas kernels: 1.81 us -> 4.16 us  [lift_rows(): pl.pallas_call(lift_kernel, out_shape=jax.ShapeDtypeStruct((mp, held + 16...]
  transfers between devices with their start and end apart: 14 -> 32, of which waited for: 9 -> 9; matrix products, arithmetic and copies ran while one was open for 1% -> 3% of each run, Pallas kernels for 9% -> 10%
where the time goes in v8:
time: 187 us; the launch traced here: 186 us
  starting transfers between devices  60.7 us (32%)
  waiting for transfers between devices  57.4 us (31%)
  Pallas kernels  23.3 us (12%)
  local copies, waits for them, and re-layouts  23.1 us (12%)
  blocking collectives  19.1 us (10%)
    all_to_all x7, starting transfers between devices, exchange(): return lax.all_to_all(value, axis, split_axis=0, concat_axis=0, tiled=True)  40.9 us
    all_to_all x7, waiting for transfers between devices, exchange(): return lax.all_to_all(value, axis, split_axis=0, concat_axis=0, tiled=True)  39.2 us
    all_to_all x1, blocking collectives, exchange(): return lax.all_to_all(value, axis, split_axis=0, concat_axis=0, tiled=True)  19.1 us
    unnamed x46, local copies, waits for them, and re-layouts  17.4 us
    ppermute x11, starting transfers between devices, shifted_by(): lax.ppermute(block, 'ctx', [(i, (i + step) % count) for i in range(count)])  16.2 us
    ppermute x11, waiting for transfers between devices, shifted_by(): lax.ppermute(block, 'ctx', [(i, (i + step) % count) for i in range(count)])  13.5 us
    pallas_call x1, Pallas kernels, prompt_part(): pl.pallas_call(functools.partial(prompt_kernel, heads=heads, head_size=wi...  6.36 us
    ppermute x14, waiting for transfers between devices, beside(): lax.ppermute(block, 'ctx', [(i, i ^ 1) for i in range(count)])  4.65 us
  transfers between devices with their start and end apart: 32, of which 9 were waited for; matrix products, arithmetic and copies ran while one was open for 3% of the time, Pallas kernels for 10%

profile of v8, /device:TPU:2, one launch (start us, length us, event | category | flops | bytes accessed | tf_op | source)
XLA Modules:
  0.0 185.9 jit_solution(620698634567618048)
XLA Ops:
  0.6 1.5 broadcast_in_dim.22
  2.1 4.5 %all-to-all-start = ((bf16[8,16,896]{2,1,0:T(8,128)(2,1)}), bf16[8,16,896]{2,1,0:T(8,128)(2,1)S(1)}, u32[]{:S(2)}, u32[]{:S(2)}) async-start(bf16[8,16,896]{2,1,0:T(8,128)(2,1)} %broadcast_in_dim.22), calls=%async_computation | async-start | bytes 458752 | tf_op jit(solution)/shard_map/all_to_all | solution.py:482
  7.5 1.4 copy-done.2
  8.8 1.9 %shard_map.131.looked_ref = bf16[112,1024]{1,0:T(8,128)(2,1)S(1)} custom-call(s32[1,1024]{1,0:T(1,128)S(1)} %sub.14.ids_ref, bf16[112,6400]{1,0:T(8,128)(2,1)S(1)} %bitcast.15), custom_call_target="tpu_custom_call" | custom-call | tf_op jit(solution)/shard_map/pallas_call | solution.py:143
  10.7 3.1 %all-to-all-done = bf16[8,16,896]{2,1,0:T(8,128)(2,1)S(1)} async-done(((bf16[8,16,896]{2,1,0:T(8,128)(2,1)}), bf16[8,16,896]{2,1,0:T(8,128)(2,1)S(1)}, u32[]{:S(2)}, u32[]{:S(2)}) %all-to-all-start) | async-done | bytes 229408 | tf_op jit(solution)/shard_map/all_to_all | solution.py:482
  14.3 2.7 %collective-permute-start.4 = (bf16[224,1792]{1,0:T(8,128)(2,1)}, bf16[224,1792]{1,0:T(8,128)(2,1)}, u32[]{:S(2)}, u32[]{:S(2)}) collective-permute-start(bf16[224,1792]{1,0:T(8,128)(2,1)} %bitcast.9.refs_0_), channel_id=1, source_target_pairs={{0,192},{32,224},{64,0},{96,32},{128,64},{160,96},{192,128},{224,1... | collective-permute-start | bytes 2408456 | tf_op jit(solution)/shard_map/ppermute | solution.py:463
  17.0 1.5 collective-permute-start.1
  18.5 1.8 collective-permute-start.2
  20.3 3.1 %copy-done = bf16[2,2048,896]{2,1,0:T(8,128)(2,1)S(1)} copy-done((bf16[2,2048,896]{2,1,0:T(8,128)(2,1)S(1)}, bf16[2,2048,896]{2,1,0:T(8,128)(2,1)}, u32[]{:S(2)}) %copy-start) | copy-done | bytes 7340056
  23.3 6.4 %shard_map.132 = bf16[8,240,128]{2,1,0:T(8,128)(2,1)} custom-call(s32[1]{0:T(128)} %bitcast.1.offset_ref, f32[1,8]{1,0:T(1,128)S(1)} %bitcast.21, bf16[128,896]{1,0:T(8,128)(2,1)S(1)} %bitcast.16, bf16[112,1024]{1,0:T(8,128)(2,1)S(1)} %shard_map.131.looked_ref, bf16[2,2048,896]{2,1,0:T(8,128)(2,1)S(1)} %copy-done), custom_call_target="tpu_custom_call" | custom-call | tf_op jit(solution)/shard_map/pallas_call | solution.py:111
  29.7 13.5 %collective-permute-done.refs_1_ = bf16[112,896]{1,0:T(8,128)(2,1)} collective-permute-done((bf16[112,896]{1,0:T(8,128)(2,1)}, bf16[112,896]{1,0:T(8,128)(2,1)}, u32[]{:S(2)}, u32[]{:S(2)}) %collective-permute-start) | collective-permute-done | bytes 200736 | tf_op jit(solution)/shard_map/ppermute | solution.py:463
  43.2 4.1 %all-to-all-start.1 = ((bf16[8,240,128]{2,1,0:T(8,128)(2,1)}), bf16[8,240,128]{2,1,0:T(8,128)(2,1)S(1)}, u32[]{:S(2)}, u32[]{:S(2)}) async-start(bf16[8,240,128]{2,1,0:T(8,128)(2,1)} %shard_map.132), calls=%async_computation.1 | async-start | bytes 983040 | tf_op jit(solution)/shard_map/all_to_all | solution.py:482
  49.3 1.1 shard_map.133
  50.4 6.9 %all-to-all-done.1.parts_ref = bf16[8,240,128]{2,1,0:T(8,128)(2,1)S(1)} async-done(((bf16[8,240,128]{2,1,0:T(8,128)(2,1)}), bf16[8,240,128]{2,1,0:T(8,128)(2,1)S(1)}, u32[]{:S(2)}, u32[]{:S(2)}) %all-to-all-start.1) | async-done | bytes 491552 | tf_op jit(solution)/shard_map/all_to_all | solution.py:482
  57.3 1.1 shard_map.134
  58.4 8.5 %all-to-all-start.2 = ((bf16[8,16,896]{2,1,0:T(8,128)(2,1)}), bf16[8,16,896]{2,1,0:T(8,128)(2,1)S(1)}, u32[]{:S(2)}, u32[]{:S(2)}) async-start(bf16[8,16,896]{2,1,0:T(8,128)(2,1)} %shard_map.134), calls=%async_computation.2 | async-start | bytes 458752 | tf_op jit(solution)/shard_map/all_to_all | solution.py:482
  66.9 0.8 slice.12
  68.2 1.8 slice.13
  70.0 2.7 %collective-permute-start.10 = (bf16[112,1792]{1,0:T(8,128)(2,1)}, bf16[112,1792]{1,0:T(8,128)(2,1)}, u32[]{:S(2)}, u32[]{:S(2)}) collective-permute-start(bf16[112,1792]{1,0:T(8,128)(2,1)} %slice.13), channel_id=1, source_target_pairs={{0,192},{32,224},{64,0},{96,32},{128,64},{160,96},{192,128},{224,1... | collective-permute-start | bytes 1204232 | tf_op jit(solution)/shard_map/ppermute | solution.py:463
  72.7 3.2 %collective-permute-start.12 = (bf16[224,1792]{1,0:T(8,128)(2,1)}, bf16[224,1792]{1,0:T(8,128)(2,1)S(1)}, u32[]{:S(2)}, u32[]{:S(2)}) collective-permute-start(bf16[224,1792]{1,0:T(8,128)(2,1)} %refs_0_), channel_id=1, source_target_pairs={{0,192},{32,224},{64,0},{96,32},{128,64},{160,96},{192,128},{224,1... | collective-permute-start | bytes 2408456 | tf_op jit(solution)/shard_map/ppermute | solution.py:463
  75.9 1.7 collective-permute-done.8.refs_7_
  78.3 0.9 copy-done.15
  79.2 0.9 copy-done.17
  80.1 2.9 %shard_map.135 = bf16[32,2,16,128]{3,2,1,0:T(8,128)(2,1)} custom-call(s32[1]{0:T(128)} %bitcast.ctx_ref, bf16[8,16,896]{2,1,0:T(8,128)(2,1)S(1)} %all-to-all-done.2.rows_ref, bf16[8,240,128]{2,1,0:T(8,128)(2,1)S(1)} %all-to-all-done.1.parts_ref, bf16[112,896]{1,0:T(8,128)(2,1)} %bitcast.6.refs_0_, bf16[112,896]{1,0:T(8,128)(2,1)} %collective-permute-done.refs_1_, ...), custom_call_target="tpu_custom_call" | custom-call | tf_op jit(solution)/shard_map/pallas_call | solution.py:309
  83.1 10.4 %all-to-all-start.3 = ((bf16[32,2,16,128]{3,2,1,0:T(8,128)(2,1)}), bf16[32,2,16,128]{3,2,1,0:T(8,128)(2,1)S(1)}, u32[]{:S(2)}, u32[]{:S(2)}) async-start(bf16[32,2,16,128]{3,2,1,0:T(8,128)(2,1)} %shard_map.135), calls=%async_computation.3 | async-start | bytes 524288 | tf_op jit(solution)/shard_map/all_to_all | solution.py:482
  93.5 11.5 %all-to-all-done.3.parts_ref = bf16[32,2,16,128]{3,2,1,0:T(8,128)(2,1)S(1)} async-done(((bf16[32,2,16,128]{3,2,1,0:T(8,128)(2,1)}), bf16[32,2,16,128]{3,2,1,0:T(8,128)(2,1)S(1)}, u32[]{:S(2)}, u32[]{:S(2)}) %all-to-all-start.3) | async-done | bytes 262176 | tf_op jit(solution)/shard_map/all_to_all | solution.py:482
  105.0 0.8 shard_map.136
  106.6 3.5 %all-to-all-start.4 = ((bf16[8,16,1920]{2,1,0:T(8,128)(2,1)}), bf16[8,16,1920]{2,1,0:T(8,128)(2,1)S(1)}, u32[]{:S(2)}, u32[]{:S(2)}) async-start(bf16[8,16,1920]{2,1,0:T(8,128)(2,1)} %copy-done.9), calls=%async_computation.4 | async-start | bytes 983040 | tf_op jit(solution)/shard_map/all_to_all | solution.py:482
  112.0 0.8 slice.15
  112.8 3.0 %collective-permute-done.16.refs_8_ = bf16[112,1792]{1,0:T(8,128)(2,1)S(1)} collective-permute-done((bf16[112,1792]{1,0:T(8,128)(2,1)S(1)}, bf16[112,1792]{1,0:T(8,128)(2,1)S(1)}, u32[]{:S(2)}, u32[]{:S(2)}) %collective-permute-start.16) | collective-permute-done | bytes 401440 | tf_op jit(solution)/shard_map/ppermute | solution.py:468
  117.3 3.2 %collective-permute-start.19 = (bf16[112,1792]{1,0:T(8,128)(2,1)}, bf16[112,1792]{1,0:T(8,128)(2,1)}, u32[]{:S(2)}, u32[]{:S(2)}) collective-permute-start(bf16[112,1792]{1,0:T(8,128)(2,1)} %slice.15), channel_id=1, source_target_pairs={{0,192},{32,224},{64,0},{96,32},{128,64},{160,96},{192,128},{224,1... | collective-permute-start | bytes 1204232 | tf_op jit(solution)/shard_map/ppermute | solution.py:463
  120.5 0.9 copy-done.3
  121.4 0.9 copy-done.5
  122.3 0.9 copy-done.7
  123.2 2.5 %all-to-all-done.4 = bf16[8,16,1920]{2,1,0:T(8,128)(2,1)S(1)} async-done(((bf16[8,16,1920]{2,1,0:T(8,128)(2,1)}), bf16[8,16,1920]{2,1,0:T(8,128)(2,1)S(1)}, u32[]{:S(2)}, u32[]{:S(2)}) %all-to-all-start.4) | async-done | bytes 491552 | tf_op jit(solution)/shard_map/all_to_all | solution.py:482
  125.7 1.1 copy-done.4
  126.9 1.1 copy-done.6
  128.0 1.1 copy-done.8
  129.2 1.0 copy-done.11
  130.2 1.0 copy-done.13
  131.1 4.2 %shard_map.137 = bf16[4,464,128]{2,1,0:T(8,128)(2,1)} custom-call(bf16[128,1920]{1,0:T(8,128)(2,1)S(1)} %bitcast.13, bf16[224,1792]{1,0:T(8,128)(2,1)} %bitcast.9.refs_0_, bf16[224,1792]{1,0:T(8,128)(2,1)S(1)} %collective-permute-done.3.refs_1_, bf16[224,1792]{1,0:T(8,128)(2,1)} %collective-permute-done.4.refs_2_, ...), custom_call_target="tpu_custom_call" | custom-call | tf_op jit(solution)/shard_map/pallas_call | solution.py:376
  136.0 5.1 %all-to-all-start.5 = ((bf16[4,464,128]{2,1,0:T(8,128)(2,1)}), bf16[4,464,128]{2,1,0:T(8,128)(2,1)S(1)}, u32[]{:S(2)}, u32[]{:S(2)}) async-start(bf16[4,464,128]{2,1,0:T(8,128)(2,1)} %shard_map.137), calls=%async_computation.5 | async-start | bytes 950272 | tf_op jit(solution)/shard_map/all_to_all | solution.py:482
  141.6 7.9 %all-to-all-done.5.parts_ref = bf16[4,464,128]{2,1,0:T(8,128)(2,1)S(1)} async-done(((bf16[4,464,128]{2,1,0:T(8,128)(2,1)}), bf16[4,464,128]{2,1,0:T(8,128)(2,1)S(1)}, u32[]{:S(2)}, u32[]{:S(2)}) %all-to-all-start.5) | async-done | bytes 475168 | tf_op jit(solution)/shard_map/all_to_all | solution.py:482
  149.5 0.9 shard_map.138
  150.3 4.9 %all-to-all-start.6 = ((bf16[4,448,128]{2,1,0:T(8,128)(2,1)}), bf16[4,448,128]{2,1,0:T(8,128)(2,1)S(1)}, u32[]{:S(2)}, u32[]{:S(2)}) async-start(bf16[4,448,128]{2,1,0:T(8,128)(2,1)} %shard_map.138), calls=%async_computation.6 | async-start | bytes 917504 | tf_op jit(solution)/shard_map/all_to_all | solution.py:482
  155.3 7.4 %all-to-all-done.6.hidden_ref = bf16[4,448,128]{2,1,0:T(8,128)(2,1)S(1)} async-done(((bf16[4,448,128]{2,1,0:T(8,128)(2,1)}), bf16[4,448,128]{2,1,0:T(8,128)(2,1)S(1)}, u32[]{:S(2)}, u32[]{:S(2)}) %all-to-all-start.6) | async-done | bytes 458784 | tf_op jit(solution)/shard_map/all_to_all | solution.py:482
  162.7 3.4 %shard_map.139 = bf16[8,16,1792]{2,1,0:T(8,128)(2,1)S(1)} custom-call(bf16[4,448,128]{2,1,0:T(8,128)(2,1)S(1)} %all-to-all-done.6.hidden_ref, bf16[224,1792]{1,0:T(8,128)(2,1)} %refs_0_, bf16[224,1792]{1,0:T(8,128)(2,1)S(1)} %collective-permute-done.11.refs_1_, bf16[224,1792]{1,0:T(8,128)(2,1)S(1)} %collective-permute-done.12.refs_2_, ...), custom_call_target="tpu_custom_call" | custom-call | tf_op jit(solution)/shard_map/pallas_call | solution.py:428
  166.0 19.1 %all_to_all.40.parts_ref = bf16[8,16,1792]{2,1,0:T(8,128)(2,1)S(1)} all-to-all(bf16[8,16,1792]{2,1,0:T(8,128)(2,1)S(1)} %shard_map.139), channel_id=1, replica_groups=mesh['ctx'=8,'req'=8,'mp'=4] {'req'}, dimensions={0} | all-to-all | bytes 917504 | tf_op jit(solution)/shard_map/all_to_all | solution.py:482
  (82 shorter events, 10.2 us)
Async XLA Ops:
  0.6 19.6 %copy-start.21 = (f32[8]{0:T(128)S(1)}, f32[8]{0:T(128)}, u32[]{:S(2)}) copy-start(f32[8]{0:T(128)} %param.19) | copy-start | bytes 100
  2.1 11.7 %all-to-all-start = ((bf16[8,16,896]{2,1,0:T(8,128)(2,1)}), bf16[8,16,896]{2,1,0:T(8,128)(2,1)S(1)}, u32[]{:S(2)}, u32[]{:S(2)}) async-start(bf16[8,16,896]{2,1,0:T(8,128)(2,1)} %broadcast_in_dim.22), calls=%async_computation | async-start | bytes 458752 | tf_op jit(solution)/shard_map/all_to_all | solution.py:482
  7.5 1.4 copy-start.2
  13.8 44.6 %collective-permute-start.3 = (bf16[224,1792]{1,0:T(8,128)(2,1)}, bf16[224,1792]{1,0:T(8,128)(2,1)S(1)}, u32[]{:S(2)}, u32[]{:S(2)}) collective-permute-start(bf16[224,1792]{1,0:T(8,128)(2,1)} %bitcast.9.refs_0_), channel_id=1, source_target_pairs={{0,64},{32,96},{64,128},{96,160},{128,192},{160,224},{192,0},{224,... | collective-permute-start | bytes 2408456 | tf_op jit(solution)/shard_map/ppermute | solution.py:463
  14.3 44.1 %collective-permute-start.4 = (bf16[224,1792]{1,0:T(8,128)(2,1)}, bf16[224,1792]{1,0:T(8,128)(2,1)}, u32[]{:S(2)}, u32[]{:S(2)}) collective-permute-start(bf16[224,1792]{1,0:T(8,128)(2,1)} %bitcast.9.refs_0_), channel_id=1, source_target_pairs={{0,192},{32,224},{64,0},{96,32},{128,64},{160,96},{192,128},{224,1... | collective-permute-start | bytes 2408456 | tf_op jit(solution)/shard_map/ppermute | solution.py:463
  17.0 26.2 %collective-permute-start = (bf16[112,896]{1,0:T(8,128)(2,1)}, bf16[112,896]{1,0:T(8,128)(2,1)}, u32[]{:S(2)}, u32[]{:S(2)}) collective-permute-start(bf16[112,896]{1,0:T(8,128)(2,1)} %bitcast.6.refs_0_), channel_id=1, source_target_pairs={{0,64},{32,96},{64,128},{96,160},{128,192},{160,224},{192,0},{224,... | collective-permute-start | bytes 602120 | tf_op jit(solution)/shard_map/ppermute | solution.py:463
  17.0 26.2 %collective-permute-start.1 = (bf16[112,896]{1,0:T(8,128)(2,1)}, bf16[112,896]{1,0:T(8,128)(2,1)}, u32[]{:S(2)}, u32[]{:S(2)}) collective-permute-start(bf16[112,896]{1,0:T(8,128)(2,1)} %bitcast.6.refs_0_), channel_id=1, source_target_pairs={{0,128},{32,160},{64,192},{96,224},{128,0},{160,32},{192,64},{224,... | collective-permute-start | bytes 602120 | tf_op jit(solution)/shard_map/ppermute | solution.py:463
  18.5 24.7 %collective-permute-start.2 = (bf16[112,896]{1,0:T(8,128)(2,1)}, bf16[112,896]{1,0:T(8,128)(2,1)S(1)}, u32[]{:S(2)}, u32[]{:S(2)}) collective-permute-start(bf16[112,896]{1,0:T(8,128)(2,1)} %bitcast.6.refs_0_), channel_id=1, source_target_pairs={{0,192},{32,224},{64,0},{96,32},{128,64},{160,96},{192,128},{224,1... | collective-permute-start | bytes 602120 | tf_op jit(solution)/shard_map/ppermute | solution.py:463
  20.3 3.1 %copy-start = (bf16[2,2048,896]{2,1,0:T(8,128)(2,1)S(1)}, bf16[2,2048,896]{2,1,0:T(8,128)(2,1)}, u32[]{:S(2)}) copy-start(bf16[2,2048,896]{2,1,0:T(8,128)(2,1)} %prefix_ref.1) | copy-start | bytes 22020100
  23.3 25.9 %copy-start.1 = (bf16[2,1,512,896]{3,2,1,0:T(8,128)(2,1)S(1)}, bf16[2,1,512,896]{3,2,1,0:T(8,128)(2,1)}, u32[]{:S(2)}) copy-start(bf16[2,1,512,896]{3,2,1,0:T(8,128)(2,1)} %param.17) | copy-start | bytes 5505028
  23.3 25.9 %copy-start.18 = (bf16[1,16,896]{2,1,0:T(8,128)(2,1)S(1)}, bf16[1,16,896]{2,1,0:T(8,128)(2,1)}, u32[]{:S(2)}) copy-start(bf16[1,16,896]{2,1,0:T(8,128)(2,1)} %param.14) | copy-start | bytes 86020
  23.3 25.9 %copy-start.20 = (bf16[2,1,16,896]{3,2,1,0:T(8,128)(2,1)S(1)}, bf16[2,1,16,896]{3,2,1,0:T(8,128)(2,1)}, u32[]{:S(2)}) copy-start(bf16[2,1,16,896]{3,2,1,0:T(8,128)(2,1)} %param.15) | copy-start | bytes 172036
  43.2 23.7 %copy-start.14 = (bf16[112,896]{1,0:T(8,128)(2,1)}, bf16[112,896]{1,0:T(8,128)(2,1)S(1)}, u32[]{:S(2)}) copy-start(bf16[112,896]{1,0:T(8,128)(2,1)S(1)} %collective-permute-done.2.refs_3_) | copy-start | bytes 602116
  43.2 14.1 %all-to-all-start.1 = ((bf16[8,240,128]{2,1,0:T(8,128)(2,1)}), bf16[8,240,128]{2,1,0:T(8,128)(2,1)S(1)}, u32[]{:S(2)}, u32[]{:S(2)}) async-start(bf16[8,240,128]{2,1,0:T(8,128)(2,1)} %shard_map.132), calls=%async_computation.1 | async-start | bytes 983040 | tf_op jit(solution)/shard_map/all_to_all | solution.py:482
  47.3 25.3 %collective-permute-start.5 = (bf16[112,896]{1,0:T(8,128)(2,1)}, bf16[112,896]{1,0:T(8,128)(2,1)}, u32[]{:S(2)}, u32[]{:S(2)}) collective-permute-start(bf16[112,896]{1,0:T(8,128)(2,1)} %bitcast.6.refs_0_), channel_id=1, source_target_pairs={{0,32},{32,0},{64,96},{96,64},{128,160},{160,128},{192,224},{224,1... | collective-permute-start | bytes 602120 | tf_op jit(solution)/shard_map/ppermute | solution.py:468
  47.8 24.8 %collective-permute-start.6 = (bf16[112,896]{1,0:T(8,128)(2,1)}, bf16[112,896]{1,0:T(8,128)(2,1)}, u32[]{:S(2)}, u32[]{:S(2)}) collective-permute-start(bf16[112,896]{1,0:T(8,128)(2,1)} %collective-permute-done.refs_1_), channel_id=1, source_target_pairs={{0,32},{32,0},{64,96},{96,64},{128,160},{160,128},{192,224},{224,1... | collective-permute-start | bytes 602120 | tf_op jit(solution)/shard_map/ppermute | solution.py:468
  48.5 27.4 %collective-permute-start.7 = (bf16[112,896]{1,0:T(8,128)(2,1)}, bf16[112,896]{1,0:T(8,128)(2,1)}, u32[]{:S(2)}, u32[]{:S(2)}) collective-permute-start(bf16[112,896]{1,0:T(8,128)(2,1)} %collective-permute-done.1.refs_2_), channel_id=1, source_target_pairs={{0,32},{32,0},{64,96},{96,64},{128,160},{160,128},{192,224},{224,1... | collective-permute-start | bytes 602120 | tf_op jit(solution)/shard_map/ppermute | solution.py:468
  58.4 19.8 %all-to-all-start.2 = ((bf16[8,16,896]{2,1,0:T(8,128)(2,1)}), bf16[8,16,896]{2,1,0:T(8,128)(2,1)S(1)}, u32[]{:S(2)}, u32[]{:S(2)}) async-start(bf16[8,16,896]{2,1,0:T(8,128)(2,1)} %shard_map.134), calls=%async_computation.2 | async-start | bytes 458752 | tf_op jit(solution)/shard_map/all_to_all | solution.py:482
  67.7 25.8 %copy-start.22 = (f32[1792]{0:T(1024)S(1)}, f32[1792]{0:T(1024)}, u32[]{:S(2)}) copy-start(f32[1792]{0:T(1024)} %param.21) | copy-start | bytes 21508
  67.7 15.4 %collective-permute-start.9 = (bf16[112,1792]{1,0:T(8,128)(2,1)}, bf16[112,1792]{1,0:T(8,128)(2,1)S(1)}, u32[]{:S(2)}, u32[]{:S(2)}) collective-permute-start(bf16[112,1792]{1,0:T(8,128)(2,1)} %slice.12), channel_id=1, source_target_pairs={{0,64},{32,96},{64,128},{96,160},{128,192},{160,224},{192,0},{224,... | collective-permute-start | bytes 1204232 | tf_op jit(solution)/shard_map/ppermute | solution.py:463
  70.0 13.1 %collective-permute-start.10 = (bf16[112,1792]{1,0:T(8,128)(2,1)}, bf16[112,1792]{1,0:T(8,128)(2,1)}, u32[]{:S(2)}, u32[]{:S(2)}) collective-permute-start(bf16[112,1792]{1,0:T(8,128)(2,1)} %slice.13), channel_id=1, source_target_pairs={{0,192},{32,224},{64,0},{96,32},{128,64},{160,96},{192,128},{224,1... | collective-permute-start | bytes 1204232 | tf_op jit(solution)/shard_map/ppermute | solution.py:463
  72.7 33.1 %collective-permute-start.11 = (bf16[224,1792]{1,0:T(8,128)(2,1)}, bf16[224,1792]{1,0:T(8,128)(2,1)S(1)}, u32[]{:S(2)}, u32[]{:S(2)}) collective-permute-start(bf16[224,1792]{1,0:T(8,128)(2,1)} %refs_0_), channel_id=1, source_target_pairs={{0,64},{32,96},{64,128},{96,160},{128,192},{160,224},{192,0},{224,... | collective-permute-start | bytes 2408456 | tf_op jit(solution)/shard_map/ppermute | solution.py:463
  72.7 33.1 %collective-permute-start.12 = (bf16[224,1792]{1,0:T(8,128)(2,1)}, bf16[224,1792]{1,0:T(8,128)(2,1)S(1)}, u32[]{:S(2)}, u32[]{:S(2)}) collective-permute-start(bf16[224,1792]{1,0:T(8,128)(2,1)} %refs_0_), channel_id=1, source_target_pairs={{0,192},{32,224},{64,0},{96,32},{128,64},{160,96},{192,128},{224,1... | collective-permute-start | bytes 2408456 | tf_op jit(solution)/shard_map/ppermute | solution.py:463
  75.9 1.7 collective-permute-start.8
  78.3 0.9 copy-start.15
  79.2 0.9 copy-start.17
  83.1 21.9 %all-to-all-start.3 = ((bf16[32,2,16,128]{3,2,1,0:T(8,128)(2,1)}), bf16[32,2,16,128]{3,2,1,0:T(8,128)(2,1)S(1)}, u32[]{:S(2)}, u32[]{:S(2)}) async-start(bf16[32,2,16,128]{3,2,1,0:T(8,128)(2,1)} %shard_map.135), calls=%async_computation.3 | async-start | bytes 524288 | tf_op jit(solution)/shard_map/all_to_all | solution.py:482
  106.6 19.2 %all-to-all-start.4 = ((bf16[8,16,1920]{2,1,0:T(8,128)(2,1)}), bf16[8,16,1920]{2,1,0:T(8,128)(2,1)S(1)}, u32[]{:S(2)}, u32[]{:S(2)}) async-start(bf16[8,16,1920]{2,1,0:T(8,128)(2,1)} %copy-done.9), calls=%async_computation.4 | async-start | bytes 983040 | tf_op jit(solution)/shard_map/all_to_all | solution.py:482
  110.1 10.5 %collective-permute-start.13 = (bf16[224,1792]{1,0:T(8,128)(2,1)}, bf16[224,1792]{1,0:T(8,128)(2,1)S(1)}, u32[]{:S(2)}, u32[]{:S(2)}) collective-permute-start(bf16[224,1792]{1,0:T(8,128)(2,1)} %bitcast.9.refs_0_), channel_id=1, source_target_pairs={{0,32},{32,0},{64,96},{96,64},{128,160},{160,128},{192,224},{224,1... | collective-permute-start | bytes 2408456 | tf_op jit(solution)/shard_map/ppermute | solution.py:468
  110.2 11.3 %collective-permute-start.14 = (bf16[224,1792]{1,0:T(8,128)(2,1)S(1)}, bf16[224,1792]{1,0:T(8,128)(2,1)S(1)}, u32[]{:S(2)}, u32[]{:S(2)}) collective-permute-start(bf16[224,1792]{1,0:T(8,128)(2,1)S(1)} %collective-permute-done.3.refs_1_), channel_id=1, source_target_pairs={{0,32},{32,0},{64,96},{96,64},{128,160},{160,128},{192,224},{224,1... | collective-permute-start | bytes 2408456 | tf_op jit(solution)/shard_map/ppermute | solution.py:468
  110.7 11.7 %collective-permute-start.15 = (bf16[224,1792]{1,0:T(8,128)(2,1)}, bf16[224,1792]{1,0:T(8,128)(2,1)S(1)}, u32[]{:S(2)}, u32[]{:S(2)}) collective-permute-start(bf16[224,1792]{1,0:T(8,128)(2,1)} %collective-permute-done.4.refs_2_), channel_id=1, source_target_pairs={{0,32},{32,0},{64,96},{96,64},{128,160},{160,128},{192,224},{224,1... | collective-permute-start | bytes 2408456 | tf_op jit(solution)/shard_map/ppermute | solution.py:468
  110.8 5.0 %collective-permute-start.16 = (bf16[112,1792]{1,0:T(8,128)(2,1)S(1)}, bf16[112,1792]{1,0:T(8,128)(2,1)S(1)}, u32[]{:S(2)}, u32[]{:S(2)}) collective-permute-start(bf16[112,1792]{1,0:T(8,128)(2,1)S(1)} %collective-permute-done.9.refs_3_), channel_id=1, source_target_pairs={{0,32},{32,0},{64,96},{96,64},{128,160},{160,128},{192,224},{224,1... | collective-permute-start | bytes 1204232 | tf_op jit(solution)/shard_map/ppermute | solution.py:468
  111.2 5.4 %collective-permute-start.17 = (bf16[112,1792]{1,0:T(8,128)(2,1)}, bf16[112,1792]{1,0:T(8,128)(2,1)S(1)}, u32[]{:S(2)}, u32[]{:S(2)}) collective-permute-start(bf16[112,1792]{1,0:T(8,128)(2,1)} %collective-permute-done.10.refs_4_), channel_id=1, source_target_pairs={{0,32},{32,0},{64,96},{96,64},{128,160},{160,128},{192,224},{224,1... | collective-permute-start | bytes 1204232 | tf_op jit(solution)/shard_map/ppermute | solution.py:468
  116.5 18.8 %collective-permute-start.18 = (bf16[112,1792]{1,0:T(8,128)(2,1)}, bf16[112,1792]{1,0:T(8,128)(2,1)}, u32[]{:S(2)}, u32[]{:S(2)}) collective-permute-start(bf16[112,1792]{1,0:T(8,128)(2,1)} %slice.14), channel_id=1, source_target_pairs={{0,64},{32,96},{64,128},{96,160},{128,192},{160,224},{192,0},{224,... | collective-permute-start | bytes 1204232 | tf_op jit(solution)/shard_map/ppermute | solution.py:463
  117.3 18.0 %collective-permute-start.19 = (bf16[112,1792]{1,0:T(8,128)(2,1)}, bf16[112,1792]{1,0:T(8,128)(2,1)}, u32[]{:S(2)}, u32[]{:S(2)}) collective-permute-start(bf16[112,1792]{1,0:T(8,128)(2,1)} %slice.15), channel_id=1, source_target_pairs={{0,192},{32,224},{64,0},{96,32},{128,64},{160,96},{192,128},{224,1... | collective-permute-start | bytes 1204232 | tf_op jit(solution)/shard_map/ppermute | solution.py:463
  125.7 1.1 copy-start.4
  126.9 1.1 copy-start.6
  128.0 1.1 copy-start.8
  129.1 1.0 copy-start.11
  130.1 1.0 copy-start.13
  135.3 27.3 %collective-permute-start.20 = (bf16[224,1792]{1,0:T(8,128)(2,1)}, bf16[224,1792]{1,0:T(8,128)(2,1)S(1)}, u32[]{:S(2)}, u32[]{:S(2)}) collective-permute-start(bf16[224,1792]{1,0:T(8,128)(2,1)} %refs_0_), channel_id=1, source_target_pairs={{0,32},{32,0},{64,96},{96,64},{128,160},{160,128},{192,224},{224,1... | collective-permute-start | bytes 2408456 | tf_op jit(solution)/shard_map/ppermute | solution.py:468
  135.4 27.2 %collective-permute-start.21 = (bf16[224,1792]{1,0:T(8,128)(2,1)S(1)}, bf16[224,1792]{1,0:T(8,128)(2,1)}, u32[]{:S(2)}, u32[]{:S(2)}) collective-permute-start(bf16[224,1792]{1,0:T(8,128)(2,1)S(1)} %collective-permute-done.11.refs_1_), channel_id=1, source_target_pairs={{0,32},{32,0},{64,96},{96,64},{128,160},{160,128},{192,224},{224,1... | collective-permute-start | bytes 2408456 | tf_op jit(solution)/shard_map/ppermute | solution.py:468
  135.9 26.7 %collective-permute-start.22 = (bf16[224,1792]{1,0:T(8,128)(2,1)S(1)}, bf16[224,1792]{1,0:T(8,128)(2,1)}, u32[]{:S(2)}, u32[]{:S(2)}) collective-permute-start(bf16[224,1792]{1,0:T(8,128)(2,1)S(1)} %collective-permute-done.12.refs_2_), channel_id=1, source_target_pairs={{0,32},{32,0},{64,96},{96,64},{128,160},{160,128},{192,224},{224,1... | collective-permute-start | bytes 2408456 | tf_op jit(solution)/shard_map/ppermute | solution.py:468
  136.0 13.4 %all-to-all-start.5 = ((bf16[4,464,128]{2,1,0:T(8,128)(2,1)}), bf16[4,464,128]{2,1,0:T(8,128)(2,1)S(1)}, u32[]{:S(2)}, u32[]{:S(2)}) async-start(bf16[4,464,128]{2,1,0:T(8,128)(2,1)} %shard_map.137), calls=%async_computation.5 | async-start | bytes 950272 | tf_op jit(solution)/shard_map/all_to_all | solution.py:482
  141.1 14.2 %collective-permute-start.23 = (bf16[112,1792]{1,0:T(8,128)(2,1)}, bf16[112,1792]{1,0:T(8,128)(2,1)S(1)}, u32[]{:S(2)}, u32[]{:S(2)}) collective-permute-start(bf16[112,1792]{1,0:T(8,128)(2,1)} %collective-permute-done.18.refs_3_), channel_id=1, source_target_pairs={{0,32},{32,0},{64,96},{96,64},{128,160},{160,128},{192,224},{224,1... | collective-permute-start | bytes 1204232 | tf_op jit(solution)/shard_map/ppermute | solution.py:468
  141.2 14.0 %collective-permute-start.24 = (bf16[112,1792]{1,0:T(8,128)(2,1)}, bf16[112,1792]{1,0:T(8,128)(2,1)}, u32[]{:S(2)}, u32[]{:S(2)}) collective-permute-start(bf16[112,1792]{1,0:T(8,128)(2,1)} %collective-permute-done.19.refs_4_), channel_id=1, source_target_pairs={{0,32},{32,0},{64,96},{96,64},{128,160},{160,128},{192,224},{224,1... | collective-permute-start | bytes 1204232 | tf_op jit(solution)/shard_map/ppermute | solution.py:468
  150.3 12.3 %all-to-all-start.6 = ((bf16[4,448,128]{2,1,0:T(8,128)(2,1)}), bf16[4,448,128]{2,1,0:T(8,128)(2,1)S(1)}, u32[]{:S(2)}, u32[]{:S(2)}) async-start(bf16[4,448,128]{2,1,0:T(8,128)(2,1)} %shard_map.138), calls=%async_computation.6 | async-start | bytes 917504 | tf_op jit(solution)/shard_map/all_to_all | solution.py:482
  155.2 29.9 %copy-start.19 = (f32[16,1792]{1,0:T(8,128)S(1)}, f32[16,1792]{1,0:T(8,128)}, u32[]{:S(2)}) copy-start(f32[16,1792]{1,0:T(8,128)} %get-tuple-element.54.residual_ref) | copy-start | bytes 344068
  (7 other events, 5.7 us)

commit v9 on v8

--- a/solution.py
+++ b/solution.py
@@ -352,34 +352,34 @@
     )(parts, gain[None, :])
 
 
-def lift_kernel(rows_ref, *refs):
-    *weight_refs, out_ref = refs
-    width = weight_refs[0].shape[1]
+def lift_kernel(ctx_ref, rows_ref, weight_ref, out_ref):
+    blocks, hidden, width = weight_ref.shape
     mp, height, _ = out_ref.shape
-    held = sum(ref.shape[0] for ref in weight_refs) // mp
+    pair = blocks // mp
     rows = rows_ref[:, :width]
-    first = 0
-    for ref in weight_refs:
-        piece, place = divmod(first, held)
-        out_ref[piece, place : place + ref.shape[0]] = lax.dot_general(
-            ref[...], rows, (((1,), (1,)), ((), ())), preferred_element_type=F32
+    for place in range(blocks):
+        other, step = divmod(place, blocks // 2)
+        step = (0, blocks - 2, 2, 4)[step]
+        block = lax.rem(ctx_ref[0] + step, blocks) ^ other
+        piece, line = divmod(place, pair)
+        out_ref[piece, line * hidden : (line + 1) * hidden] = lax.dot_general(
+            weight_ref[block], rows, (((1,), (1,)), ((), ())), preferred_element_type=F32
         ).astype(BF16)
-        first += ref.shape[0]
     squares = jnp.transpose(rows_ref[:, width:].astype(F32)).astype(BF16)
     for piece in range(mp):
-        out_ref[piece, held:] = squares[: height - held]
-
-
-def lift_rows(rows, weights, mp):
-    held = sum(weight.shape[0] for weight in weights) // mp
+        out_ref[piece, pair * hidden :] = squares[: height - pair * hidden]
+
+
+def lift_rows(rows, weight, ctx_index, mp):
+    blocks, hidden, _ = weight.shape
     vmem = pl.BlockSpec(memory_space=pltpu.VMEM)
     return pl.pallas_call(
         lift_kernel,
-        out_shape=jax.ShapeDtypeStruct((mp, held + 16, rows.shape[0]), BF16),
-        in_specs=[vmem] * (1 + len(weights)),
+        out_shape=jax.ShapeDtypeStruct((mp, blocks // mp * hidden + 16, rows.shape[0]), BF16),
+        in_specs=[pl.BlockSpec(memory_space=pltpu.SMEM), vmem, vmem],
         out_specs=vmem,
         compiler_params=pltpu.CompilerParams(vmem_limit_bytes=20 * MIB),
-    )(rows, *weights)
+    )(ctx_index, rows, weight)
 
 
 def gelu_kernel(parts_ref, out_ref, *, model_width):
@@ -514,8 +514,6 @@
     gathered, looked_up = lax.optimization_barrier((gathered, looked_up))
     out_blocks = [after(out_weight.T, looked_up)]
     out_blocks += [shifted_by(out_blocks[0], step) for step in range(2, ctx_count, 2)]
-    up_blocks = nearest(after(up_weight.T, looked_up))
-
     offset = (prompt_local * (ctx_count - ctx_index)).astype(jnp.int32).reshape(1)
     parts = prompt_part(
         gathered.reshape(ctx_count * draft, width),
@@ -532,17 +530,13 @@
     parts = exchange(parts, "ctx")
     out_blocks += beside(out_blocks)
     merged = merge_parts(parts, own, own_level, heads, req_count)
-    merged, *up_blocks = lax.optimization_barrier((merged, *up_blocks))
+    up_all = lax.all_gather(after(up_weight, merged).T, "ctx")
     attended = exchange(merged, "req")
-    up_blocks += farthest(up_blocks)
-    down_blocks = nearest(after(down_weight, merged))
-
-    pieces = project_rows(
-        attended, out_blocks, parts, ctx_index.astype(jnp.int32).reshape(1), mp_count
-    )
-    pieces, *up_blocks = lax.optimization_barrier((pieces, *up_blocks))
+
+    ctx_number = ctx_index.astype(jnp.int32).reshape(1)
+    pieces = project_rows(attended, out_blocks, parts, ctx_number, mp_count)
+    down_blocks = nearest(after(down_weight, pieces))
     pieces = exchange(pieces, ("req", "mp"))
-    up_blocks += beside(up_blocks)
     residual, centred = residual_rows(
         pieces, ln_gain, mp_count, draft, out_weight.shape[1], req_count
     )
@@ -550,7 +544,7 @@
     centred = exchange(centred, "req").reshape(req_count * draft, -1)
     down_blocks += farthest(down_blocks)
 
-    lifted = lift_rows(centred, up_blocks, mp_count)
+    lifted = lift_rows(centred, up_all, ctx_number, mp_count)
     lifted, *down_blocks = lax.optimization_barrier((lifted, *down_blocks))
     lifted = exchange(lifted, "mp")
     down_blocks += beside(down_blocks)

time: 187 us -> 189 us (1.011)
  waiting for transfers between devices: 57.4 us -> 71.7 us
  between operations: 1.45 us -> 14.8 us
  starting transfers between devices: 60.7 us -> 47.6 us
  local copies, waits for them, and re-layouts: 23.1 us -> 14.3 us
  Pallas kernels: 23.3 us -> 21.2 us
  blocking collectives: 19.1 us -> 17 us
    all_to_all x7, waiting for transfers between devices: 39.2 us -> 51.5 us  [exchange(): return lax.all_to_all(value, axis, split_axis=0, concat_axis=0, tiled=True)]
    ppermute x11 -> x7, starting transfers between devices: 16.2 us -> 9.71 us  [shifted_by(): lax.ppermute(block, 'ctx', [(i, (i + step) % count) for i in range(count)])]
    unnamed x46 -> x28, local copies, waits for them, and re-layouts: 17.4 us -> 10.9 us
    all_to_all x7, starting transfers between devices: 40.9 us -> 35.5 us  [exchange(): return lax.all_to_all(value, axis, split_axis=0, concat_axis=0, tiled=True)]
    ppermute x11 -> x7, waiting for transfers between devices: 13.5 us -> 18.7 us  [shifted_by(): lax.ppermute(block, 'ctx', [(i, (i + step) % count) for i in range(count)])]
    ppermute x14 -> x9, waiting for transfers between devices: 4.65 us -> 1.51 us  [beside(): lax.ppermute(block, 'ctx', [(i, i ^ 1) for i in range(count)])]
    slice x4 -> x2, local copies, waits for them, and re-layouts: 4.1 us -> 1.62 us  [farthest(): return [shifted_by(back[:half], 2), shifted_by(on[half:], -2)]]
    all_to_all x1, blocking collectives: 19.1 us -> 17 us  [exchange(): return lax.all_to_all(value, axis, split_axis=0, concat_axis=0, tiled=True)]
  transfers between devices with their start and end apart: 32 -> 24, of which waited for: 9 -> 12; matrix products, arithmetic and copies ran while one was open for 3% -> 1% of each run, Pallas kernels for 10% -> 9%
where the time goes in v9:
time: 189 us; the launch traced here: 187 us
  waiting for transfers between devices  71.7 us (38%)
  starting transfers between devices  47.6 us (25%)
  Pallas kernels  21.2 us (11%)
  blocking collectives  17 us (9%)
  between operations  14.8 us (8%)
  local copies, waits for them, and re-layouts  14.3 us (8%)
    all_to_all x7, waiting for transfers between devices, exchange(): return lax.all_to_all(value, axis, split_axis=0, concat_axis=0, tiled=True)  51.5 us
    all_to_all x7, starting transfers between devices, exchange(): return lax.all_to_all(value, axis, split_axis=0, concat_axis=0, tiled=True)  35.5 us
    ppermute x7, waiting for transfers between devices, shifted_by(): lax.ppermute(block, 'ctx', [(i, (i + step) % count) for i in range(count)])  18.7 us
    all_to_all x1, blocking collectives, exchange(): return lax.all_to_all(value, axis, split_axis=0, concat_axis=0, tiled=True)  17 us
    unnamed x28, local copies, waits for them, and re-layouts  10.9 us
    ppermute x7, starting transfers between devices, shifted_by(): lax.ppermute(block, 'ctx', [(i, (i + step) % count) for i in range(count)])  9.71 us
    pallas_call x1, Pallas kernels, prompt_part(): pl.pallas_call(functools.partial(prompt_kernel, heads=heads, head_size=wi...  5.95 us
  transfers between devices with their start and end apart: 24, of which 12 were waited for; matrix products, arithmetic and copies ran while one was open for 1% of the time, Pallas kernels for 9%

profile of v9, /device:TPU:2, one launch (start us, length us, event | category | flops | bytes accessed | tf_op | source)
XLA Modules:
  0.0 187.4 jit_solution(1978321792222348608)
XLA Ops:
  7.2 1.6 broadcast_in_dim.22
  8.8 4.5 %all-to-all-start = ((bf16[8,16,896]{2,1,0:T(8,128)(2,1)}), bf16[8,16,896]{2,1,0:T(8,128)(2,1)S(1)}, u32[]{:S(2)}, u32[]{:S(2)}) async-start(bf16[8,16,896]{2,1,0:T(8,128)(2,1)} %broadcast_in_dim.22), calls=%async_computation | async-start | bytes 458752 | tf_op jit(solution)/shard_map/all_to_all | solution.py:482
  13.3 0.7 broadcast_subtract_fusion
  14.1 1.4 copy-done.3
  15.5 1.9 shard_map.131.looked_ref
  17.4 3.1 %all-to-all-done = bf16[8,16,896]{2,1,0:T(8,128)(2,1)S(1)} async-done(((bf16[8,16,896]{2,1,0:T(8,128)(2,1)}), bf16[8,16,896]{2,1,0:T(8,128)(2,1)S(1)}, u32[]{:S(2)}, u32[]{:S(2)}) %all-to-all-start) | async-done | bytes 229408 | tf_op jit(solution)/shard_map/all_to_all | solution.py:482
  20.4 0.6 collective-permute-start
  21.0 2.1 %collective-permute-start.1 = (bf16[112,896]{1,0:T(8,128)(2,1)}, bf16[112,896]{1,0:T(8,128)(2,1)}, u32[]{:S(2)}, u32[]{:S(2)}) collective-permute-start(bf16[112,896]{1,0:T(8,128)(2,1)} %bitcast.20), channel_id=1, source_target_pairs={{0,128},{32,160},{64,192},{96,224},{128,0},{160,32},{192,64},{224,... | collective-permute-start | bytes 602120 | tf_op jit(solution)/shard_map/ppermute | solution.py:463
  23.1 0.6 collective-permute-start.2
  23.7 3.1 %copy-done = bf16[2,2048,896]{2,1,0:T(8,128)(2,1)S(1)} copy-done((bf16[2,2048,896]{2,1,0:T(8,128)(2,1)S(1)}, bf16[2,2048,896]{2,1,0:T(8,128)(2,1)}, u32[]{:S(2)}) %copy-start) | copy-done | bytes 7340056
  26.8 0.7 copy-done.11
  27.4 6.0 %shard_map.132 = bf16[8,240,128]{2,1,0:T(8,128)(2,1)} custom-call(s32[1]{0:T(128)} %bitcast.1.offset_ref, f32[1,8]{1,0:T(1,128)S(1)} %bitcast.28, bf16[128,896]{1,0:T(8,128)(2,1)S(1)} %bitcast.18, bf16[112,1024]{1,0:T(8,128)(2,1)S(1)} %shard_map.131.looked_ref, bf16[2,2048,896]{2,1,0:T(8,128)(2,1)S(1)} %copy-done), custom_call_target="tpu_custom_call" | custom-call | tf_op jit(solution)/shard_map/pallas_call | solution.py:111
  33.4 4.2 %all-to-all-start.1 = ((bf16[8,240,128]{2,1,0:T(8,128)(2,1)}), bf16[8,240,128]{2,1,0:T(8,128)(2,1)S(1)}, u32[]{:S(2)}, u32[]{:S(2)}) async-start(bf16[8,240,128]{2,1,0:T(8,128)(2,1)} %shard_map.132), calls=%async_computation.1 | async-start | bytes 983040 | tf_op jit(solution)/shard_map/all_to_all | solution.py:482
  38.3 0.7 copy-done.6
  39.1 0.8 copy-done.10
  39.9 1.1 shard_map.133
  41.0 0.6 copy-done.8
  41.6 6.0 %all-to-all-done.1.parts_ref = bf16[8,240,128]{2,1,0:T(8,128)(2,1)S(1)} async-done(((bf16[8,240,128]{2,1,0:T(8,128)(2,1)}), bf16[8,240,128]{2,1,0:T(8,128)(2,1)S(1)}, u32[]{:S(2)}, u32[]{:S(2)}) %all-to-all-start.1) | async-done | bytes 491552 | tf_op jit(solution)/shard_map/all_to_all | solution.py:482
  47.6 0.8 copy-done.9
  48.4 1.1 shard_map.134
  49.5 8.5 %all-to-all-start.2 = ((bf16[8,16,896]{2,1,0:T(8,128)(2,1)}), bf16[8,16,896]{2,1,0:T(8,128)(2,1)S(1)}, u32[]{:S(2)}, u32[]{:S(2)}) async-start(bf16[8,16,896]{2,1,0:T(8,128)(2,1)} %shard_map.134), calls=%async_computation.2 | async-start | bytes 458752 | tf_op jit(solution)/shard_map/all_to_all | solution.py:482
  58.1 0.5 collective-permute-start.4
  59.8 0.5 collective-permute-done.5.refs_6_
  60.6 8.4 %all-to-all-done.2.rows_ref = bf16[8,16,896]{2,1,0:T(8,128)(2,1)S(1)} async-done(((bf16[8,16,896]{2,1,0:T(8,128)(2,1)}), bf16[8,16,896]{2,1,0:T(8,128)(2,1)S(1)}, u32[]{:S(2)}, u32[]{:S(2)}) %all-to-all-start.2) | async-done | bytes 229408 | tf_op jit(solution)/shard_map/all_to_all | solution.py:482
  69.0 2.6 %shard_map.135 = bf16[32,2,16,128]{3,2,1,0:T(8,128)(2,1)} custom-call(s32[1]{0:T(128)} %bitcast.ctx_ref, bf16[8,16,896]{2,1,0:T(8,128)(2,1)S(1)} %all-to-all-done.2.rows_ref, bf16[8,240,128]{2,1,0:T(8,128)(2,1)S(1)} %all-to-all-done.1.parts_ref, bf16[112,896]{1,0:T(8,128)(2,1)S(1)} %bitcast.23, bf16[112,896]{1,0:T(8,128)(2,1)S(1)} %collective-permute-done.refs_1_, ...), custom_call_target="tpu_custom_call" | custom-call | tf_op jit(solution)/shard_map/pallas_call | solution.py:309
  71.6 0.6 collective-permute-start.7
  72.2 2.7 %collective-permute-start.8 = (bf16[224,1792]{1,0:T(8,128)(2,1)S(1)}, bf16[224,1792]{1,0:T(8,128)(2,1)S(1)}, u32[]{:S(2)}, u32[]{:S(2)}) collective-permute-start(bf16[224,1792]{1,0:T(8,128)(2,1)S(1)} %copy-done.4), channel_id=1, source_target_pairs={{0,192},{32,224},{64,0},{96,32},{128,64},{160,96},{192,128},{224,1... | collective-permute-start | bytes 2408456 | tf_op jit(solution)/shard_map/ppermute | solution.py:463
  74.9 5.2 %all-to-all-start.3 = ((bf16[32,2,16,128]{3,2,1,0:T(8,128)(2,1)}), bf16[32,2,16,128]{3,2,1,0:T(8,128)(2,1)S(1)}, u32[]{:S(2)}, u32[]{:S(2)}) async-start(bf16[32,2,16,128]{3,2,1,0:T(8,128)(2,1)} %shard_map.135), calls=%async_computation.3 | async-start | bytes 524288 | tf_op jit(solution)/shard_map/all_to_all | solution.py:482
  80.1 9.9 %all-to-all-done.3.parts_ref = bf16[32,2,16,128]{3,2,1,0:T(8,128)(2,1)S(1)} async-done(((bf16[32,2,16,128]{3,2,1,0:T(8,128)(2,1)}), bf16[32,2,16,128]{3,2,1,0:T(8,128)(2,1)S(1)}, u32[]{:S(2)}, u32[]{:S(2)}) %all-to-all-start.3) | async-done | bytes 262176 | tf_op jit(solution)/shard_map/all_to_all | solution.py:482
  90.0 1.1 shard_map.136
  91.0 18.7 %collective-permute-done.7.refs_1_ = bf16[224,1792]{1,0:T(8,128)(2,1)S(1)} collective-permute-done((bf16[224,1792]{1,0:T(8,128)(2,1)S(1)}, bf16[224,1792]{1,0:T(8,128)(2,1)S(1)}, u32[]{:S(2)}, u32[]{:S(2)}) %collective-permute-start.7) | collective-permute-done | bytes 802848 | tf_op jit(solution)/shard_map/ppermute | solution.py:463
  109.7 3.5 %all-to-all-start.4 = ((bf16[8,16,1920]{2,1,0:T(8,128)(2,1)}), bf16[8,16,1920]{2,1,0:T(8,128)(2,1)S(1)}, u32[]{:S(2)}, u32[]{:S(2)}) async-start(bf16[8,16,1920]{2,1,0:T(8,128)(2,1)} %get-tuple-element.41), calls=%async_computation.4 | async-start | bytes 983040 | tf_op jit(solution)/shard_map/all_to_all | solution.py:482
  113.2 0.8 slice.6
  114.0 0.8 slice.7
  114.8 3.2 %collective-permute-start.10 = (bf16[112,1792]{1,0:T(8,128)(2,1)}, bf16[112,1792]{1,0:T(8,128)(2,1)}, u32[]{:S(2)}, u32[]{:S(2)}) collective-permute-start(bf16[112,1792]{1,0:T(8,128)(2,1)} %slice.7), channel_id=1, source_target_pairs={{0,192},{32,224},{64,0},{96,32},{128,64},{160,96},{192,128},{224,1... | collective-permute-start | bytes 1204232 | tf_op jit(solution)/shard_map/ppermute | solution.py:463
  118.0 9.5 %all-to-all-done.4 = bf16[8,16,1920]{2,1,0:T(8,128)(2,1)S(1)} async-done(((bf16[8,16,1920]{2,1,0:T(8,128)(2,1)}), bf16[8,16,1920]{2,1,0:T(8,128)(2,1)S(1)}, u32[]{:S(2)}, u32[]{:S(2)}) %all-to-all-start.4) | async-done | bytes 491552 | tf_op jit(solution)/shard_map/all_to_all | solution.py:482
  127.5 2.8 %copy-done.1 = bf16[1792,1792]{1,0:T(8,128)(2,1)S(1)} copy-done((bf16[1792,1792]{1,0:T(8,128)(2,1)S(1)}, bf16[1792,1792]{1,0:T(8,128)(2,1)}, u32[]{:S(2)}) %copy-start.1) | copy-done | bytes 6422552
  130.4 2.6 %shard_map.137 = bf16[4,464,128]{2,1,0:T(8,128)(2,1)} custom-call(s32[1]{0:T(128)} %bitcast.ctx_ref, bf16[128,1920]{1,0:T(8,128)(2,1)S(1)} %bitcast.15, bf16[8,224,1792]{2,1,0:T(8,128)(2,1)S(1)} %bitcast.14), custom_call_target="tpu_custom_call" | custom-call | tf_op jit(solution)/shard_map/pallas_call | solution.py:376
  133.1 0.5 collective-permute-start.12
  133.7 4.8 %all-to-all-start.5 = ((bf16[4,464,128]{2,1,0:T(8,128)(2,1)}), bf16[4,464,128]{2,1,0:T(8,128)(2,1)S(1)}, u32[]{:S(2)}, u32[]{:S(2)}) async-start(bf16[4,464,128]{2,1,0:T(8,128)(2,1)} %shard_map.137), calls=%async_computation.5 | async-start | bytes 950272 | tf_op jit(solution)/shard_map/all_to_all | solution.py:482
  138.5 0.5 collective-permute-start.15
  139.0 7.6 %all-to-all-done.5.parts_ref = bf16[4,464,128]{2,1,0:T(8,128)(2,1)S(1)} async-done(((bf16[4,464,128]{2,1,0:T(8,128)(2,1)}), bf16[4,464,128]{2,1,0:T(8,128)(2,1)S(1)}, u32[]{:S(2)}, u32[]{:S(2)}) %all-to-all-start.5) | async-done | bytes 475168 | tf_op jit(solution)/shard_map/all_to_all | solution.py:482
  146.5 0.9 shard_map.138
  147.4 4.9 %all-to-all-start.6 = ((bf16[4,448,128]{2,1,0:T(8,128)(2,1)}), bf16[4,448,128]{2,1,0:T(8,128)(2,1)S(1)}, u32[]{:S(2)}, u32[]{:S(2)}) async-start(bf16[4,448,128]{2,1,0:T(8,128)(2,1)} %shard_map.138), calls=%async_computation.6 | async-start | bytes 917504 | tf_op jit(solution)/shard_map/all_to_all | solution.py:482
  152.3 7.1 %all-to-all-done.6.hidden_ref = bf16[4,448,128]{2,1,0:T(8,128)(2,1)S(1)} async-done(((bf16[4,448,128]{2,1,0:T(8,128)(2,1)}), bf16[4,448,128]{2,1,0:T(8,128)(2,1)S(1)}, u32[]{:S(2)}, u32[]{:S(2)}) %all-to-all-start.6) | async-done | bytes 458784 | tf_op jit(solution)/shard_map/all_to_all | solution.py:482
  159.4 3.4 %shard_map.139 = bf16[8,16,1792]{2,1,0:T(8,128)(2,1)S(1)} custom-call(bf16[4,448,128]{2,1,0:T(8,128)(2,1)S(1)} %all-to-all-done.6.hidden_ref, bf16[224,1792]{1,0:T(8,128)(2,1)S(1)} %copy-done.4, bf16[224,1792]{1,0:T(8,128)(2,1)S(1)} %collective-permute-done.7.refs_1_, bf16[224,1792]{1,0:T(8,128)(2,1)S(1)} %collective-permute-done.8.refs_2_, ...), custom_call_target="tpu_custom_call" | custom-call | tf_op jit(solution)/shard_map/pallas_call | solution.py:428
  162.8 17.0 %all_to_all.40.parts_ref = bf16[8,16,1792]{2,1,0:T(8,128)(2,1)S(1)} all-to-all(bf16[8,16,1792]{2,1,0:T(8,128)(2,1)S(1)} %shard_map.139), channel_id=1, replica_groups=mesh['ctx'=8,'req'=8,'mp'=4] {'req'}, dimensions={0} | all-to-all | bytes 917504 | tf_op jit(solution)/shard_map/all_to_all | solution.py:482
  179.8 0.7 shard_map.140
  (47 shorter events, 2.1 us)
Async XLA Ops:
  7.2 31.1 %copy-start.2 = (bf16[2,1,512,896]{3,2,1,0:T(8,128)(2,1)S(1)}, bf16[2,1,512,896]{3,2,1,0:T(8,128)(2,1)}, u32[]{:S(2)}) copy-start(bf16[2,1,512,896]{3,2,1,0:T(8,128)(2,1)} %param.17) | copy-start | bytes 5505028
  8.8 11.7 %all-to-all-start = ((bf16[8,16,896]{2,1,0:T(8,128)(2,1)}), bf16[8,16,896]{2,1,0:T(8,128)(2,1)S(1)}, u32[]{:S(2)}, u32[]{:S(2)}) async-start(bf16[8,16,896]{2,1,0:T(8,128)(2,1)} %broadcast_in_dim.22), calls=%async_computation | async-start | bytes 458752 | tf_op jit(solution)/shard_map/all_to_all | solution.py:482
  14.1 1.4 copy-start.3
  15.5 22.8 %copy-start.12 = (f32[8]{0:T(128)S(1)}, f32[8]{0:T(128)}, u32[]{:S(2)}) copy-start(f32[8]{0:T(128)} %param.19) | copy-start | bytes 100
  20.4 12.9 %collective-permute-start = (bf16[112,896]{1,0:T(8,128)(2,1)}, bf16[112,896]{1,0:T(8,128)(2,1)S(1)}, u32[]{:S(2)}, u32[]{:S(2)}) collective-permute-start(bf16[112,896]{1,0:T(8,128)(2,1)} %bitcast.19), channel_id=1, source_target_pairs={{0,64},{32,96},{64,128},{96,160},{128,192},{160,224},{192,0},{224,... | collective-permute-start | bytes 602120 | tf_op jit(solution)/shard_map/ppermute | solution.py:463
  21.0 12.4 %collective-permute-start.1 = (bf16[112,896]{1,0:T(8,128)(2,1)}, bf16[112,896]{1,0:T(8,128)(2,1)}, u32[]{:S(2)}, u32[]{:S(2)}) collective-permute-start(bf16[112,896]{1,0:T(8,128)(2,1)} %bitcast.20), channel_id=1, source_target_pairs={{0,128},{32,160},{64,192},{96,224},{128,0},{160,32},{192,64},{224,... | collective-permute-start | bytes 602120 | tf_op jit(solution)/shard_map/ppermute | solution.py:463
  23.1 10.3 %collective-permute-start.2 = (bf16[112,896]{1,0:T(8,128)(2,1)}, bf16[112,896]{1,0:T(8,128)(2,1)}, u32[]{:S(2)}, u32[]{:S(2)}) collective-permute-start(bf16[112,896]{1,0:T(8,128)(2,1)} %bitcast.21), channel_id=1, source_target_pairs={{0,192},{32,224},{64,0},{96,32},{128,64},{160,96},{192,128},{224,1... | collective-permute-start | bytes 602120 | tf_op jit(solution)/shard_map/ppermute | solution.py:463
  23.7 3.1 %copy-start = (bf16[2,2048,896]{2,1,0:T(8,128)(2,1)S(1)}, bf16[2,2048,896]{2,1,0:T(8,128)(2,1)}, u32[]{:S(2)}) copy-start(bf16[2,2048,896]{2,1,0:T(8,128)(2,1)} %prefix_ref.1) | copy-start | bytes 22020100
  26.8 0.7 copy-start.11
  27.4 30.6 %copy-start.5 = (bf16[896,112]{0,1:T(8,128)(2,1)S(1)}, bf16[896,112]{0,1:T(8,128)(2,1)}, u32[]{:S(2)}) copy-start(bf16[896,112]{0,1:T(8,128)(2,1)} %param.20) | copy-start | bytes 602116
  27.4 44.2 %copy-start.4 = (bf16[224,1792]{1,0:T(8,128)(2,1)S(1)}, bf16[224,1792]{1,0:T(8,128)(2,1)}, u32[]{:S(2)}) copy-start(bf16[224,1792]{1,0:T(8,128)(2,1)} %refs_0_) | copy-start | bytes 2408452
  27.4 52.6 %copy-start.13 = (f32[1792]{0:T(1024)S(1)}, f32[1792]{0:T(1024)}, u32[]{:S(2)}) copy-start(f32[1792]{0:T(1024)} %param.21) | copy-start | bytes 21508
  33.4 14.2 %all-to-all-start.1 = ((bf16[8,240,128]{2,1,0:T(8,128)(2,1)}), bf16[8,240,128]{2,1,0:T(8,128)(2,1)S(1)}, u32[]{:S(2)}, u32[]{:S(2)}) async-start(bf16[8,240,128]{2,1,0:T(8,128)(2,1)} %shard_map.132), calls=%async_computation.1 | async-start | bytes 983040 | tf_op jit(solution)/shard_map/all_to_all | solution.py:482
  37.6 89.9 %all-gather.3.cloned.1.call-start = ((), (), s32[]{:S(2)}) async-start(), calls=%async_computation.8 | async-start | bytes 7225344 | tf_op jit(solution)/shard_map/all_gather | solution.py:533
  38.3 0.8 copy-start.6
  39.1 0.8 copy-start.10
  41.0 0.6 copy-start.8
  47.6 0.8 copy-start.9
  49.5 19.5 %all-to-all-start.2 = ((bf16[8,16,896]{2,1,0:T(8,128)(2,1)}), bf16[8,16,896]{2,1,0:T(8,128)(2,1)S(1)}, u32[]{:S(2)}, u32[]{:S(2)}) async-start(bf16[8,16,896]{2,1,0:T(8,128)(2,1)} %shard_map.134), calls=%async_computation.2 | async-start | bytes 458752 | tf_op jit(solution)/shard_map/all_to_all | solution.py:482
  58.0 1.5 collective-permute-start.3
  58.1 1.7 collective-permute-start.4
  58.6 1.7 collective-permute-start.5
  58.7 1.9 %collective-permute-start.6 = (bf16[112,896]{1,0:T(8,128)(2,1)}, bf16[112,896]{1,0:T(8,128)(2,1)S(1)}, u32[]{:S(2)}, u32[]{:S(2)}) collective-permute-start(bf16[112,896]{1,0:T(8,128)(2,1)} %collective-permute-done.2.refs_3_), channel_id=1, source_target_pairs={{0,32},{32,0},{64,96},{96,64},{128,160},{160,128},{192,224},{224,1... | collective-permute-start | bytes 602120 | tf_op jit(solution)/shard_map/ppermute | solution.py:468
  71.6 38.1 %collective-permute-start.7 = (bf16[224,1792]{1,0:T(8,128)(2,1)S(1)}, bf16[224,1792]{1,0:T(8,128)(2,1)S(1)}, u32[]{:S(2)}, u32[]{:S(2)}) collective-permute-start(bf16[224,1792]{1,0:T(8,128)(2,1)S(1)} %copy-done.4), channel_id=1, source_target_pairs={{0,64},{32,96},{64,128},{96,160},{128,192},{160,224},{192,0},{224,... | collective-permute-start | bytes 2408456 | tf_op jit(solution)/shard_map/ppermute | solution.py:463
  72.2 37.5 %collective-permute-start.8 = (bf16[224,1792]{1,0:T(8,128)(2,1)S(1)}, bf16[224,1792]{1,0:T(8,128)(2,1)S(1)}, u32[]{:S(2)}, u32[]{:S(2)}) collective-permute-start(bf16[224,1792]{1,0:T(8,128)(2,1)S(1)} %copy-done.4), channel_id=1, source_target_pairs={{0,192},{32,224},{64,0},{96,32},{128,64},{160,96},{192,128},{224,1... | collective-permute-start | bytes 2408456 | tf_op jit(solution)/shard_map/ppermute | solution.py:463
  74.9 15.1 %all-to-all-start.3 = ((bf16[32,2,16,128]{3,2,1,0:T(8,128)(2,1)}), bf16[32,2,16,128]{3,2,1,0:T(8,128)(2,1)S(1)}, u32[]{:S(2)}, u32[]{:S(2)}) async-start(bf16[32,2,16,128]{3,2,1,0:T(8,128)(2,1)} %shard_map.135), calls=%async_computation.3 | async-start | bytes 524288 | tf_op jit(solution)/shard_map/all_to_all | solution.py:482
  109.7 17.8 %all-to-all-start.4 = ((bf16[8,16,1920]{2,1,0:T(8,128)(2,1)}), bf16[8,16,1920]{2,1,0:T(8,128)(2,1)S(1)}, u32[]{:S(2)}, u32[]{:S(2)}) async-start(bf16[8,16,1920]{2,1,0:T(8,128)(2,1)} %get-tuple-element.41), calls=%async_computation.4 | async-start | bytes 983040 | tf_op jit(solution)/shard_map/all_to_all | solution.py:482
  114.0 18.9 %collective-permute-start.9 = (bf16[112,1792]{1,0:T(8,128)(2,1)}, bf16[112,1792]{1,0:T(8,128)(2,1)S(1)}, u32[]{:S(2)}, u32[]{:S(2)}) collective-permute-start(bf16[112,1792]{1,0:T(8,128)(2,1)} %slice.6), channel_id=1, source_target_pairs={{0,64},{32,96},{64,128},{96,160},{128,192},{160,224},{192,0},{224,... | collective-permute-start | bytes 1204232 | tf_op jit(solution)/shard_map/ppermute | solution.py:463
  114.8 18.1 %collective-permute-start.10 = (bf16[112,1792]{1,0:T(8,128)(2,1)}, bf16[112,1792]{1,0:T(8,128)(2,1)}, u32[]{:S(2)}, u32[]{:S(2)}) collective-permute-start(bf16[112,1792]{1,0:T(8,128)(2,1)} %slice.7), channel_id=1, source_target_pairs={{0,192},{32,224},{64,0},{96,32},{128,64},{160,96},{192,128},{224,1... | collective-permute-start | bytes 1204232 | tf_op jit(solution)/shard_map/ppermute | solution.py:463
  127.5 2.8 %copy-start.1 = (bf16[1792,1792]{1,0:T(8,128)(2,1)S(1)}, bf16[1792,1792]{1,0:T(8,128)(2,1)}, u32[]{:S(2)}) copy-start(bf16[1792,1792]{1,0:T(8,128)(2,1)} %all-gather.3.cloned.1.call-done) | copy-start | bytes 19267588
  132.9 46.9 %copy-start.7 = (f32[16,1792]{1,0:T(8,128)S(1)}, f32[16,1792]{1,0:T(8,128)}, u32[]{:S(2)}) copy-start(f32[16,1792]{1,0:T(8,128)} %get-tuple-element.38.residual_ref) | copy-start | bytes 344068
  133.0 26.5 %collective-permute-start.11 = (bf16[224,1792]{1,0:T(8,128)(2,1)S(1)}, bf16[224,1792]{1,0:T(8,128)(2,1)}, u32[]{:S(2)}, u32[]{:S(2)}) collective-permute-start(bf16[224,1792]{1,0:T(8,128)(2,1)S(1)} %copy-done.4), channel_id=1, source_target_pairs={{0,32},{32,0},{64,96},{96,64},{128,160},{160,128},{192,224},{224,1... | collective-permute-start | bytes 2408456 | tf_op jit(solution)/shard_map/ppermute | solution.py:468
  133.1 26.4 %collective-permute-start.12 = (bf16[224,1792]{1,0:T(8,128)(2,1)S(1)}, bf16[224,1792]{1,0:T(8,128)(2,1)}, u32[]{:S(2)}, u32[]{:S(2)}) collective-permute-start(bf16[224,1792]{1,0:T(8,128)(2,1)S(1)} %collective-permute-done.7.refs_1_), channel_id=1, source_target_pairs={{0,32},{32,0},{64,96},{96,64},{128,160},{160,128},{192,224},{224,1... | collective-permute-start | bytes 2408456 | tf_op jit(solution)/shard_map/ppermute | solution.py:468
  133.6 25.9 %collective-permute-start.13 = (bf16[224,1792]{1,0:T(8,128)(2,1)S(1)}, bf16[224,1792]{1,0:T(8,128)(2,1)}, u32[]{:S(2)}, u32[]{:S(2)}) collective-permute-start(bf16[224,1792]{1,0:T(8,128)(2,1)S(1)} %collective-permute-done.8.refs_2_), channel_id=1, source_target_pairs={{0,32},{32,0},{64,96},{96,64},{128,160},{160,128},{192,224},{224,1... | collective-permute-start | bytes 2408456 | tf_op jit(solution)/shard_map/ppermute | solution.py:468
  133.7 12.9 %all-to-all-start.5 = ((bf16[4,464,128]{2,1,0:T(8,128)(2,1)}), bf16[4,464,128]{2,1,0:T(8,128)(2,1)S(1)}, u32[]{:S(2)}, u32[]{:S(2)}) async-start(bf16[4,464,128]{2,1,0:T(8,128)(2,1)} %shard_map.137), calls=%async_computation.5 | async-start | bytes 950272 | tf_op jit(solution)/shard_map/all_to_all | solution.py:482
  138.5 13.9 %collective-permute-start.14 = (bf16[112,1792]{1,0:T(8,128)(2,1)S(1)}, bf16[112,1792]{1,0:T(8,128)(2,1)}, u32[]{:S(2)}, u32[]{:S(2)}) collective-permute-start(bf16[112,1792]{1,0:T(8,128)(2,1)S(1)} %collective-permute-done.9.refs_3_), channel_id=1, source_target_pairs={{0,32},{32,0},{64,96},{96,64},{128,160},{160,128},{192,224},{224,1... | collective-permute-start | bytes 1204232 | tf_op jit(solution)/shard_map/ppermute | solution.py:468
  138.5 13.9 %collective-permute-start.15 = (bf16[112,1792]{1,0:T(8,128)(2,1)}, bf16[112,1792]{1,0:T(8,128)(2,1)}, u32[]{:S(2)}, u32[]{:S(2)}) collective-permute-start(bf16[112,1792]{1,0:T(8,128)(2,1)} %collective-permute-done.10.refs_4_), channel_id=1, source_target_pairs={{0,32},{32,0},{64,96},{96,64},{128,160},{160,128},{192,224},{224,1... | collective-permute-start | bytes 1204232 | tf_op jit(solution)/shard_map/ppermute | solution.py:468
  147.4 12.0 %all-to-all-start.6 = ((bf16[4,448,128]{2,1,0:T(8,128)(2,1)}), bf16[4,448,128]{2,1,0:T(8,128)(2,1)S(1)}, u32[]{:S(2)}, u32[]{:S(2)}) async-start(bf16[4,448,128]{2,1,0:T(8,128)(2,1)} %shard_map.138), calls=%async_computation.6 | async-start | bytes 917504 | tf_op jit(solution)/shard_map/all_to_all | solution.py:482
Sparse Core Ops, SparseCore 0:
  49.6 62.1 all-gather.2

commit v10 on v7

--- a/solution.py
+++ b/solution.py
@@ -488,9 +488,6 @@
     shifted = token_ids.reshape(1, -1) - model_index * vocab_local
     looked_up = look_up(shifted, embed_table.T)
     gathered, looked_up = lax.optimization_barrier((gathered, looked_up))
-    up_all = lax.all_gather(after(up_weight, gathered).T, "ctx")
-    down_all = lax.all_gather(after(down_weight, gathered), "ctx")
-
     out_blocks = [after(out_weight.T, looked_up)]
     out_blocks += [
         lax.ppermute(out_blocks[0], "ctx", [(i, (i + step) % ctx_count) for i in range(ctx_count)])
@@ -507,6 +504,8 @@
         ctx_count,
     )
     parts, *out_blocks = lax.optimization_barrier((parts, *out_blocks))
+    up_all = lax.all_gather(after(up_weight, parts).T, "ctx")
+    down_all = lax.all_gather(after(down_weight, parts), "ctx")
     own, own_level = own_part(
         after(queries[0], parts), suffix_kv[:, 0], draft_kv[:, 0], slopes, suffix_len
     )

time: 166 us -> 162 us (0.976)
  waiting for transfers between devices: 44.1 us -> 38.8 us
    all_to_all x5, waiting for transfers between devices: 41.8 us -> 36.8 us  [exchange(): return lax.all_to_all(value, axis, split_axis=0, concat_axis=0, tiled=True)]
  transfers between devices with their start and end apart: 14 -> 14, of which waited for: 9 -> 9; matrix products, arithmetic and copies ran while one was open for 1% -> 1% of each run, Pallas kernels for 9% -> 10%
where the time goes in v10:
time: 162 us
  blocking collectives  45.6 us (28%)
  waiting for transfers between devices  38.8 us (24%)
  starting transfers between devices  31.6 us (20%)
  Pallas kernels  17.5 us (11%)
  between operations  14.9 us (9%)
  local copies, waits for them, and re-layouts  12.6 us (8%)
    all_to_all x3, blocking collectives, exchange(): return lax.all_to_all(value, axis, split_axis=0, concat_axis=0, tiled=True)  45.6 us
    all_to_all x5, waiting for transfers between devices, exchange(): return lax.all_to_all(value, axis, split_axis=0, concat_axis=0, tiled=True)  36.8 us
    all_to_all x5, starting transfers between devices, exchange(): return lax.all_to_all(value, axis, split_axis=0, concat_axis=0, tiled=True)  27.1 us
    unnamed x24, local copies, waits for them, and re-layouts  10.9 us
    pallas_call x1, Pallas kernels, prompt_part(): pl.pallas_call(functools.partial(prompt_kernel, heads=heads, head_size=wi...  6.36 us
    ppermute x3, starting transfers between devices, per_device(): lax.ppermute(out_blocks[0], 'ctx', [(i, (i + step) % ctx_count) for i in...  3.28 us
  transfers between devices with their start and end apart: 14, of which 9 were waited for; matrix products, arithmetic and copies ran while one was open for 1% of the time, Pallas kernels for 10%

profile of v10, /device:TPU:2, one launch (start us, length us, event | category | flops | bytes accessed | tf_op | source)
XLA Modules:
  0.0 161.6 jit_solution(3785842065660118640)
XLA Ops:
  7.2 1.5 broadcast_in_dim.22
  8.7 4.6 %all-to-all-start = ((bf16[8,16,896]{2,1,0:T(8,128)(2,1)}), bf16[8,16,896]{2,1,0:T(8,128)(2,1)S(1)}, u32[]{:S(2)}, u32[]{:S(2)}) async-start(bf16[8,16,896]{2,1,0:T(8,128)(2,1)} %broadcast_in_dim.22), calls=%async_computation | async-start | bytes 458752 | tf_op jit(solution)/shard_map/all_to_all | solution.py:458
  13.3 0.0 all-gather.5.cloned.1.call-start
  13.3 0.7 broadcast_subtract_fusion
  14.0 0.1 copy.15
  14.1 0.1 sub.14.ids_ref
  14.2 1.4 copy-done.4
  15.6 1.9 %shard_map.131.looked_ref = bf16[112,1024]{1,0:T(8,128)(2,1)S(1)} custom-call(s32[1,1024]{1,0:T(1,128)S(1)} %sub.14.ids_ref, bf16[112,6400]{1,0:T(8,128)(2,1)S(1)} %bitcast.19), custom_call_target="tpu_custom_call" | custom-call | tf_op jit(solution)/shard_map/pallas_call | solution.py:143
  17.5 3.0 %all-to-all-done = bf16[8,16,896]{2,1,0:T(8,128)(2,1)S(1)} async-done(((bf16[8,16,896]{2,1,0:T(8,128)(2,1)}), bf16[8,16,896]{2,1,0:T(8,128)(2,1)S(1)}, u32[]{:S(2)}, u32[]{:S(2)}) %all-to-all-start) | async-done | bytes 229408 | tf_op jit(solution)/shard_map/all_to_all | solution.py:458
  20.5 0.6 collective-permute-start
  21.0 2.1 %collective-permute-start.1 = (bf16[112,896]{1,0:T(8,128)(2,1)}, bf16[112,896]{1,0:T(8,128)(2,1)S(1)}, u32[]{:S(2)}, u32[]{:S(2)}) collective-permute-start(bf16[112,896]{1,0:T(8,128)(2,1)} %bitcast.22), channel_id=1, source_target_pairs={{0,128},{32,160},{64,192},{96,224},{128,0},{160,32},{192,64},{224,... | collective-permute-start | bytes 602120 | tf_op jit(solution)/shard_map/ppermute | solution.py:493
  23.1 0.6 collective-permute-start.2
  23.8 3.1 %copy-done = bf16[2,2048,896]{2,1,0:T(8,128)(2,1)S(1)} copy-done((bf16[2,2048,896]{2,1,0:T(8,128)(2,1)S(1)}, bf16[2,2048,896]{2,1,0:T(8,128)(2,1)}, u32[]{:S(2)}) %copy-start) | copy-done | bytes 7340056
  26.8 0.7 copy-done.9
  27.5 6.4 %shard_map.132 = bf16[8,240,128]{2,1,0:T(8,128)(2,1)} custom-call(s32[1]{0:T(128)} %bitcast.1.offset_ref, f32[1,8]{1,0:T(1,128)S(1)} %bitcast.30, bf16[128,896]{1,0:T(8,128)(2,1)S(1)} %bitcast.20, bf16[112,1024]{1,0:T(8,128)(2,1)S(1)} %shard_map.131.looked_ref, bf16[2,2048,896]{2,1,0:T(8,128)(2,1)S(1)} %copy-done), custom_call_target="tpu_custom_call" | custom-call | tf_op jit(solution)/shard_map/pallas_call | solution.py:111
  33.9 0.0 all-gather.5.cloned.1.call-update
  33.9 0.0 all-gather.7.cloned.1.call-start
  34.0 0.7 all-gather.7.cloned.1.call-update
  34.7 4.2 %all-to-all-start.1 = ((bf16[8,240,128]{2,1,0:T(8,128)(2,1)}), bf16[8,240,128]{2,1,0:T(8,128)(2,1)S(1)}, u32[]{:S(2)}, u32[]{:S(2)}) async-start(bf16[8,240,128]{2,1,0:T(8,128)(2,1)} %shard_map.132), calls=%async_computation.1 | async-start | bytes 983040 | tf_op jit(solution)/shard_map/all_to_all | solution.py:458
  39.5 1.1 shard_map.133
  40.7 8.2 %all-to-all-done.1.parts_ref = bf16[8,240,128]{2,1,0:T(8,128)(2,1)S(1)} async-done(((bf16[8,240,128]{2,1,0:T(8,128)(2,1)}), bf16[8,240,128]{2,1,0:T(8,128)(2,1)S(1)}, u32[]{:S(2)}, u32[]{:S(2)}) %all-to-all-start.1) | async-done | bytes 491552 | tf_op jit(solution)/shard_map/all_to_all | solution.py:458
  48.8 1.1 shard_map.134
  49.9 8.5 %all-to-all-start.2 = ((bf16[8,16,896]{2,1,0:T(8,128)(2,1)}), bf16[8,16,896]{2,1,0:T(8,128)(2,1)S(1)}, u32[]{:S(2)}, u32[]{:S(2)}) async-start(bf16[8,16,896]{2,1,0:T(8,128)(2,1)} %shard_map.134), calls=%async_computation.2 | async-start | bytes 458752 | tf_op jit(solution)/shard_map/all_to_all | solution.py:458
  58.4 0.1 collective-permute-start.3
  58.5 0.5 collective-permute-start.4
  59.0 0.1 collective-permute-start.5
  59.1 0.4 collective-permute-start.6
  59.5 0.4 collective-permute-done.3.refs_4_
  59.9 0.3 collective-permute-done.4.refs_5_
  60.2 0.3 collective-permute-done.5.refs_6_
  60.5 0.3 collective-permute-done.6.refs_7_
  60.8 8.6 %all-to-all-done.2.rows_ref = bf16[8,16,896]{2,1,0:T(8,128)(2,1)S(1)} async-done(((bf16[8,16,896]{2,1,0:T(8,128)(2,1)}), bf16[8,16,896]{2,1,0:T(8,128)(2,1)S(1)}, u32[]{:S(2)}, u32[]{:S(2)}) %all-to-all-start.2) | async-done | bytes 229408 | tf_op jit(solution)/shard_map/all_to_all | solution.py:458
  69.3 1.6 %shard_map.135 = bf16[32,2,16,128]{3,2,1,0:T(8,128)(2,1)} custom-call(s32[1]{0:T(128)} %bitcast.ctx_ref, bf16[8,16,896]{2,1,0:T(8,128)(2,1)S(1)} %all-to-all-done.2.rows_ref, bf16[8,240,128]{2,1,0:T(8,128)(2,1)S(1)} %all-to-all-done.1.parts_ref, bf16[112,896]{1,0:T(8,128)(2,1)S(1)} %bitcast.25, bf16[112,896]{1,0:T(8,128)(2,1)S(1)} %collective-permute-done.refs_1_, ...), custom_call_target="tpu_custom_call" | custom-call | tf_op jit(solution)/shard_map/pallas_call | solution.py:309
  71.0 5.0 %all-to-all-start.3 = ((bf16[32,2,16,128]{3,2,1,0:T(8,128)(2,1)}), bf16[32,2,16,128]{3,2,1,0:T(8,128)(2,1)S(1)}, u32[]{:S(2)}, u32[]{:S(2)}) async-start(bf16[32,2,16,128]{3,2,1,0:T(8,128)(2,1)} %shard_map.135), calls=%async_computation.3 | async-start | bytes 524288 | tf_op jit(solution)/shard_map/all_to_all | solution.py:458
  76.0 10.8 %all-to-all-done.3.parts_ref = bf16[32,2,16,128]{3,2,1,0:T(8,128)(2,1)S(1)} async-done(((bf16[32,2,16,128]{3,2,1,0:T(8,128)(2,1)}), bf16[32,2,16,128]{3,2,1,0:T(8,128)(2,1)S(1)}, u32[]{:S(2)}, u32[]{:S(2)}) %all-to-all-start.3) | async-done | bytes 262176 | tf_op jit(solution)/shard_map/all_to_all | solution.py:458
  86.7 0.8 shard_map.136
  87.6 18.0 %all_to_all.40 = bf16[8,16,1920]{2,1,0:T(8,128)(2,1)S(1)} all-to-all(bf16[8,16,1920]{2,1,0:T(8,128)(2,1)S(1)} %get-tuple-element.29), channel_id=1, replica_groups=mesh['ctx'=8,'req'=8,'mp'=4] {'req'}, dimensions={0} | all-to-all | bytes 983040 | tf_op jit(solution)/shard_map/all_to_all | solution.py:458
  105.6 3.0 %copy-done.2 = bf16[1792,1792]{1,0:T(8,128)(2,1)S(1)} copy-done((bf16[1792,1792]{1,0:T(8,128)(2,1)S(1)}, bf16[1792,1792]{1,0:T(8,128)(2,1)}, u32[]{:S(2)}) %copy-start.2) | copy-done | bytes 6422552
  108.6 1.8 %shard_map.137 = bf16[4,464,128]{2,1,0:T(8,128)(2,1)S(1)} custom-call(bf16[128,1920]{1,0:T(8,128)(2,1)S(1)} %bitcast.17, bf16[8,224,1792]{2,1,0:T(8,128)(2,1)S(1)} %bitcast.16), custom_call_target="tpu_custom_call" | custom-call | tf_op jit(solution)/shard_map/pallas_call | solution.py:376
  110.4 0.0 copy-start.7
  110.4 11.1 %all_to_all.41.parts_ref = bf16[4,464,128]{2,1,0:T(8,128)(2,1)S(1)} all-to-all(bf16[4,464,128]{2,1,0:T(8,128)(2,1)S(1)} %shard_map.137), channel_id=1, replica_groups=mesh['ctx'=8,'req'=8,'mp'=4] {'mp'}, dimensions={0} | all-to-all | bytes 950272 | tf_op jit(solution)/shard_map/all_to_all | solution.py:458
  121.5 0.9 shard_map.138
  122.4 4.9 %all-to-all-start.6 = ((bf16[4,448,128]{2,1,0:T(8,128)(2,1)}), bf16[4,448,128]{2,1,0:T(8,128)(2,1)S(1)}, u32[]{:S(2)}, u32[]{:S(2)}) async-start(bf16[4,448,128]{2,1,0:T(8,128)(2,1)} %shard_map.138), calls=%async_computation.6 | async-start | bytes 917504 | tf_op jit(solution)/shard_map/all_to_all | solution.py:458
  127.3 6.3 %all-to-all-done.6.hidden_ref = bf16[4,448,128]{2,1,0:T(8,128)(2,1)S(1)} async-done(((bf16[4,448,128]{2,1,0:T(8,128)(2,1)}), bf16[4,448,128]{2,1,0:T(8,128)(2,1)S(1)}, u32[]{:S(2)}, u32[]{:S(2)}) %all-to-all-start.6) | async-done | bytes 458784 | tf_op jit(solution)/shard_map/all_to_all | solution.py:458
  133.5 2.8 %copy-done.1 = bf16[1792,1792]{1,0:T(8,128)(2,1)S(1)} copy-done((bf16[1792,1792]{1,0:T(8,128)(2,1)S(1)}, bf16[1792,1792]{1,0:T(8,128)(2,1)}, u32[]{:S(2)}) %copy-start.1) | copy-done | bytes 6422552
  136.4 1.2 shard_map.139
  137.5 16.5 %all_to_all.42.parts_ref = bf16[8,16,1792]{2,1,0:T(8,128)(2,1)S(1)} all-to-all(bf16[8,16,1792]{2,1,0:T(8,128)(2,1)S(1)} %shard_map.139), channel_id=1, replica_groups=mesh['ctx'=8,'req'=8,'mp'=4] {'req'}, dimensions={0} | all-to-all | bytes 917504 | tf_op jit(solution)/shard_map/all_to_all | solution.py:458
  154.0 0.7 shard_map.140
  (24 shorter events, 0.1 us)
Async XLA Ops:
  7.2 32.3 %copy-start.6 = (bf16[1,16,896]{2,1,0:T(8,128)(2,1)S(1)}, bf16[1,16,896]{2,1,0:T(8,128)(2,1)}, u32[]{:S(2)}) copy-start(bf16[1,16,896]{2,1,0:T(8,128)(2,1)} %param.14) | copy-start | bytes 86020
  7.2 32.3 %copy-start.8 = (bf16[2,1,16,896]{3,2,1,0:T(8,128)(2,1)S(1)}, bf16[2,1,16,896]{3,2,1,0:T(8,128)(2,1)}, u32[]{:S(2)}) copy-start(bf16[2,1,16,896]{3,2,1,0:T(8,128)(2,1)} %param.15) | copy-start | bytes 172036
  7.2 32.3 %copy-start.10 = (f32[8]{0:T(128)S(1)}, f32[8]{0:T(128)}, u32[]{:S(2)}) copy-start(f32[8]{0:T(128)} %param.19) | copy-start | bytes 100
  8.7 30.8 %copy-start.3 = (bf16[2,1,512,896]{3,2,1,0:T(8,128)(2,1)S(1)}, bf16[2,1,512,896]{3,2,1,0:T(8,128)(2,1)}, u32[]{:S(2)}) copy-start(bf16[2,1,512,896]{3,2,1,0:T(8,128)(2,1)} %param.17) | copy-start | bytes 5505028
  8.7 11.8 %all-to-all-start = ((bf16[8,16,896]{2,1,0:T(8,128)(2,1)}), bf16[8,16,896]{2,1,0:T(8,128)(2,1)S(1)}, u32[]{:S(2)}, u32[]{:S(2)}) async-start(bf16[8,16,896]{2,1,0:T(8,128)(2,1)} %broadcast_in_dim.22), calls=%async_computation | async-start | bytes 458752 | tf_op jit(solution)/shard_map/all_to_all | solution.py:458
  13.3 92.3 %all-gather.5.cloned.1.call-start = ((), (), s32[]{:S(2)}) async-start(), calls=%async_computation.8 | async-start | bytes 7225344 | tf_op jit(solution)/shard_map/all_gather | solution.py:507
  14.2 1.4 copy-start.4
  20.5 13.4 %collective-permute-start = (bf16[112,896]{1,0:T(8,128)(2,1)}, bf16[112,896]{1,0:T(8,128)(2,1)S(1)}, u32[]{:S(2)}, u32[]{:S(2)}) collective-permute-start(bf16[112,896]{1,0:T(8,128)(2,1)} %bitcast.21), channel_id=1, source_target_pairs={{0,64},{32,96},{64,128},{96,160},{128,192},{160,224},{192,0},{224,... | collective-permute-start | bytes 602120 | tf_op jit(solution)/shard_map/ppermute | solution.py:493
  21.0 12.8 %collective-permute-start.1 = (bf16[112,896]{1,0:T(8,128)(2,1)}, bf16[112,896]{1,0:T(8,128)(2,1)S(1)}, u32[]{:S(2)}, u32[]{:S(2)}) collective-permute-start(bf16[112,896]{1,0:T(8,128)(2,1)} %bitcast.22), channel_id=1, source_target_pairs={{0,128},{32,160},{64,192},{96,224},{128,0},{160,32},{192,64},{224,... | collective-permute-start | bytes 602120 | tf_op jit(solution)/shard_map/ppermute | solution.py:493
  23.1 10.8 %collective-permute-start.2 = (bf16[112,896]{1,0:T(8,128)(2,1)}, bf16[112,896]{1,0:T(8,128)(2,1)S(1)}, u32[]{:S(2)}, u32[]{:S(2)}) collective-permute-start(bf16[112,896]{1,0:T(8,128)(2,1)} %bitcast.23), channel_id=1, source_target_pairs={{0,192},{32,224},{64,0},{96,32},{128,64},{160,96},{192,128},{224,1... | collective-permute-start | bytes 602120 | tf_op jit(solution)/shard_map/ppermute | solution.py:493
  23.8 3.1 %copy-start = (bf16[2,2048,896]{2,1,0:T(8,128)(2,1)S(1)}, bf16[2,2048,896]{2,1,0:T(8,128)(2,1)}, u32[]{:S(2)}) copy-start(bf16[2,2048,896]{2,1,0:T(8,128)(2,1)} %prefix_ref.1) | copy-start | bytes 22020100
  26.8 0.7 copy-start.9
  27.5 30.9 %copy-start.5 = (bf16[896,112]{0,1:T(8,128)(2,1)S(1)}, bf16[896,112]{0,1:T(8,128)(2,1)}, u32[]{:S(2)}) copy-start(bf16[896,112]{0,1:T(8,128)(2,1)} %param.20) | copy-start | bytes 602116
  33.9 42.1 %copy-start.11 = (f32[1792]{0:T(1024)S(1)}, f32[1792]{0:T(1024)}, u32[]{:S(2)}) copy-start(f32[1792]{0:T(1024)} %param.21) | copy-start | bytes 21508
  33.9 93.4 %all-gather.7.cloned.1.call-start = ((), (), s32[]{:S(2)}) async-start(), calls=%async_computation.9 | async-start | bytes 7225344 | tf_op jit(solution)/shard_map/all_gather | solution.py:508
  34.7 14.2 %all-to-all-start.1 = ((bf16[8,240,128]{2,1,0:T(8,128)(2,1)}), bf16[8,240,128]{2,1,0:T(8,128)(2,1)S(1)}, u32[]{:S(2)}, u32[]{:S(2)}) async-start(bf16[8,240,128]{2,1,0:T(8,128)(2,1)} %shard_map.132), calls=%async_computation.1 | async-start | bytes 983040 | tf_op jit(solution)/shard_map/all_to_all | solution.py:458
  49.9 19.4 %all-to-all-start.2 = ((bf16[8,16,896]{2,1,0:T(8,128)(2,1)}), bf16[8,16,896]{2,1,0:T(8,128)(2,1)S(1)}, u32[]{:S(2)}, u32[]{:S(2)}) async-start(bf16[8,16,896]{2,1,0:T(8,128)(2,1)} %shard_map.134), calls=%async_computation.2 | async-start | bytes 458752 | tf_op jit(solution)/shard_map/all_to_all | solution.py:458
  58.4 1.5 collective-permute-start.3
  58.5 1.7 %collective-permute-start.4 = (bf16[112,896]{1,0:T(8,128)(2,1)S(1)}, bf16[112,896]{1,0:T(8,128)(2,1)S(1)}, u32[]{:S(2)}, u32[]{:S(2)}) collective-permute-start(bf16[112,896]{1,0:T(8,128)(2,1)S(1)} %collective-permute-done.refs_1_), channel_id=1, source_target_pairs={{0,32},{32,0},{64,96},{96,64},{128,160},{160,128},{192,224},{224,1... | collective-permute-start | bytes 602120 | tf_op jit(solution)/shard_map/ppermute | solution.py:514
  59.0 1.5 collective-permute-start.5
  59.1 1.7 %collective-permute-start.6 = (bf16[112,896]{1,0:T(8,128)(2,1)S(1)}, bf16[112,896]{1,0:T(8,128)(2,1)S(1)}, u32[]{:S(2)}, u32[]{:S(2)}) collective-permute-start(bf16[112,896]{1,0:T(8,128)(2,1)S(1)} %collective-permute-done.2.refs_3_), channel_id=1, source_target_pairs={{0,32},{32,0},{64,96},{96,64},{128,160},{160,128},{192,224},{224,1... | collective-permute-start | bytes 602120 | tf_op jit(solution)/shard_map/ppermute | solution.py:514
  71.0 15.8 %all-to-all-start.3 = ((bf16[32,2,16,128]{3,2,1,0:T(8,128)(2,1)}), bf16[32,2,16,128]{3,2,1,0:T(8,128)(2,1)S(1)}, u32[]{:S(2)}, u32[]{:S(2)}) async-start(bf16[32,2,16,128]{3,2,1,0:T(8,128)(2,1)} %shard_map.135), calls=%async_computation.3 | async-start | bytes 524288 | tf_op jit(solution)/shard_map/all_to_all | solution.py:458
  105.6 3.0 %copy-start.2 = (bf16[1792,1792]{1,0:T(8,128)(2,1)S(1)}, bf16[1792,1792]{1,0:T(8,128)(2,1)}, u32[]{:S(2)}) copy-start(bf16[1792,1792]{1,0:T(8,128)(2,1)} %all-gather.5.cloned.1.call-done) | copy-start | bytes 19267588
  110.4 43.7 %copy-start.7 = (f32[16,1792]{1,0:T(8,128)S(1)}, f32[16,1792]{1,0:T(8,128)}, u32[]{:S(2)}) copy-start(f32[16,1792]{1,0:T(8,128)} %get-tuple-element.28.residual_ref) | copy-start | bytes 344068
  122.4 11.2 %all-to-all-start.6 = ((bf16[4,448,128]{2,1,0:T(8,128)(2,1)}), bf16[4,448,128]{2,1,0:T(8,128)(2,1)S(1)}, u32[]{:S(2)}, u32[]{:S(2)}) async-start(bf16[4,448,128]{2,1,0:T(8,128)(2,1)} %shard_map.138), calls=%async_computation.6 | async-start | bytes 917504 | tf_op jit(solution)/shard_map/all_to_all | solution.py:458
  133.5 2.8 %copy-start.1 = (bf16[1792,1792]{1,0:T(8,128)(2,1)S(1)}, bf16[1792,1792]{1,0:T(8,128)(2,1)}, u32[]{:S(2)}) copy-start(bf16[1792,1792]{1,0:T(8,128)(2,1)} %all-gather.7.cloned.1.call-done) | copy-start | bytes 19267588
Sparse Core Ops, SparseCore 0:
  34.0 46.6 all-gather.4
  82.6 44.1 all-gather.6
